TPU v7x, 256 devices: a whole 4x4x8 slice. The times are simulated.
256 devices in a mesh: gossip: 8 (over x_hi, y), shard: 32 (over x_lo, z, core).
Axes of the slice: x: 4 (x_hi: 2, x_lo: 2; x = x_hi * 2 + x_lo), y: 4, z: 8, core: 2. Of those that a mesh axis runs over, the one named last changes fastest.
Arguments:
- activ: bfloat16 [8, 16384, 2048], P('gossip', 'shard'), may hold values from -48 to 48
- grad_out: bfloat16 [8, 16384, 2048], P('gossip', 'shard'), may hold values from -6 to 6
- weight: bfloat16 [8, 2048, 2048], P('gossip', 'shard'), may hold values from -0.125 to 0.125
- q_seed: int32 [8, 2048, 2], replicated, may hold values from -4 to 4
Outputs:
- grad_in: bfloat16 [8, 16384, 2048], P('gossip', 'shard')
- new_weight: float32 [8, 2048, 2048], P('gossip', 'shard')
- next_q: float32 [8, 2048, 2], P('gossip')
All inputs are finite; a program needn't handle non-finite values.
Results may differ from a plain program's by a relative error of at most 0.00045.
Values may be sent and summed in bfloat16 or wider, within the bound.
No kernel may reach another device: no remote copies, remote signals or barrier semaphores. Data moves between devices by JAX's collectives and lax.ppermute only.
A program may use at most 128 MiB of HBM per device.

v0:
```python
import functools

import jax
import jax.numpy as jnp
from jax import lax
from jax.experimental import pallas as pl
from jax.experimental.pallas import tpu as pltpu
from jax.sharding import Mesh
from jax.sharding import PartitionSpec as P

LEARN = 0.002
GOSSIP = 0.5
EPS = 1e-06
LANES = 128
LEVELS = 64.0
STEPS = 32767.0
VMEM = 16 * 2**20
MOST_VMEM = 24 * 2**20
NO_ROOM = 56 * 2**20
MARK = jax.ShapeDtypeStruct((8, 128), jnp.float32)
NO_COST = pl.CostEstimate(flops=0, bytes_accessed=0, transcendentals=0)
STEPS_BACK = (("core", 1), ("z", 1), ("z", 2), ("z", 4), ("xl", 1))
STEPS_ALONG = (("core", 1), ("xl", 1), ("z", 1), ("z", 2), ("z", 4))

CYCLE = ("xh", "y")
SHARD = ("xl", "z", "core")
NT = (((1,), (1,)), ((), ()))
NN = (((1,), (0,)), ((), ()))
TN = (((0,), (0,)), ((), ()))


def dot(left, right, dims):
    return lax.dot_general(left, right, dims, preferred_element_type=jnp.float32)


def terms(value):
    high = value.astype(jnp.bfloat16)
    rest = value - high.astype(jnp.float32)
    middle = rest.astype(jnp.bfloat16)
    low = (rest - middle.astype(jnp.float32)).astype(jnp.bfloat16)
    parts = [part.astype(jnp.float32) for part in (high, middle, low)]
    return jnp.concatenate(parts, 0).astype(jnp.bfloat16)


def summed(value):
    return value[:8] + (value[8:16] + value[16:])


def thin(left, right, dims):
    return summed(dot(left, right, dims))


def own_columns(own, rows, width):
    row = lax.broadcasted_iota(jnp.int32, (rows, width), 0) + own * rows
    column = lax.broadcasted_iota(jnp.int32, (rows, width), 1)
    return jnp.where(row == column, 1.0, 0.0).astype(jnp.bfloat16)


def kernel_call(kernel, operands, out_shape, scalars=None, after=()):
    whole = pl.BlockSpec(memory_space=pltpu.VMEM)
    specs = [whole] * (len(operands) + len(after))
    first = []
    if scalars is not None:
        specs, first = [pl.BlockSpec(memory_space=pltpu.SMEM)] + specs, [scalars]
    lead, unused = len(first) + len(operands), len(after)

    def body(*refs):
        kernel(*refs[:lead], *refs[lead + unused :])

    return pl.pallas_call(
        body,
        in_specs=specs,
        out_specs=jax.tree.map(lambda _: whole, out_shape),
        out_shape=out_shape,
        cost_estimate=NO_COST,
        compiler_params=pltpu.CompilerParams(vmem_limit_bytes=VMEM),
    )(*first, *operands, *after)


def f32(*shape):
    return jax.ShapeDtypeStruct(shape, jnp.float32)


def probe_kernel(own, probes, acts, cotan, weight, out):
    rows, width = weight.shape
    from_grads = thin(terms(dot(probes[...], cotan[...], NT)[:8]), acts[...], NN)
    from_weight = terms(dot(probes[...], weight[...], NT)[:8])
    placed = thin(from_weight, own_columns(own[0], rows, width), NN)
    out[...] = (placed - LEARN * from_grads)[:4]


def unit_vectors(proj):
    first, second = proj[0:1], proj[1:2]
    unit_first = first * lax.rsqrt(jnp.sum(first * first, keepdims=True) + EPS)
    remain = second - jnp.sum(unit_first * second, keepdims=True) * unit_first
    unit_second = remain * lax.rsqrt(jnp.sum(remain * remain, keepdims=True) + EPS)
    return [unit_first, unit_second]


def basis_kernel(
    own, right, left, from_right, from_left, acts, cotan, weight, out, out_basis
):
    rows, width = weight.shape
    units = unit_vectors(right[...] - from_right[...])
    units += unit_vectors(from_left[...] - left[...])
    row = lax.broadcasted_iota(jnp.int32, (8, width), 0)
    basis = jnp.zeros((8, width), jnp.float32)
    for k, unit in enumerate(units):
        basis = jnp.where(row == k, jnp.broadcast_to(unit, (8, width)), basis)
    parts = terms(basis)
    own_parts = dot(parts, own_columns(own[0], rows, width), NT)
    out_basis[...] = summed(own_parts)
    from_weight = thin(own_parts.astype(jnp.bfloat16), weight[...], NN)
    from_grads = thin(terms(thin(parts, acts[...], NT)), cotan[...], NN)
    out[...] = (from_weight - LEARN * from_grads)[:4]


def add_kernel(left, right, out):
    out[...] = left[...] + right[...]


def add_split_kernel(left, right, out_right, out_left):
    total = left[...] + right[...]
    out_right[...] = total[:2]
    out_left[...] = total[2:]


def partner(value, axis, step):
    count = lax.axis_size(axis)
    return lax.ppermute(value, axis, [(i, i ^ step) for i in range(count)])


def shard_sum(value, steps, after, split=None):
    for axis, step in steps:
        key = axis + str(step)
        operands = (value, partner(value, axis, step))
        if key == split:
            halves = (f32(2, value.shape[1]), f32(2, value.shape[1]))
            value = kernel_call(add_split_kernel, operands, halves, after=after.get(key, ()))
        else:
            value = kernel_call(add_kernel, operands, f32(*value.shape), after=after.get(key, ()))
    return value


def passed_along(value, steps):
    count, row = lax.axis_size(CYCLE), lax.axis_size("y")
    pairs = []
    for source in range(count):
        target = (source + steps) % count
        crossed = int(source // row != target // row)
        pairs += [(2 * source + x, 2 * target + (x ^ crossed)) for x in range(2)]
    return lax.ppermute(value, CYCLE + ("xl",), pairs)


def neighbours(right, left):
    return passed_along(left, -1), passed_along(right, 1)


def coded(value):
    largest = jnp.maximum(jnp.max(jnp.abs(value), 1, keepdims=True), 1e-30)
    level = jnp.ceil(jnp.log2(largest) * LEVELS + 0.01)
    steps = jnp.floor(value * (STEPS * jnp.exp2(level * (-1.0 / LEVELS))) + 0.5)
    steps = jnp.clip(steps, -STEPS, STEPS).astype(jnp.int32)
    level = jnp.broadcast_to(level, (value.shape[0], LANES)).astype(jnp.int32)
    return jnp.concatenate([steps, level], 1).astype(jnp.int16)


def decoded(code):
    code = code.astype(jnp.int32).astype(jnp.float32)
    size = jnp.exp2(code[:, -1:] * (1.0 / LEVELS)) * (1.0 / STEPS)
    return code[:, :-LANES] * size


def product(place, first, count, acts, other_acts, cotan, other_cotan):
    rows = acts.shape[1] // 8

    def columns(ref):
        return jnp.concatenate(
            [ref[:, pl.ds(pl.multiple_of(place[first + k] * rows, rows), rows)] for k in range(count)], 1
        )

    return dot(columns(acts), cotan[...], TN) + dot(columns(other_acts), other_cotan[...], TN)


def chunk_kernel(first, place, acts, other_acts, cotan, other_cotan, *outs):
    rows = acts.shape[1] // 8
    outs, mark = outs[:-1], outs[-1]
    mark[...] = jnp.zeros_like(mark)
    for out in outs:
        count = out.shape[0]
        value = product(place, first, count, acts, other_acts, cotan, other_cotan)
        for k in range(count):
            out[k] = coded(value[k * rows : (k + 1) * rows])
        first += count


def mine_kernel(place, acts, other_acts, cotan, other_cotan, out, mark):
    rows = acts.shape[1] // 8
    mark[...] = jnp.zeros_like(mark)
    for k in range(2):
        value = product(place, 4 * k, 4, acts, other_acts, cotan, other_cotan)
        for j in range(4):
            out[4 * k + j] = value[rows * j : rows * (j + 1)]


def chunks(kernel, out_shape, scalars, acts, other_acts, cotan, other_cotan, after):
    tokens, width = acts.shape
    half = width // 2
    unused = len(after)

    def body(place, *refs):
        kernel(place, *refs[:4], *refs[4 + unused :])

    def spec(shape):
        return pl.BlockSpec(shape, lambda i, at: (0,) * len(shape))

    return pl.pallas_call(
        body,
        grid_spec=pltpu.PrefetchScalarGridSpec(
            num_scalar_prefetch=1,
            grid=(1,),
            in_specs=[
                pl.BlockSpec((tokens, half), lambda i, at: (0, at[8])),
                pl.BlockSpec((tokens, half), lambda i, at: (0, at[8])),
                pl.BlockSpec((tokens, half), lambda i, at: (0, at[9])),
                pl.BlockSpec((tokens, half), lambda i, at: (0, at[9])),
            ]
            + [pl.BlockSpec(memory_space=pltpu.VMEM)] * unused,
            out_specs=jax.tree.map(lambda a: spec(a.shape), out_shape),
        ),
        out_shape=out_shape,
        cost_estimate=NO_COST,
        compiler_params=pltpu.CompilerParams(vmem_limit_bytes=MOST_VMEM),
    )(scalars, acts, other_acts, cotan, other_cotan, *after)


def hop_kernel(step, unused, *refs):
    mine, from_x = refs[:2]
    down = mine[0] + decoded(from_x[0])
    up = mine[1] + decoded(from_x[1])
    if step > 0:
        down = down + decoded(refs[2][...])
        up = up + decoded(refs[3][...])
    refs[-3][...] = coded(down)
    refs[-2][...] = up if step == 3 else coded(up)
    refs[-1][...] = jnp.zeros_like(refs[-1])


def hop(step, mine, from_x, received, after):
    _, rows, columns = mine.shape
    wide = columns + LANES
    whole = pl.BlockSpec((rows, wide), lambda i: (0, 0))
    sent = jax.ShapeDtypeStruct((rows, wide), jnp.int16)
    last = jax.ShapeDtypeStruct((rows, columns), jnp.float32) if step == 3 else sent
    return pl.pallas_call(
        functools.partial(hop_kernel, step, len(after)),
        grid=(1,),
        in_specs=[
            pl.BlockSpec((2, rows, columns), lambda i: (step, 0, 0)),
            pl.BlockSpec((2, rows, wide), lambda i: (step % 2, 0, 0)),
        ]
        + [whole] * len(received)
        + [pl.BlockSpec(memory_space=pltpu.VMEM)] * len(after),
        out_specs=[whole] + [pl.BlockSpec(a.shape, lambda i: (0, 0)) for a in (last, MARK)],
        out_shape=[sent, last, MARK],
        cost_estimate=NO_COST,
        compiler_params=pltpu.CompilerParams(vmem_limit_bytes=VMEM),
    )(mine, from_x, *received, *after)


def total_kernel(core, up, down, kept, given, mark):
    total = up[...] + decoded(down[...])
    mark[...] = jnp.zeros_like(mark)
    rows = kept.shape[0]
    mine = jnp.where(core[0] == 0, 1.0, 0.0)
    kept[...] = jnp.where(mine > 0.5, total[:rows], total[rows:])
    given[...] = jnp.where(mine > 0.5, total[rows:], total[:rows])


def shifted(value, axis, steps):
    count = lax.axis_size(axis)
    return lax.ppermute(value, axis, [(i, (i + steps) % count) for i in range(count)])


def held(value, after, arrays=(), limit=VMEM):
    def body(*refs):
        pass

    anywhere = pl.BlockSpec(memory_space=pl.ANY)
    return pl.pallas_call(
        body,
        in_specs=[anywhere] * (1 + len(arrays))
        + [pl.BlockSpec(memory_space=pltpu.VMEM)] * len(after),
        out_specs=anywhere,
        out_shape=jax.ShapeDtypeStruct(value.shape, value.dtype),
        input_output_aliases={0: 0},
        cost_estimate=NO_COST,
        compiler_params=pltpu.CompilerParams(vmem_limit_bytes=limit),
    )(value, *arrays, *after)


def input_kernel(unused, at, cotan, weights, other_weights, *refs):
    out, mark = refs[unused:]
    mark[...] = jnp.zeros_like(mark)
    core, x, z = at[0], at[1], pl.program_id(0)
    wide = 2 * weights.shape[1]

    def planes(first, second):
        blocks = [first[0], second[0], first[1], second[1]]
        value = dot(cotan[...], jnp.concatenate(blocks, 0), NT).astype(jnp.bfloat16)
        for column in range(2):
            chip = (x * (1 - column) + (1 - x) * column) * 8 + z
            place = pl.ds(pl.multiple_of(chip * wide, wide), wide)
            out[:, place] = value[:, column * wide : (column + 1) * wide]

    @pl.when(core == 0)
    def _():
        planes(weights, other_weights)

    @pl.when(core == 1)
    def _():
        planes(other_weights, weights)


def backward_input(core, x, cotan, weights, other_weights, after):
    tokens, width = cotan.shape
    rows = weights.shape[1]
    plane = pl.BlockSpec((2, rows, width), lambda i, at: (i, 0, 0))
    return pl.pallas_call(
        functools.partial(input_kernel, len(after)),
        grid_spec=pltpu.PrefetchScalarGridSpec(
            num_scalar_prefetch=1,
            grid=(8,),
            in_specs=[pl.BlockSpec((tokens, width), lambda i, at: (0, 0)), plane, plane]
            + [pl.BlockSpec(memory_space=pltpu.VMEM)] * len(after),
            out_specs=[
                pl.BlockSpec((tokens, width), lambda i, at: (0, 0)),
                pl.BlockSpec(MARK.shape, lambda i, at: (0, 0)),
            ],
        ),
        out_shape=[jax.ShapeDtypeStruct((tokens, width), jnp.bfloat16), MARK],
        cost_estimate=NO_COST,
        compiler_params=pltpu.CompilerParams(vmem_limit_bytes=NO_ROOM),
    )(jnp.stack([core, x]).astype(jnp.int32), cotan, weights, other_weights, *after)


def update_kernel(core, weight, kept, taken, basis, right, left, from_right, from_left, out, out_q):
    next_right = right[...] - from_right[...]
    next_left = from_left[...] - left[...]
    out_q[...] = next_right
    moves = (
        basis[:, 0:1] * next_right[0:1]
        + basis[:, 1:2] * next_right[1:2]
        - basis[:, 2:3] * next_left[0:1]
        - basis[:, 3:4] * next_left[1:2]
    )
    stepped = weight[...].astype(jnp.float32) - GOSSIP * moves
    columns = kept.shape[1]
    swapped = jnp.broadcast_to(core[0], kept.shape) == 1
    first = jnp.where(swapped, taken[...], kept[...])
    second = jnp.where(swapped, kept[...], taken[...])
    out[:, :columns] = stepped[:, :columns] - LEARN * first
    out[:, columns:] = stepped[:, columns:] - LEARN * second


def on_device(activ, grad_out, weight, q_seed):
    acts = activ[0]
    cotan = grad_out[0]
    weight_bf = weight[0]
    rows, width = weight_bf.shape
    columns = width // 2
    core, x, z = lax.axis_index("core"), lax.axis_index("xl"), lax.axis_index("z")
    own = lax.axis_index(SHARD)
    replica = lax.axis_index(CYCLE)
    cycle_size = lax.axis_size(CYCLE)

    other_acts = partner(acts, "core", 1)
    other_cotan = partner(cotan, "core", 1)
    tokens = (acts, other_acts, cotan, other_cotan)

    q_right = lax.dynamic_index_in_dim(q_seed, replica, 0, keepdims=False)
    q_left = lax.dynamic_index_in_dim(
        q_seed, (replica + cycle_size - 1) % cycle_size, 0, keepdims=False
    )
    probes = jnp.concatenate([q_right, q_left], 1).astype(jnp.bfloat16).T
    probes = jnp.pad(probes, ((0, 12), (0, 0)))
    at = own[None].astype(jnp.int32)
    part = kernel_call(probe_kernel, (probes, acts, cotan, weight_bf), f32(4, width), at)

    place = [(z + offset) % 8 for step in range(4) for offset in (4 + step, 3 - step)]
    scalars = jnp.stack(place + [1 - x, core]).astype(jnp.int32)
    mine_scalars = jnp.stack(place + [x, core]).astype(jnp.int32)
    pieces = jax.ShapeDtypeStruct((4, 2 * rows, columns + LANES), jnp.int16)
    value = shard_sum(part, STEPS_ALONG[:1], {})

    pair = held(
        jnp.stack([weight_bf, partner(weight_bf, "xl", 1)], 0), (value,), (other_acts, other_cotan)
    )
    weights = lax.all_gather(pair, "z", axis=0, tiled=True)

    first, mark = chunks(
        functools.partial(chunk_kernel, 0), (pieces, MARK), scalars, *tokens, (value,)
    )
    value = shard_sum(value, STEPS_ALONG[1:2], {"xl1": (mark,)})
    first = partner(held(first, (value,)), "xl", 1)
    value = shard_sum(value, STEPS_ALONG[2:3], {})
    mine, mark = chunks(
        mine_kernel, (f32(8, 2 * rows, columns), MARK), mine_scalars, *tokens, (value,)
    )

    def hops(step, received, after, from_x):
        down, up, mark = hop(step, mine, from_x, received, after)
        return (shifted(down, "z", -1), shifted(up, "z", 1) if step < 3 else up), (mark,)

    value = shard_sum(value, STEPS_ALONG[3:4], {"z2": (mark,)})
    second, mark = chunks(
        functools.partial(chunk_kernel, 4), (pieces, MARK), scalars, *tokens, (value,)
    )
    right, left = shard_sum(value, STEPS_ALONG[4:], {"z4": (mark,)}, "z4")
    arrived = neighbours(right, left)
    received, sent = hops(0, (), arrived, first)
    second = partner(held(second, sent), "xl", 1)
    back, basis = kernel_call(
        basis_kernel,
        (right, left, *arrived, acts, cotan, weight_bf),
        (f32(4, width), f32(8, rows)),
        at,
        sent,
    )
    value = shard_sum(back, STEPS_BACK[:2], {})
    received, sent = hops(1, received, (value,), first)
    value = shard_sum(value, STEPS_BACK[2:3], {"z2": sent})
    received, sent = hops(2, received, (value,), second)
    weights = held(weights, sent, (), NO_ROOM)
    right, left = shard_sum(value, STEPS_BACK[3:], {"z4": sent}, "xl1")
    received, sent = hops(3, received, (right,), second)
    arrived = neighbours(right, left)
    grad_in, mark = backward_input(
        core, x, cotan, weights, partner(weights, "core", 1), sent
    )
    kept, given, _ = kernel_call(
        total_kernel,
        (received[1], received[0]),
        (f32(rows, columns), f32(rows, columns), MARK),
        core[None].astype(jnp.int32),
        (mark, *arrived),
    )
    new_weight, next_q = kernel_call(
        update_kernel,
        (weight_bf, kept, partner(given, "core", 1), basis.T, right, left, *arrived),
        (f32(rows, width), f32(2, width)),
        core[None].astype(jnp.int32),
        (mark,),
    )
    return (grad_in[None], new_weight[None], next_q.T[None])


def solution(mesh):
    fine = Mesh(mesh.devices.reshape(2, 4, 2, 8, 2), CYCLE + SHARD)
    tokens = P(CYCLE, SHARD, None)
    return jax.shard_map(
        on_device,
        mesh=fine,
        in_specs=(tokens, tokens, tokens, P()),
        out_specs=(tokens, tokens, P(CYCLE, None, None)),
        check_vma=False,
    )
```

profile of v0, /device:TPU:1, one launch (start us, length us, event | category | flops | bytes accessed | tf_op | source)
XLA Modules:
  0.0 143.1 jit_solution(12750920209519747763)
XLA Ops:
  7.2 3.3 %collective-permute-start.2 = (bf16[512,2048]{1,0:T(8,128)(2,1)}, bf16[512,2048]{1,0:T(8,128)(2,1)}, u32[]{:S(2)}, u32[]{:S(2)}) collective-permute-start(bf16[512,2048]{1,0:T(8,128)(2,1)} %bitcast.28), channel_id=1, source_target_pairs={{0,1},{1,0},{2,3},{3,2},{4,5},{5,4},{6,7},{7,6},{8,9},{9,8},{10,11... | collective-permute-start | bytes 6291464 | tf_op jit(solution)/shard_map/ppermute | solution.py:130
  11.5 1.6 %copy-done = bf16[1,512,2048]{2,1,0:T(8,128)(2,1)S(1)} copy-done((bf16[1,512,2048]{2,1,0:T(8,128)(2,1)S(1)}, bf16[1,512,2048]{2,1,0:T(8,128)(2,1)}, u32[]{:S(2)}) %copy-start) | copy-done | bytes 2097176
  13.1 1.6 %copy-done.4 = bf16[1,512,2048]{2,1,0:T(8,128)(2,1)S(1)} copy-done((bf16[1,512,2048]{2,1,0:T(8,128)(2,1)S(1)}, bf16[1,512,2048]{2,1,0:T(8,128)(2,1)}, u32[]{:S(2)}) %copy-start.4) | copy-done | bytes 2097176
  15.6 1.4 shard_map.67.refs_0_
  19.2 1.8 %collective-permute-start.4 = (f32[4,2048]{1,0:T(4,128)S(1)}, f32[4,2048]{1,0:T(4,128)S(1)}, u32[]{:S(2)}, u32[]{:S(2)}) collective-permute-start(f32[4,2048]{1,0:T(4,128)S(1)} %shard_map.68.refs_3_.refs_4_.refs_0_), channel_id=1, source_target_pairs={{0,16},{16,0},{1,17},{17,1},{2,18},{18,2},{3,19},{19,3},{4,20},{20... | collective-permute-start | bytes 98312 | tf_op jit(solution)/shard_map/ppermute | solution.py:130
  21.2 1.6 %copy-done.5 = bf16[1,512,2048]{2,1,0:T(8,128)(2,1)S(1)} copy-done((bf16[1,512,2048]{2,1,0:T(8,128)(2,1)S(1)}, bf16[1,512,2048]{2,1,0:T(8,128)(2,1)}, u32[]{:S(2)}) %copy-start.5) | copy-done | bytes 2097176
  22.7 5.0 %shard_map.70 = (s16[4,128,1152]{2,1,0:T(8,128)(2,1)}, f32[8,128]{1,0:T(8,128)S(1)}) custom-call(s32[10]{0:T(128)S(1)} %stack.74.place, bf16[512,2048]{1,0:T(8,128)(2,1)S(1)} %bitcast.37, bf16[512,2048]{1,0:T(8,128)(2,1)} %collective-permute-done.1.refs_1_, bf16[512,2048]{1,0:T(8,128)(2,1)S(1)} %bitcast.31, ...), custom_call_target="tpu_custom_call" | custom-call | tf_op jit(solution)/shard_map/pallas_call | solution.py:217
  27.8 1.4 %collective-permute-start.7 = (s16[4,128,1152]{2,1,0:T(8,128)(2,1)}, s16[4,128,1152]{2,1,0:T(8,128)(2,1)S(1)}, u32[]{:S(2)}, u32[]{:S(2)}) collective-permute-start(s16[4,128,1152]{2,1,0:T(8,128)(2,1)} %shard_map.76), channel_id=1, source_target_pairs={{0,16},{16,0},{1,17},{17,1},{2,18},{18,2},{3,19},{19,3},{4,20},{20... | collective-permute-start | bytes 3538952 | tf_op jit(solution)/shard_map/ppermute | solution.py:130
  29.3 3.1 %collective-permute-done.5.refs_1_ = f32[4,2048]{1,0:T(4,128)S(1)} collective-permute-done((f32[4,2048]{1,0:T(4,128)S(1)}, f32[4,2048]{1,0:T(4,128)S(1)}, u32[]{:S(2)}, u32[]{:S(2)}) %collective-permute-start.5) | collective-permute-done | bytes 32800 | tf_op jit(solution)/shard_map/ppermute | solution.py:130
  33.5 1.6 %copy-done.6 = bf16[1,512,2048]{2,1,0:T(8,128)(2,1)S(1)} copy-done((bf16[1,512,2048]{2,1,0:T(8,128)(2,1)S(1)}, bf16[1,512,2048]{2,1,0:T(8,128)(2,1)}, u32[]{:S(2)}) %copy-start.6) | copy-done | bytes 2097176
  35.1 4.6 %shard_map.73 = (f32[8,128,1024]{2,1,0:T(8,128)S(1)}, f32[8,128]{1,0:T(8,128)S(1)}) custom-call(s32[10]{0:T(128)S(1)} %stack.72.place, bf16[512,2048]{1,0:T(8,128)(2,1)S(1)} %bitcast.38, bf16[512,2048]{1,0:T(8,128)(2,1)} %collective-permute-done.1.refs_1_, bf16[512,2048]{1,0:T(8,128)(2,1)S(1)} %bitcast.32, ...), custom_call_target="tpu_custom_call" | custom-call | tf_op jit(solution)/shard_map/pallas_call | solution.py:217
  39.7 5.3 %collective-permute-start.8 = (f32[4,2048]{1,0:T(4,128)S(1)}, f32[4,2048]{1,0:T(4,128)S(1)}, u32[]{:S(2)}, u32[]{:S(2)}) collective-permute-start(f32[4,2048]{1,0:T(4,128)S(1)} %shard_map.74.refs_4_.refs_0_), channel_id=1, source_target_pairs={{0,8},{2,10},{4,12},{6,14},{8,0},{10,2},{12,4},{14,6},{1,9},{3,11}... | collective-permute-start | bytes 98312 | tf_op jit(solution)/shard_map/ppermute | solution.py:130
  45.0 4.0 %shard_map.75 = (s16[4,128,1152]{2,1,0:T(8,128)(2,1)S(1)}, f32[8,128]{1,0:T(8,128)S(1)}) custom-call(s32[10]{0:T(128)S(1)} %stack.74.place, bf16[512,2048]{1,0:T(8,128)(2,1)S(1)} %bitcast.39, bf16[512,2048]{1,0:T(8,128)(2,1)} %collective-permute-done.1.refs_1_, bf16[512,2048]{1,0:T(8,128)(2,1)S(1)} %bitcast.33, ...), custom_call_target="tpu_custom_call" | custom-call | tf_op jit(solution)/shard_map/pallas_call | solution.py:217
  49.0 1.4 collective-permute-start.10
  50.4 4.0 %collective-permute-start.9 = (f32[2,2048]{1,0:T(2,128)S(1)}, f32[2,2048]{1,0:T(2,128)S(1)}, u32[]{:S(2)}, u32[]{:S(2)}) collective-permute-start(f32[2,2048]{1,0:T(2,128)S(1)} %get-tuple-element.39.refs_2_), channel_id=1, source_target_pairs={{0,240},{16,224},{32,0},{48,16},{64,32},{80,48},{96,64},{112,80},{... | collective-permute-start | bytes 49160 | tf_op jit(solution)/shard_map/ppermute | solution.py:152
  56.5 1.3 collective-permute-start.11
  57.8 3.6 %collective-permute-start.12 = (s16[128,1152]{1,0:T(8,128)(2,1)S(1)}, s16[128,1152]{1,0:T(8,128)(2,1)S(1)}, u32[]{:S(2)}, u32[]{:S(2)}) collective-permute-start(s16[128,1152]{1,0:T(8,128)(2,1)S(1)} %get-tuple-element.42), channel_id=1, source_target_pairs={{0,14},{2,0},{4,2},{6,4},{8,6},{10,8},{12,10},{14,12},{1,15},{3,1}... | collective-permute-start | bytes 884744 | tf_op jit(solution)/shard_map/ppermute | solution.py:282
  61.4 2.1 %shard_map.80 = (f32[4,2048]{1,0:T(4,128)S(1)}, f32[8,64]{1,0:T(8,128)S(1)}) custom-call(s32[1]{0:T(128)} %bitcast.6.refs_0_, f32[2,2048]{1,0:T(2,128)S(1)} %get-tuple-element.40.refs_1_, f32[2,2048]{1,0:T(2,128)S(1)} %get-tuple-element.39.refs_2_, f32[2,2048]{1,0:T(2,128)S(1)} %collective-permute-done.9.refs_2_.refs_3_, ...), custom_call_target="tpu_custom_call" | custom-call | tf_op jit(solution)/shard_map/pallas_call | solution.py:70
  63.5 2.0 %collective-permute-start.14 = (f32[4,2048]{1,0:T(4,128)S(1)}, f32[4,2048]{1,0:T(4,128)S(1)}, u32[]{:S(2)}, u32[]{:S(2)}) collective-permute-start(f32[4,2048]{1,0:T(4,128)S(1)} %get-tuple-element.44.refs_0_), channel_id=1, source_target_pairs={{0,1},{1,0},{2,3},{3,2},{4,5},{5,4},{6,7},{7,6},{8,9},{9,8},{10,11... | collective-permute-start | bytes 98312 | tf_op jit(solution)/shard_map/ppermute | solution.py:130
  66.4 8.6 %collective-permute-done.15.refs_1_ = f32[4,2048]{1,0:T(4,128)S(1)} collective-permute-done((f32[4,2048]{1,0:T(4,128)S(1)}, f32[4,2048]{1,0:T(4,128)S(1)}, u32[]{:S(2)}, u32[]{:S(2)}) %collective-permute-start.15) | collective-permute-done | bytes 32800 | tf_op jit(solution)/shard_map/ppermute | solution.py:130
  75.0 2.3 %collective-permute-done.13.refs_3_ = s16[128,1152]{1,0:T(8,128)(2,1)S(1)} collective-permute-done((s16[128,1152]{1,0:T(8,128)(2,1)S(1)}, s16[128,1152]{1,0:T(8,128)(2,1)S(1)}, u32[]{:S(2)}, u32[]{:S(2)}) %collective-permute-start.13) | collective-permute-done | bytes 294944 | tf_op jit(solution)/shard_map/ppermute | solution.py:282
  79.4 10.8 %collective-permute-done.18.refs_1_ = f32[4,2048]{1,0:T(4,128)S(1)} collective-permute-done((f32[4,2048]{1,0:T(4,128)S(1)}, f32[4,2048]{1,0:T(4,128)S(1)}, u32[]{:S(2)}, u32[]{:S(2)}) %collective-permute-start.18) | collective-permute-done | bytes 32800 | tf_op jit(solution)/shard_map/ppermute | solution.py:130
  92.4 1.9 %collective-permute-start.19 = (bf16[16,64,2048]{2,1,0:T(8,128)(2,1)}, bf16[16,64,2048]{2,1,0:T(8,128)(2,1)}, u32[]{:S(2)}, u32[]{:S(2)}) collective-permute-start(bf16[16,64,2048]{2,1,0:T(8,128)(2,1)} %shard_map.86.weights), channel_id=1, source_target_pairs={{0,1},{1,0},{2,3},{3,2},{4,5},{5,4},{6,7},{7,6},{8,9},{9,8},{10,11... | collective-permute-start | bytes 12582920 | tf_op jit(solution)/shard_map/ppermute | solution.py:130
  94.2 2.7 %collective-permute-start.20 = (s16[128,1152]{1,0:T(8,128)(2,1)S(1)}, s16[128,1152]{1,0:T(8,128)(2,1)S(1)}, u32[]{:S(2)}, u32[]{:S(2)}) collective-permute-start(s16[128,1152]{1,0:T(8,128)(2,1)S(1)} %get-tuple-element.49), channel_id=1, source_target_pairs={{0,14},{2,0},{4,2},{6,4},{8,6},{10,8},{12,10},{14,12},{1,15},{3,1}... | collective-permute-start | bytes 884744 | tf_op jit(solution)/shard_map/ppermute | solution.py:282
  96.9 2.8 %collective-permute-start.22 = (f32[4,2048]{1,0:T(4,128)S(1)}, f32[4,2048]{1,0:T(4,128)S(1)}, u32[]{:S(2)}, u32[]{:S(2)}) collective-permute-start(f32[4,2048]{1,0:T(4,128)S(1)} %shard_map.84.refs_4_.refs_0_), channel_id=1, source_target_pairs={{0,8},{2,10},{4,12},{6,14},{8,0},{10,2},{12,4},{14,6},{1,9},{3,11}... | collective-permute-start | bytes 98312 | tf_op jit(solution)/shard_map/ppermute | solution.py:130
  99.7 8.0 %collective-permute-done.22.refs_1_ = f32[4,2048]{1,0:T(4,128)S(1)} collective-permute-done((f32[4,2048]{1,0:T(4,128)S(1)}, f32[4,2048]{1,0:T(4,128)S(1)}, u32[]{:S(2)}, u32[]{:S(2)}) %collective-permute-start.22) | collective-permute-done | bytes 32800 | tf_op jit(solution)/shard_map/ppermute | solution.py:130
  107.7 1.3 collective-permute-start.23
  109.0 1.6 %collective-permute-done.23.refs_1_ = f32[4,2048]{1,0:T(4,128)S(1)} collective-permute-done((f32[4,2048]{1,0:T(4,128)S(1)}, f32[4,2048]{1,0:T(4,128)S(1)}, u32[]{:S(2)}, u32[]{:S(2)}) %collective-permute-start.23) | collective-permute-done | bytes 32800 | tf_op jit(solution)/shard_map/ppermute | solution.py:130
  111.7 1.2 collective-permute-start.26
  112.9 3.6 %collective-permute-start.25 = (f32[2,2048]{1,0:T(2,128)S(1)}, f32[2,2048]{1,0:T(2,128)S(1)}, u32[]{:S(2)}, u32[]{:S(2)}) collective-permute-start(f32[2,2048]{1,0:T(2,128)S(1)} %get-tuple-element.57.refs_6_), channel_id=1, source_target_pairs={{0,240},{16,224},{32,0},{48,16},{64,32},{80,48},{96,64},{112,80},{... | collective-permute-start | bytes 49160 | tf_op jit(solution)/shard_map/ppermute | solution.py:152
  117.1 11.7 %shard_map.90 = (bf16[512,2048]{1,0:T(8,128)(2,1)}, f32[8,128]{1,0:T(8,128)}) custom-call(s32[2]{0:T(128)} %pad_add_fusion.at, bf16[512,2048]{1,0:T(8,128)(2,1)} %bitcast.29, bf16[16,64,2048]{2,1,0:T(8,128)(2,1)} %shard_map.86.weights, bf16[16,64,2048]{2,1,0:T(8,128)(2,1)} %collective-permute-done.19.other_weights, f32[8,128]{1,0:T(8,128)} %copy-done.15), custom_call_target="tpu_custom_call" | custom-call | tf_op jit(solution)/shard_map/pallas_call | solution.py:329
  130.1 3.1 %collective-permute-start.27 = (f32[64,1024]{1,0:T(8,128)S(1)}, f32[64,1024]{1,0:T(8,128)S(1)}, u32[]{:S(2)}, u32[]{:S(2)}) collective-permute-start(f32[64,1024]{1,0:T(8,128)S(1)} %get-tuple-element.59), channel_id=1, source_target_pairs={{0,1},{1,0},{2,3},{3,2},{4,5},{5,4},{6,7},{7,6},{8,9},{9,8},{10,11... | collective-permute-start | bytes 786440 | tf_op jit(solution)/shard_map/ppermute | solution.py:130
  (93 shorter events, 18.7 us)
Async XLA Ops:
  7.2 84.4 %all-gather.2.cloned.1.call-start = ((), (), s32[]{:S(2)}) async-start(), calls=%async_computation | async-start | bytes 4718592 | tf_op jit(solution)/shard_map/all_gather | solution.py:399
  7.2 12.0 %collective-permute-start.2 = (bf16[512,2048]{1,0:T(8,128)(2,1)}, bf16[512,2048]{1,0:T(8,128)(2,1)}, u32[]{:S(2)}, u32[]{:S(2)}) collective-permute-start(bf16[512,2048]{1,0:T(8,128)(2,1)} %bitcast.28), channel_id=1, source_target_pairs={{0,1},{1,0},{2,3},{3,2},{4,5},{5,4},{6,7},{7,6},{8,9},{9,8},{10,11... | collective-permute-start | bytes 6291464 | tf_op jit(solution)/shard_map/ppermute | solution.py:130
  10.5 8.7 %collective-permute-start.1 = (bf16[512,2048]{1,0:T(8,128)(2,1)}, bf16[512,2048]{1,0:T(8,128)(2,1)}, u32[]{:S(2)}, u32[]{:S(2)}) collective-permute-start(bf16[512,2048]{1,0:T(8,128)(2,1)} %bitcast.35), channel_id=1, source_target_pairs={{0,1},{1,0},{2,3},{3,2},{4,5},{5,4},{6,7},{7,6},{8,9},{9,8},{10,11... | collective-permute-start | bytes 6291464 | tf_op jit(solution)/shard_map/ppermute | solution.py:130
  10.6 7.7 %collective-permute-start = (bf16[64,2048]{1,0:T(8,128)(2,1)}, bf16[64,2048]{1,0:T(8,128)(2,1)S(1)}, u32[]{:S(2)}, u32[]{:S(2)}) collective-permute-start(bf16[64,2048]{1,0:T(8,128)(2,1)} %bitcast.41), channel_id=1, source_target_pairs={{0,16},{16,0},{1,17},{17,1},{2,18},{18,2},{3,19},{19,3},{4,20},{20... | collective-permute-start | bytes 786440 | tf_op jit(solution)/shard_map/ppermute | solution.py:130
  17.0 1.4 collective-permute-start.3
  19.2 8.6 %collective-permute-start.4 = (f32[4,2048]{1,0:T(4,128)S(1)}, f32[4,2048]{1,0:T(4,128)S(1)}, u32[]{:S(2)}, u32[]{:S(2)}) collective-permute-start(f32[4,2048]{1,0:T(4,128)S(1)} %shard_map.68.refs_3_.refs_4_.refs_0_), channel_id=1, source_target_pairs={{0,16},{16,0},{1,17},{17,1},{2,18},{18,2},{3,19},{19,3},{4,20},{20... | collective-permute-start | bytes 98312 | tf_op jit(solution)/shard_map/ppermute | solution.py:130
  27.8 27.6 %collective-permute-start.7 = (s16[4,128,1152]{2,1,0:T(8,128)(2,1)}, s16[4,128,1152]{2,1,0:T(8,128)(2,1)S(1)}, u32[]{:S(2)}, u32[]{:S(2)}) collective-permute-start(s16[4,128,1152]{2,1,0:T(8,128)(2,1)} %shard_map.76), channel_id=1, source_target_pairs={{0,16},{16,0},{1,17},{17,1},{2,18},{18,2},{3,19},{19,3},{4,20},{20... | collective-permute-start | bytes 3538952 | tf_op jit(solution)/shard_map/ppermute | solution.py:130
  29.3 3.1 %collective-permute-start.5 = (f32[4,2048]{1,0:T(4,128)S(1)}, f32[4,2048]{1,0:T(4,128)S(1)}, u32[]{:S(2)}, u32[]{:S(2)}) collective-permute-start(f32[4,2048]{1,0:T(4,128)S(1)} %shard_map.71.refs_0_.refs_1_), channel_id=1, source_target_pairs={{0,2},{2,0},{4,6},{6,4},{8,10},{10,8},{12,14},{14,12},{1,3},{3,1},... | collective-permute-start | bytes 98312 | tf_op jit(solution)/shard_map/ppermute | solution.py:130
  32.3 7.4 %collective-permute-start.6 = (f32[4,2048]{1,0:T(4,128)S(1)}, f32[4,2048]{1,0:T(4,128)S(1)}, u32[]{:S(2)}, u32[]{:S(2)}) collective-permute-start(f32[4,2048]{1,0:T(4,128)S(1)} %shard_map.72.refs_4_.refs_0_), channel_id=1, source_target_pairs={{0,4},{2,6},{4,0},{6,2},{8,12},{10,14},{12,8},{14,10},{1,5},{3,7},... | collective-permute-start | bytes 98312 | tf_op jit(solution)/shard_map/ppermute | solution.py:130
  39.7 50.6 %copy-start.2 = (f32[8,128,1024]{2,1,0:T(8,128)}, f32[8,128,1024]{2,1,0:T(8,128)S(1)}, u32[]{:S(2)}) copy-start(f32[8,128,1024]{2,1,0:T(8,128)S(1)} %get-tuple-element.34.refs_0_) | copy-start | bytes 12582916
  39.7 9.3 %collective-permute-start.8 = (f32[4,2048]{1,0:T(4,128)S(1)}, f32[4,2048]{1,0:T(4,128)S(1)}, u32[]{:S(2)}, u32[]{:S(2)}) collective-permute-start(f32[4,2048]{1,0:T(4,128)S(1)} %shard_map.74.refs_4_.refs_0_), channel_id=1, source_target_pairs={{0,8},{2,10},{4,12},{6,14},{8,0},{10,2},{12,4},{14,6},{1,9},{3,11}... | collective-permute-start | bytes 98312 | tf_op jit(solution)/shard_map/ppermute | solution.py:130
  49.0 6.4 %collective-permute-start.10 = (f32[2,2048]{1,0:T(2,128)S(1)}, f32[2,2048]{1,0:T(2,128)S(1)}, u32[]{:S(2)}, u32[]{:S(2)}) collective-permute-start(f32[2,2048]{1,0:T(2,128)S(1)} %get-tuple-element.40.refs_1_), channel_id=1, source_target_pairs={{0,32},{16,48},{32,64},{48,80},{64,96},{80,112},{96,144},{112,128}... | collective-permute-start | bytes 49160 | tf_op jit(solution)/shard_map/ppermute | solution.py:152
  50.4 5.0 %collective-permute-start.9 = (f32[2,2048]{1,0:T(2,128)S(1)}, f32[2,2048]{1,0:T(2,128)S(1)}, u32[]{:S(2)}, u32[]{:S(2)}) collective-permute-start(f32[2,2048]{1,0:T(2,128)S(1)} %get-tuple-element.39.refs_2_), channel_id=1, source_target_pairs={{0,240},{16,224},{32,0},{48,16},{64,32},{80,48},{96,64},{112,80},{... | collective-permute-start | bytes 49160 | tf_op jit(solution)/shard_map/ppermute | solution.py:152
  56.5 33.8 %collective-permute-start.11 = (s16[4,128,1152]{2,1,0:T(8,128)(2,1)S(1)}, s16[4,128,1152]{2,1,0:T(8,128)(2,1)S(1)}, u32[]{:S(2)}, u32[]{:S(2)}) collective-permute-start(s16[4,128,1152]{2,1,0:T(8,128)(2,1)S(1)} %shard_map.79), channel_id=1, source_target_pairs={{0,16},{16,0},{1,17},{17,1},{2,18},{18,2},{3,19},{19,3},{4,20},{20... | collective-permute-start | bytes 3538952 | tf_op jit(solution)/shard_map/ppermute | solution.py:130
  57.8 17.2 %collective-permute-start.12 = (s16[128,1152]{1,0:T(8,128)(2,1)S(1)}, s16[128,1152]{1,0:T(8,128)(2,1)S(1)}, u32[]{:S(2)}, u32[]{:S(2)}) collective-permute-start(s16[128,1152]{1,0:T(8,128)(2,1)S(1)} %get-tuple-element.42), channel_id=1, source_target_pairs={{0,14},{2,0},{4,2},{6,4},{8,6},{10,8},{12,10},{14,12},{1,15},{3,1}... | collective-permute-start | bytes 884744 | tf_op jit(solution)/shard_map/ppermute | solution.py:282
  61.4 15.8 %collective-permute-start.13 = (s16[128,1152]{1,0:T(8,128)(2,1)S(1)}, s16[128,1152]{1,0:T(8,128)(2,1)S(1)}, u32[]{:S(2)}, u32[]{:S(2)}) collective-permute-start(s16[128,1152]{1,0:T(8,128)(2,1)S(1)} %get-tuple-element.43), channel_id=1, source_target_pairs={{0,2},{2,4},{4,6},{6,8},{8,10},{10,12},{12,14},{14,0},{1,3},{3,5},... | collective-permute-start | bytes 884744 | tf_op jit(solution)/shard_map/ppermute | solution.py:282
  63.5 2.8 %collective-permute-start.14 = (f32[4,2048]{1,0:T(4,128)S(1)}, f32[4,2048]{1,0:T(4,128)S(1)}, u32[]{:S(2)}, u32[]{:S(2)}) collective-permute-start(f32[4,2048]{1,0:T(4,128)S(1)} %get-tuple-element.44.refs_0_), channel_id=1, source_target_pairs={{0,1},{1,0},{2,3},{3,2},{4,5},{5,4},{6,7},{7,6},{8,9},{9,8},{10,11... | collective-permute-start | bytes 98312 | tf_op jit(solution)/shard_map/ppermute | solution.py:130
  66.4 8.6 %collective-permute-start.15 = (f32[4,2048]{1,0:T(4,128)S(1)}, f32[4,2048]{1,0:T(4,128)S(1)}, u32[]{:S(2)}, u32[]{:S(2)}) collective-permute-start(f32[4,2048]{1,0:T(4,128)S(1)} %shard_map.81.refs_0_), channel_id=1, source_target_pairs={{0,2},{2,0},{4,6},{6,4},{8,10},{10,8},{12,14},{14,12},{1,3},{3,1},... | collective-permute-start | bytes 98312 | tf_op jit(solution)/shard_map/ppermute | solution.py:130
  77.9 12.4 %collective-permute-start.16 = (s16[128,1152]{1,0:T(8,128)(2,1)S(1)}, s16[128,1152]{1,0:T(8,128)(2,1)S(1)}, u32[]{:S(2)}, u32[]{:S(2)}) collective-permute-start(s16[128,1152]{1,0:T(8,128)(2,1)S(1)} %get-tuple-element.45), channel_id=1, source_target_pairs={{0,14},{2,0},{4,2},{6,4},{8,6},{10,8},{12,10},{14,12},{1,15},{3,1}... | collective-permute-start | bytes 884744 | tf_op jit(solution)/shard_map/ppermute | solution.py:282
  78.9 11.3 %collective-permute-start.17 = (s16[128,1152]{1,0:T(8,128)(2,1)S(1)}, s16[128,1152]{1,0:T(8,128)(2,1)S(1)}, u32[]{:S(2)}, u32[]{:S(2)}) collective-permute-start(s16[128,1152]{1,0:T(8,128)(2,1)S(1)} %get-tuple-element.46), channel_id=1, source_target_pairs={{0,2},{2,4},{4,6},{6,8},{8,10},{10,12},{12,14},{14,0},{1,3},{3,5},... | collective-permute-start | bytes 884744 | tf_op jit(solution)/shard_map/ppermute | solution.py:282
  79.4 10.8 %collective-permute-start.18 = (f32[4,2048]{1,0:T(4,128)S(1)}, f32[4,2048]{1,0:T(4,128)S(1)}, u32[]{:S(2)}, u32[]{:S(2)}) collective-permute-start(f32[4,2048]{1,0:T(4,128)S(1)} %shard_map.82.refs_4_.refs_0_), channel_id=1, source_target_pairs={{0,4},{2,6},{4,0},{6,2},{8,12},{10,14},{12,8},{14,10},{1,5},{3,7},... | collective-permute-start | bytes 98312 | tf_op jit(solution)/shard_map/ppermute | solution.py:130
  91.5 16.1 %copy-start.14 = (f32[8,128]{1,0:T(8,128)S(1)}, f32[8,128]{1,0:T(8,128)}, u32[]{:S(2)}) copy-start(f32[8,128]{1,0:T(8,128)} %copy-done.13) | copy-start | bytes 12292
  91.5 19.0 %copy-start.3 = (f32[8,128,1024]{2,1,0:T(8,128)S(1)}, f32[8,128,1024]{2,1,0:T(8,128)}, u32[]{:S(2)}) copy-start(f32[8,128,1024]{2,1,0:T(8,128)} %copy-done.2) | copy-start | bytes 12582916
  92.4 24.7 %collective-permute-start.19 = (bf16[16,64,2048]{2,1,0:T(8,128)(2,1)}, bf16[16,64,2048]{2,1,0:T(8,128)(2,1)}, u32[]{:S(2)}, u32[]{:S(2)}) collective-permute-start(bf16[16,64,2048]{2,1,0:T(8,128)(2,1)} %shard_map.86.weights), channel_id=1, source_target_pairs={{0,1},{1,0},{2,3},{3,2},{4,5},{5,4},{6,7},{7,6},{8,9},{9,8},{10,11... | collective-permute-start | bytes 12582920 | tf_op jit(solution)/shard_map/ppermute | solution.py:130
  94.2 16.3 %collective-permute-start.20 = (s16[128,1152]{1,0:T(8,128)(2,1)S(1)}, s16[128,1152]{1,0:T(8,128)(2,1)S(1)}, u32[]{:S(2)}, u32[]{:S(2)}) collective-permute-start(s16[128,1152]{1,0:T(8,128)(2,1)S(1)} %get-tuple-element.49), channel_id=1, source_target_pairs={{0,14},{2,0},{4,2},{6,4},{8,6},{10,8},{12,10},{14,12},{1,15},{3,1}... | collective-permute-start | bytes 884744 | tf_op jit(solution)/shard_map/ppermute | solution.py:282
  96.9 13.7 %collective-permute-start.21 = (s16[128,1152]{1,0:T(8,128)(2,1)S(1)}, s16[128,1152]{1,0:T(8,128)(2,1)S(1)}, u32[]{:S(2)}, u32[]{:S(2)}) collective-permute-start(s16[128,1152]{1,0:T(8,128)(2,1)S(1)} %get-tuple-element.50), channel_id=1, source_target_pairs={{0,2},{2,4},{4,6},{6,8},{8,10},{10,12},{12,14},{14,0},{1,3},{3,5},... | collective-permute-start | bytes 884744 | tf_op jit(solution)/shard_map/ppermute | solution.py:282
  96.9 10.8 %collective-permute-start.22 = (f32[4,2048]{1,0:T(4,128)S(1)}, f32[4,2048]{1,0:T(4,128)S(1)}, u32[]{:S(2)}, u32[]{:S(2)}) collective-permute-start(f32[4,2048]{1,0:T(4,128)S(1)} %shard_map.84.refs_4_.refs_0_), channel_id=1, source_target_pairs={{0,8},{2,10},{4,12},{6,14},{8,0},{10,2},{12,4},{14,6},{1,9},{3,11}... | collective-permute-start | bytes 98312 | tf_op jit(solution)/shard_map/ppermute | solution.py:130
  107.7 2.9 %collective-permute-start.23 = (f32[4,2048]{1,0:T(4,128)S(1)}, f32[4,2048]{1,0:T(4,128)S(1)}, u32[]{:S(2)}, u32[]{:S(2)}) collective-permute-start(f32[4,2048]{1,0:T(4,128)S(1)} %shard_map.87.refs_0_), channel_id=1, source_target_pairs={{0,16},{16,0},{1,17},{17,1},{2,18},{18,2},{3,19},{19,3},{4,20},{20... | collective-permute-start | bytes 98312 | tf_op jit(solution)/shard_map/ppermute | solution.py:130
  111.7 17.1 %collective-permute-start.24 = (s16[128,1152]{1,0:T(8,128)(2,1)S(1)}, s16[128,1152]{1,0:T(8,128)(2,1)S(1)}, u32[]{:S(2)}, u32[]{:S(2)}) collective-permute-start(s16[128,1152]{1,0:T(8,128)(2,1)S(1)} %get-tuple-element.55), channel_id=1, source_target_pairs={{0,14},{2,0},{4,2},{6,4},{8,6},{10,8},{12,10},{14,12},{1,15},{3,1}... | collective-permute-start | bytes 884744 | tf_op jit(solution)/shard_map/ppermute | solution.py:282
  111.7 17.1 %collective-permute-start.26 = (f32[2,2048]{1,0:T(2,128)S(1)}, f32[2,2048]{1,0:T(2,128)S(1)}, u32[]{:S(2)}, u32[]{:S(2)}) collective-permute-start(f32[2,2048]{1,0:T(2,128)S(1)} %get-tuple-element.51.refs_4_.refs_5_), channel_id=1, source_target_pairs={{0,32},{16,48},{32,64},{48,80},{64,96},{80,112},{96,144},{112,128}... | collective-permute-start | bytes 49160 | tf_op jit(solution)/shard_map/ppermute | solution.py:152
  112.9 15.9 %collective-permute-start.25 = (f32[2,2048]{1,0:T(2,128)S(1)}, f32[2,2048]{1,0:T(2,128)S(1)}, u32[]{:S(2)}, u32[]{:S(2)}) collective-permute-start(f32[2,2048]{1,0:T(2,128)S(1)} %get-tuple-element.57.refs_6_), channel_id=1, source_target_pairs={{0,240},{16,224},{32,0},{48,16},{64,32},{80,48},{96,64},{112,80},{... | collective-permute-start | bytes 49160 | tf_op jit(solution)/shard_map/ppermute | solution.py:152
  130.1 4.3 %collective-permute-start.27 = (f32[64,1024]{1,0:T(8,128)S(1)}, f32[64,1024]{1,0:T(8,128)S(1)}, u32[]{:S(2)}, u32[]{:S(2)}) collective-permute-start(f32[64,1024]{1,0:T(8,128)S(1)} %get-tuple-element.59), channel_id=1, source_target_pairs={{0,1},{1,0},{2,3},{3,2},{4,5},{5,4},{6,7},{7,6},{8,9},{9,8},{10,11... | collective-permute-start | bytes 786440 | tf_op jit(solution)/shard_map/ppermute | solution.py:130
  (13 other events, 33.7 us)
Sparse Core Ops, SparseCore 0:
  19.4 65.6 all-gather.1
where the time goes:
time: 144 us; the launch traced here: 143 us
  starting transfers between devices  43.9 us (30%)
  waiting for transfers between devices  38.2 us (27%)
  Pallas kernels  33.7 us (23%)
  between operations  14.3 us (10%)
  local copies, waits for them, and re-layouts  10.7 us (7%)
  other arithmetic  2.27 us (2%)
    ppermute x17, waiting for transfers between devices, partner(): return lax.ppermute(value, axis, [(i, i ^ step) for i in range(count)])  34.8 us
    ppermute x17, starting transfers between devices, partner(): return lax.ppermute(value, axis, [(i, i ^ step) for i in range(count)])  26 us
    pallas_call x3, Pallas kernels, chunks(): pl.pallas_call(body, grid_spec=pltpu.PrefetchScalarGridSpec(num_scalar_pr...  13.6 us
    pallas_call x1, Pallas kernels, backward_input(): pl.pallas_call(functools.partial(input_kernel, len(after)), grid_spec=plt...  11.7 us
    unnamed x32, local copies, waits for them, and re-layouts  10.4 us
    ppermute x4, starting transfers between devices, passed_along(): return lax.ppermute(value, CYCLE + ('xl',), pairs)  10.1 us
    ppermute x7, starting transfers between devices, shifted(): lax.ppermute(value, axis, [(i, (i + steps) % count) for i in range(count)])  7.81 us
    pallas_call x14, Pallas kernels, kernel_call(): pl.pallas_call(body, in_specs=specs, out_specs=jax.tree.map(lambda _: who...  5.3 us
  transfers between devices with their start and end apart: 29, of which 10 were waited for; matrix products, arithmetic and copies ran while one was open for 2% of the time, Pallas kernels for 22%

commit v1 on v0

--- a/solution.py
+++ b/solution.py
@@ -299,49 +299,51 @@
     )(value, *arrays, *after)
 
 
-def input_kernel(unused, at, cotan, weights, other_weights, *refs):
-    out, mark = refs[unused:]
+def input_kernel(at, cotan, weights, other_weights, *refs):
+    out, mark = refs[-2:]
     mark[...] = jnp.zeros_like(mark)
-    core, x, z = at[0], at[1], pl.program_id(0)
-    wide = 2 * weights.shape[1]
+    column = pl.program_id(1)
 
     def planes(first, second):
-        blocks = [first[0], second[0], first[1], second[1]]
-        value = dot(cotan[...], jnp.concatenate(blocks, 0), NT).astype(jnp.bfloat16)
-        for column in range(2):
-            chip = (x * (1 - column) + (1 - x) * column) * 8 + z
-            place = pl.ds(pl.multiple_of(chip * wide, wide), wide)
-            out[:, place] = value[:, column * wide : (column + 1) * wide]
-
-    @pl.when(core == 0)
+        blocks = [first[column], second[column], first[2 + column], second[2 + column]]
+        value = dot(cotan[...], jnp.concatenate(blocks, 0), NT)
+        out[...] = value.astype(jnp.bfloat16)
+
+    @pl.when(at[0] == 0)
     def _():
         planes(weights, other_weights)
 
-    @pl.when(core == 1)
+    @pl.when(at[0] == 1)
     def _():
         planes(other_weights, weights)
 
 
-def backward_input(core, x, cotan, weights, other_weights, after):
+def backward_input(core, x, first, cotan, weights, other_weights, after, into=()):
     tokens, width = cotan.shape
     rows = weights.shape[1]
-    plane = pl.BlockSpec((2, rows, width), lambda i, at: (i, 0, 0))
+    planes = pl.BlockSpec((4, rows, width), lambda i, j, at: (at[2] + i, 0, 0))
+    scalars = jnp.stack([core, x, jnp.full_like(core, first)]).astype(jnp.int32)
     return pl.pallas_call(
-        functools.partial(input_kernel, len(after)),
+        input_kernel,
         grid_spec=pltpu.PrefetchScalarGridSpec(
             num_scalar_prefetch=1,
-            grid=(8,),
-            in_specs=[pl.BlockSpec((tokens, width), lambda i, at: (0, 0)), plane, plane]
+            grid=(2, 2),
+            in_specs=[pl.BlockSpec((tokens, width), lambda i, j, at: (0, 0)), planes, planes]
+            + [pl.BlockSpec(memory_space=pl.ANY)] * len(into)
             + [pl.BlockSpec(memory_space=pltpu.VMEM)] * len(after),
             out_specs=[
-                pl.BlockSpec((tokens, width), lambda i, at: (0, 0)),
-                pl.BlockSpec(MARK.shape, lambda i, at: (0, 0)),
+                pl.BlockSpec(
+                    (tokens, width // 8),
+                    lambda i, j, at: (0, 4 * (at[1] * (1 - j) + (1 - at[1]) * j) + at[2] + i),
+                ),
+                pl.BlockSpec(MARK.shape, lambda i, j, at: (0, 0)),
             ],
         ),
         out_shape=[jax.ShapeDtypeStruct((tokens, width), jnp.bfloat16), MARK],
+        input_output_aliases={4: 0} if into else {},
         cost_estimate=NO_COST,
         compiler_params=pltpu.CompilerParams(vmem_limit_bytes=NO_ROOM),
-    )(jnp.stack([core, x]).astype(jnp.int32), cotan, weights, other_weights, *after)
+    )(scalars, cotan, weights, other_weights, *into, *after)
 
 
 def update_kernel(core, weight, kept, taken, basis, right, left, from_right, from_left, out, out_q):
@@ -432,12 +434,12 @@
     value = shard_sum(value, STEPS_BACK[2:3], {"z2": sent})
     received, sent = hops(2, received, (value,), second)
     weights = held(weights, sent, (), NO_ROOM)
-    right, left = shard_sum(value, STEPS_BACK[3:], {"z4": sent}, "xl1")
+    both = (cotan, weights, partner(weights, "core", 1))
+    half, mark = backward_input(core, x, 0, *both, sent)
+    right, left = shard_sum(value, STEPS_BACK[3:], {"z4": (mark,)}, "xl1")
     received, sent = hops(3, received, (right,), second)
     arrived = neighbours(right, left)
-    grad_in, mark = backward_input(
-        core, x, cotan, weights, partner(weights, "core", 1), sent
-    )
+    grad_in, mark = backward_input(core, x, 2, *both, sent, (half,))
     kept, given, _ = kernel_call(
         total_kernel,
         (received[1], received[0]),

time: 144 us -> 144 us (level)
  waiting for transfers between devices: 38.2 us -> 30.7 us
  Pallas kernels: 33.7 us -> 37.6 us
  starting transfers between devices: 43.9 us -> 46.6 us
    ppermute x17, waiting for transfers between devices: 34.8 us -> 23.2 us  [partner(): return lax.ppermute(value, axis, [(i, i ^ step) for i in range(count)])]
    ppermute x4, waiting for transfers between devices: 1.05 us -> 5.91 us  [passed_along(): return lax.ppermute(value, CYCLE + ('xl',), pairs)]
    ppermute x17, starting transfers between devices: 26 us -> 30.2 us  [partner(): return lax.ppermute(value, axis, [(i, i ^ step) for i in range(count)])]
    pallas_call x1 -> x2, Pallas kernels: 11.7 us -> 15.7 us  [backward_input(): pl.pallas_call(input_kernel, grid_spec=pltpu.PrefetchScalarGridSpec(num_s...]
    ppermute x7, starting transfers between devices: 7.81 us -> 6.24 us  [shifted(): lax.ppermute(value, axis, [(i, (i + steps) % count) for i in range(count)])]
  transfers between devices with their start and end apart: 29 -> 29, of which waited for: 10 -> 11; matrix products, arithmetic and copies ran while one was open for 2% -> 2% of each run, Pallas kernels for 22% -> 24%
where the time goes in v1:
time: 144 us; the launch traced here: 143 us
  starting transfers between devices  46.6 us (32%)
  Pallas kernels  37.6 us (26%)
  waiting for transfers between devices  30.7 us (21%)
  between operations  14.3 us (10%)
  local copies, waits for them, and re-layouts  11.3 us (8%)
  other arithmetic  2.84 us (2%)
    ppermute x17, starting transfers between devices, partner(): return lax.ppermute(value, axis, [(i, i ^ step) for i in range(count)])  30.2 us
    ppermute x17, waiting for transfers between devices, partner(): return lax.ppermute(value, axis, [(i, i ^ step) for i in range(count)])  23.2 us
    pallas_call x2, Pallas kernels, backward_input(): pl.pallas_call(input_kernel, grid_spec=pltpu.PrefetchScalarGridSpec(num_s...  15.7 us
    pallas_call x3, Pallas kernels, chunks(): pl.pallas_call(body, grid_spec=pltpu.PrefetchScalarGridSpec(num_scalar_pr...  13.6 us
    unnamed x32, local copies, waits for them, and re-layouts  11.1 us
    ppermute x4, starting transfers between devices, passed_along(): return lax.ppermute(value, CYCLE + ('xl',), pairs)  10 us
    ppermute x7, starting transfers between devices, shifted(): lax.ppermute(value, axis, [(i, (i + steps) % count) for i in range(count)])  6.24 us
    ppermute x4, waiting for transfers between devices, passed_along(): return lax.ppermute(value, CYCLE + ('xl',), pairs)  5.91 us
  transfers between devices with their start and end apart: 29, of which 11 were waited for; matrix products, arithmetic and copies ran while one was open for 2% of the time, Pallas kernels for 24%

profile of v1, /device:TPU:1, one launch (start us, length us, event | category | flops | bytes accessed | tf_op | source)
XLA Modules:
  0.0 143.4 jit_solution(1864301605300917300)
XLA Ops:
  7.2 3.3 %collective-permute-start.1 = (bf16[512,2048]{1,0:T(8,128)(2,1)}, bf16[512,2048]{1,0:T(8,128)(2,1)}, u32[]{:S(2)}, u32[]{:S(2)}) collective-permute-start(bf16[512,2048]{1,0:T(8,128)(2,1)} %bitcast.36), channel_id=1, source_target_pairs={{0,1},{1,0},{2,3},{3,2},{4,5},{5,4},{6,7},{7,6},{8,9},{9,8},{10,11... | collective-permute-start | bytes 6291464 | tf_op jit(solution)/shard_map/ppermute | solution.py:130
  11.5 1.6 %copy-done = bf16[1,512,2048]{2,1,0:T(8,128)(2,1)S(1)} copy-done((bf16[1,512,2048]{2,1,0:T(8,128)(2,1)S(1)}, bf16[1,512,2048]{2,1,0:T(8,128)(2,1)}, u32[]{:S(2)}) %copy-start) | copy-done | bytes 2097176
  13.1 1.6 %copy-done.4 = bf16[1,512,2048]{2,1,0:T(8,128)(2,1)S(1)} copy-done((bf16[1,512,2048]{2,1,0:T(8,128)(2,1)S(1)}, bf16[1,512,2048]{2,1,0:T(8,128)(2,1)}, u32[]{:S(2)}) %copy-start.4) | copy-done | bytes 2097176
  15.6 1.4 shard_map.67.refs_0_
  19.2 1.8 %collective-permute-start.4 = (f32[4,2048]{1,0:T(4,128)S(1)}, f32[4,2048]{1,0:T(4,128)S(1)}, u32[]{:S(2)}, u32[]{:S(2)}) collective-permute-start(f32[4,2048]{1,0:T(4,128)S(1)} %shard_map.68.refs_3_.refs_4_.refs_0_), channel_id=1, source_target_pairs={{0,16},{16,0},{1,17},{17,1},{2,18},{18,2},{3,19},{19,3},{4,20},{20... | collective-permute-start | bytes 98312 | tf_op jit(solution)/shard_map/ppermute | solution.py:130
  21.2 1.6 %copy-done.5 = bf16[1,512,2048]{2,1,0:T(8,128)(2,1)S(1)} copy-done((bf16[1,512,2048]{2,1,0:T(8,128)(2,1)S(1)}, bf16[1,512,2048]{2,1,0:T(8,128)(2,1)}, u32[]{:S(2)}) %copy-start.5) | copy-done | bytes 2097176
  22.7 5.0 %shard_map.70 = (s16[4,128,1152]{2,1,0:T(8,128)(2,1)}, f32[8,128]{1,0:T(8,128)S(1)}) custom-call(s32[10]{0:T(128)S(1)} %stack.79.place, bf16[512,2048]{1,0:T(8,128)(2,1)S(1)} %bitcast.38, bf16[512,2048]{1,0:T(8,128)(2,1)} %collective-permute-done.1.refs_1_, bf16[512,2048]{1,0:T(8,128)(2,1)S(1)} %bitcast.32, ...), custom_call_target="tpu_custom_call" | custom-call | tf_op jit(solution)/shard_map/pallas_call | solution.py:217
  27.8 1.4 %collective-permute-start.7 = (s16[4,128,1152]{2,1,0:T(8,128)(2,1)}, s16[4,128,1152]{2,1,0:T(8,128)(2,1)S(1)}, u32[]{:S(2)}, u32[]{:S(2)}) collective-permute-start(s16[4,128,1152]{2,1,0:T(8,128)(2,1)} %shard_map.76), channel_id=1, source_target_pairs={{0,16},{16,0},{1,17},{17,1},{2,18},{18,2},{3,19},{19,3},{4,20},{20... | collective-permute-start | bytes 3538952 | tf_op jit(solution)/shard_map/ppermute | solution.py:130
  29.3 3.1 %collective-permute-done.5.refs_1_ = f32[4,2048]{1,0:T(4,128)S(1)} collective-permute-done((f32[4,2048]{1,0:T(4,128)S(1)}, f32[4,2048]{1,0:T(4,128)S(1)}, u32[]{:S(2)}, u32[]{:S(2)}) %collective-permute-start.5) | collective-permute-done | bytes 32800 | tf_op jit(solution)/shard_map/ppermute | solution.py:130
  32.3 1.1 collective-permute-start.6
  33.5 1.6 %copy-done.6 = bf16[1,512,2048]{2,1,0:T(8,128)(2,1)S(1)} copy-done((bf16[1,512,2048]{2,1,0:T(8,128)(2,1)S(1)}, bf16[1,512,2048]{2,1,0:T(8,128)(2,1)}, u32[]{:S(2)}) %copy-start.6) | copy-done | bytes 2097176
  35.1 4.6 %shard_map.73 = (f32[8,128,1024]{2,1,0:T(8,128)S(1)}, f32[8,128]{1,0:T(8,128)S(1)}) custom-call(s32[10]{0:T(128)S(1)} %stack.77.place, bf16[512,2048]{1,0:T(8,128)(2,1)S(1)} %bitcast.39, bf16[512,2048]{1,0:T(8,128)(2,1)} %collective-permute-done.1.refs_1_, bf16[512,2048]{1,0:T(8,128)(2,1)S(1)} %bitcast.33, ...), custom_call_target="tpu_custom_call" | custom-call | tf_op jit(solution)/shard_map/pallas_call | solution.py:217
  39.7 5.3 %collective-permute-start.8 = (f32[4,2048]{1,0:T(4,128)S(1)}, f32[4,2048]{1,0:T(4,128)S(1)}, u32[]{:S(2)}, u32[]{:S(2)}) collective-permute-start(f32[4,2048]{1,0:T(4,128)S(1)} %shard_map.74.refs_4_.refs_0_), channel_id=1, source_target_pairs={{0,8},{2,10},{4,12},{6,14},{8,0},{10,2},{12,4},{14,6},{1,9},{3,11}... | collective-permute-start | bytes 98312 | tf_op jit(solution)/shard_map/ppermute | solution.py:130
  45.0 4.0 %shard_map.75 = (s16[4,128,1152]{2,1,0:T(8,128)(2,1)S(1)}, f32[8,128]{1,0:T(8,128)S(1)}) custom-call(s32[10]{0:T(128)S(1)} %stack.79.place, bf16[512,2048]{1,0:T(8,128)(2,1)S(1)} %bitcast.40, bf16[512,2048]{1,0:T(8,128)(2,1)} %collective-permute-done.1.refs_1_, bf16[512,2048]{1,0:T(8,128)(2,1)S(1)} %bitcast.34, ...), custom_call_target="tpu_custom_call" | custom-call | tf_op jit(solution)/shard_map/pallas_call | solution.py:217
  49.0 5.3 %collective-permute-start.9 = (f32[2,2048]{1,0:T(2,128)S(1)}, f32[2,2048]{1,0:T(2,128)S(1)}, u32[]{:S(2)}, u32[]{:S(2)}) collective-permute-start(f32[2,2048]{1,0:T(2,128)S(1)} %get-tuple-element.41.refs_2_), channel_id=1, source_target_pairs={{0,240},{16,224},{32,0},{48,16},{64,32},{80,48},{96,64},{112,80},{... | collective-permute-start | bytes 49160 | tf_op jit(solution)/shard_map/ppermute | solution.py:152
  55.2 5.0 %collective-permute-done.10.refs_3_.refs_4_ = f32[2,2048]{1,0:T(2,128)S(1)} collective-permute-done((f32[2,2048]{1,0:T(2,128)S(1)}, f32[2,2048]{1,0:T(2,128)S(1)}, u32[]{:S(2)}, u32[]{:S(2)}) %collective-permute-start.10) | collective-permute-done | bytes 16416 | tf_op jit(solution)/shard_map/ppermute | solution.py:152
  61.2 2.1 %collective-permute-start.12 = (s16[128,1152]{1,0:T(8,128)(2,1)S(1)}, s16[128,1152]{1,0:T(8,128)(2,1)S(1)}, u32[]{:S(2)}, u32[]{:S(2)}) collective-permute-start(s16[128,1152]{1,0:T(8,128)(2,1)S(1)} %get-tuple-element.44), channel_id=1, source_target_pairs={{0,14},{2,0},{4,2},{6,4},{8,6},{10,8},{12,10},{14,12},{1,15},{3,1}... | collective-permute-start | bytes 884744 | tf_op jit(solution)/shard_map/ppermute | solution.py:282
  63.4 2.1 %shard_map.80 = (f32[4,2048]{1,0:T(4,128)S(1)}, f32[8,64]{1,0:T(8,128)S(1)}) custom-call(s32[1]{0:T(128)} %bitcast.6.refs_0_, f32[2,2048]{1,0:T(2,128)S(1)} %get-tuple-element.42.refs_1_, f32[2,2048]{1,0:T(2,128)S(1)} %get-tuple-element.41.refs_2_, f32[2,2048]{1,0:T(2,128)S(1)} %collective-permute-done.9.refs_2_.refs_3_, ...), custom_call_target="tpu_custom_call" | custom-call | tf_op jit(solution)/shard_map/pallas_call | solution.py:70
  65.5 4.9 %collective-permute-start.14 = (f32[4,2048]{1,0:T(4,128)S(1)}, f32[4,2048]{1,0:T(4,128)S(1)}, u32[]{:S(2)}, u32[]{:S(2)}) collective-permute-start(f32[4,2048]{1,0:T(4,128)S(1)} %get-tuple-element.46.refs_0_), channel_id=1, source_target_pairs={{0,1},{1,0},{2,3},{3,2},{4,5},{5,4},{6,7},{7,6},{8,9},{9,8},{10,11... | collective-permute-start | bytes 98312 | tf_op jit(solution)/shard_map/ppermute | solution.py:130
  71.2 5.4 %collective-permute-done.15.refs_1_ = f32[4,2048]{1,0:T(4,128)S(1)} collective-permute-done((f32[4,2048]{1,0:T(4,128)S(1)}, f32[4,2048]{1,0:T(4,128)S(1)}, u32[]{:S(2)}, u32[]{:S(2)}) %collective-permute-start.15) | collective-permute-done | bytes 32800 | tf_op jit(solution)/shard_map/ppermute | solution.py:130
  76.7 1.5 %collective-permute-done.13.refs_3_ = s16[128,1152]{1,0:T(8,128)(2,1)S(1)} collective-permute-done((s16[128,1152]{1,0:T(8,128)(2,1)S(1)}, s16[128,1152]{1,0:T(8,128)(2,1)S(1)}, u32[]{:S(2)}, u32[]{:S(2)}) %collective-permute-start.13) | collective-permute-done | bytes 294944 | tf_op jit(solution)/shard_map/ppermute | solution.py:282
  80.4 7.8 %collective-permute-done.18.refs_1_ = f32[4,2048]{1,0:T(4,128)S(1)} collective-permute-done((f32[4,2048]{1,0:T(4,128)S(1)}, f32[4,2048]{1,0:T(4,128)S(1)}, u32[]{:S(2)}, u32[]{:S(2)}) %collective-permute-start.18) | collective-permute-done | bytes 32800 | tf_op jit(solution)/shard_map/ppermute | solution.py:130
  90.2 5.6 %collective-permute-start.19 = (bf16[16,64,2048]{2,1,0:T(8,128)(2,1)}, bf16[16,64,2048]{2,1,0:T(8,128)(2,1)}, u32[]{:S(2)}, u32[]{:S(2)}) collective-permute-start(bf16[16,64,2048]{2,1,0:T(8,128)(2,1)} %shard_map.86.weights), channel_id=1, source_target_pairs={{0,1},{1,0},{2,3},{3,2},{4,5},{5,4},{6,7},{7,6},{8,9},{9,8},{10,11... | collective-permute-start | bytes 12582920 | tf_op jit(solution)/shard_map/ppermute | solution.py:130
  97.3 2.3 %collective-permute-start.22 = (f32[4,2048]{1,0:T(4,128)S(1)}, f32[4,2048]{1,0:T(4,128)S(1)}, u32[]{:S(2)}, u32[]{:S(2)}) collective-permute-start(f32[4,2048]{1,0:T(4,128)S(1)} %shard_map.84.refs_4_.refs_0_), channel_id=1, source_target_pairs={{0,8},{2,10},{4,12},{6,14},{8,0},{10,2},{12,4},{14,6},{1,9},{3,11}... | collective-permute-start | bytes 98312 | tf_op jit(solution)/shard_map/ppermute | solution.py:130
  100.1 2.8 %collective-permute-done.19.other_weights = bf16[16,64,2048]{2,1,0:T(8,128)(2,1)} collective-permute-done((bf16[16,64,2048]{2,1,0:T(8,128)(2,1)}, bf16[16,64,2048]{2,1,0:T(8,128)(2,1)}, u32[]{:S(2)}, u32[]{:S(2)}) %collective-permute-start.19) | collective-permute-done | bytes 4194336 | tf_op jit(solution)/shard_map/ppermute | solution.py:130
  102.9 8.1 %shard_map.87 = (bf16[512,2048]{1,0:T(8,128)(2,1)}, f32[8,128]{1,0:T(8,128)}) custom-call(s32[3]{0:T(128)} %pad_add_fusion.2.at, bf16[512,2048]{1,0:T(8,128)(2,1)} %bitcast.29, bf16[16,64,2048]{2,1,0:T(8,128)(2,1)} %shard_map.86.weights, bf16[16,64,2048]{2,1,0:T(8,128)(2,1)} %collective-permute-done.19.other_weights, f32[8,128]{1,0:T(8,128)} %copy-done.11), custom_call_target="tpu_custom_call" | custom-call | tf_op jit(solution)/shard_map/pallas_call | solution.py:326
  111.8 1.8 %collective-permute-start.23 = (f32[4,2048]{1,0:T(4,128)S(1)}, f32[4,2048]{1,0:T(4,128)S(1)}, u32[]{:S(2)}, u32[]{:S(2)}) collective-permute-start(f32[4,2048]{1,0:T(4,128)S(1)} %shard_map.88.refs_0_), channel_id=1, source_target_pairs={{0,16},{16,0},{1,17},{17,1},{2,18},{18,2},{3,19},{19,3},{4,20},{20... | collective-permute-start | bytes 98312 | tf_op jit(solution)/shard_map/ppermute | solution.py:130
  113.5 1.3 collective-permute-done.23.refs_1_
  117.8 4.0 %collective-permute-start.25 = (f32[2,2048]{1,0:T(2,128)S(1)}, f32[2,2048]{1,0:T(2,128)S(1)}, u32[]{:S(2)}, u32[]{:S(2)}) collective-permute-start(f32[2,2048]{1,0:T(2,128)S(1)} %get-tuple-element.61.refs_6_), channel_id=1, source_target_pairs={{0,240},{16,224},{32,0},{48,16},{64,32},{80,48},{96,64},{112,80},{... | collective-permute-start | bytes 49160 | tf_op jit(solution)/shard_map/ppermute | solution.py:152
  122.5 7.6 %shard_map.91 = (bf16[512,2048]{1,0:T(8,128)(2,1)}, f32[8,128]{1,0:T(8,128)}) custom-call(s32[3]{0:T(128)} %pad_add_fusion.at, bf16[512,2048]{1,0:T(8,128)(2,1)} %bitcast.30, bf16[16,64,2048]{2,1,0:T(8,128)(2,1)} %shard_map.86.weights, bf16[16,64,2048]{2,1,0:T(8,128)(2,1)} %collective-permute-done.19.other_weights, ...), custom_call_target="tpu_custom_call", output_to_operand_aliasing={{0}: (4, {})} | custom-call | tf_op jit(solution)/shard_map/pallas_call | solution.py:326
  131.4 2.1 %collective-permute-start.27 = (f32[64,1024]{1,0:T(8,128)S(1)}, f32[64,1024]{1,0:T(8,128)S(1)}, u32[]{:S(2)}, u32[]{:S(2)}) collective-permute-start(f32[64,1024]{1,0:T(8,128)S(1)} %get-tuple-element.63), channel_id=1, source_target_pairs={{0,1},{1,0},{2,3},{3,2},{4,5},{5,4},{6,7},{7,6},{8,9},{9,8},{10,11... | collective-permute-start | bytes 786440 | tf_op jit(solution)/shard_map/ppermute | solution.py:130
  135.4 1.1 shard_map.93
  (95 shorter events, 20.7 us)
Async XLA Ops:
  7.2 82.3 %all-gather.2.cloned.1.call-start = ((), (), s32[]{:S(2)}) async-start(), calls=%async_computation | async-start | bytes 4718592 | tf_op jit(solution)/shard_map/all_gather | solution.py:401
  7.2 12.0 %collective-permute-start.1 = (bf16[512,2048]{1,0:T(8,128)(2,1)}, bf16[512,2048]{1,0:T(8,128)(2,1)}, u32[]{:S(2)}, u32[]{:S(2)}) collective-permute-start(bf16[512,2048]{1,0:T(8,128)(2,1)} %bitcast.36), channel_id=1, source_target_pairs={{0,1},{1,0},{2,3},{3,2},{4,5},{5,4},{6,7},{7,6},{8,9},{9,8},{10,11... | collective-permute-start | bytes 6291464 | tf_op jit(solution)/shard_map/ppermute | solution.py:130
  10.5 8.6 %collective-permute-start.2 = (bf16[512,2048]{1,0:T(8,128)(2,1)}, bf16[512,2048]{1,0:T(8,128)(2,1)}, u32[]{:S(2)}, u32[]{:S(2)}) collective-permute-start(bf16[512,2048]{1,0:T(8,128)(2,1)} %bitcast.28), channel_id=1, source_target_pairs={{0,1},{1,0},{2,3},{3,2},{4,5},{5,4},{6,7},{7,6},{8,9},{9,8},{10,11... | collective-permute-start | bytes 6291464 | tf_op jit(solution)/shard_map/ppermute | solution.py:130
  10.6 7.7 %collective-permute-start = (bf16[64,2048]{1,0:T(8,128)(2,1)}, bf16[64,2048]{1,0:T(8,128)(2,1)S(1)}, u32[]{:S(2)}, u32[]{:S(2)}) collective-permute-start(bf16[64,2048]{1,0:T(8,128)(2,1)} %bitcast.42), channel_id=1, source_target_pairs={{0,16},{16,0},{1,17},{17,1},{2,18},{18,2},{3,19},{19,3},{4,20},{20... | collective-permute-start | bytes 786440 | tf_op jit(solution)/shard_map/ppermute | solution.py:130
  17.0 1.4 collective-permute-start.3
  19.2 8.6 %collective-permute-start.4 = (f32[4,2048]{1,0:T(4,128)S(1)}, f32[4,2048]{1,0:T(4,128)S(1)}, u32[]{:S(2)}, u32[]{:S(2)}) collective-permute-start(f32[4,2048]{1,0:T(4,128)S(1)} %shard_map.68.refs_3_.refs_4_.refs_0_), channel_id=1, source_target_pairs={{0,16},{16,0},{1,17},{17,1},{2,18},{18,2},{3,19},{19,3},{4,20},{20... | collective-permute-start | bytes 98312 | tf_op jit(solution)/shard_map/ppermute | solution.py:130
  27.8 32.4 %collective-permute-start.7 = (s16[4,128,1152]{2,1,0:T(8,128)(2,1)}, s16[4,128,1152]{2,1,0:T(8,128)(2,1)S(1)}, u32[]{:S(2)}, u32[]{:S(2)}) collective-permute-start(s16[4,128,1152]{2,1,0:T(8,128)(2,1)} %shard_map.76), channel_id=1, source_target_pairs={{0,16},{16,0},{1,17},{17,1},{2,18},{18,2},{3,19},{19,3},{4,20},{20... | collective-permute-start | bytes 3538952 | tf_op jit(solution)/shard_map/ppermute | solution.py:130
  29.3 3.1 %collective-permute-start.5 = (f32[4,2048]{1,0:T(4,128)S(1)}, f32[4,2048]{1,0:T(4,128)S(1)}, u32[]{:S(2)}, u32[]{:S(2)}) collective-permute-start(f32[4,2048]{1,0:T(4,128)S(1)} %shard_map.71.refs_0_.refs_1_), channel_id=1, source_target_pairs={{0,2},{2,0},{4,6},{6,4},{8,10},{10,8},{12,14},{14,12},{1,3},{3,1},... | collective-permute-start | bytes 98312 | tf_op jit(solution)/shard_map/ppermute | solution.py:130
  32.3 7.4 %collective-permute-start.6 = (f32[4,2048]{1,0:T(4,128)S(1)}, f32[4,2048]{1,0:T(4,128)S(1)}, u32[]{:S(2)}, u32[]{:S(2)}) collective-permute-start(f32[4,2048]{1,0:T(4,128)S(1)} %shard_map.72.refs_4_.refs_0_), channel_id=1, source_target_pairs={{0,4},{2,6},{4,0},{6,2},{8,12},{10,14},{12,8},{14,10},{1,5},{3,7},... | collective-permute-start | bytes 98312 | tf_op jit(solution)/shard_map/ppermute | solution.py:130
  39.7 48.5 %copy-start.2 = (f32[8,128,1024]{2,1,0:T(8,128)}, f32[8,128,1024]{2,1,0:T(8,128)S(1)}, u32[]{:S(2)}) copy-start(f32[8,128,1024]{2,1,0:T(8,128)S(1)} %get-tuple-element.36.refs_0_) | copy-start | bytes 12582916
  39.7 9.3 %collective-permute-start.8 = (f32[4,2048]{1,0:T(4,128)S(1)}, f32[4,2048]{1,0:T(4,128)S(1)}, u32[]{:S(2)}, u32[]{:S(2)}) collective-permute-start(f32[4,2048]{1,0:T(4,128)S(1)} %shard_map.74.refs_4_.refs_0_), channel_id=1, source_target_pairs={{0,8},{2,10},{4,12},{6,14},{8,0},{10,2},{12,4},{14,6},{1,9},{3,11}... | collective-permute-start | bytes 98312 | tf_op jit(solution)/shard_map/ppermute | solution.py:130
  49.0 6.1 %collective-permute-start.9 = (f32[2,2048]{1,0:T(2,128)S(1)}, f32[2,2048]{1,0:T(2,128)S(1)}, u32[]{:S(2)}, u32[]{:S(2)}) collective-permute-start(f32[2,2048]{1,0:T(2,128)S(1)} %get-tuple-element.41.refs_2_), channel_id=1, source_target_pairs={{0,240},{16,224},{32,0},{48,16},{64,32},{80,48},{96,64},{112,80},{... | collective-permute-start | bytes 49160 | tf_op jit(solution)/shard_map/ppermute | solution.py:152
  54.3 5.9 %collective-permute-start.10 = (f32[2,2048]{1,0:T(2,128)S(1)}, f32[2,2048]{1,0:T(2,128)S(1)}, u32[]{:S(2)}, u32[]{:S(2)}) collective-permute-start(f32[2,2048]{1,0:T(2,128)S(1)} %get-tuple-element.42.refs_1_), channel_id=1, source_target_pairs={{0,32},{16,48},{32,64},{48,80},{64,96},{80,112},{96,144},{112,128}... | collective-permute-start | bytes 49160 | tf_op jit(solution)/shard_map/ppermute | solution.py:152
  61.2 27.0 %collective-permute-start.11 = (s16[4,128,1152]{2,1,0:T(8,128)(2,1)S(1)}, s16[4,128,1152]{2,1,0:T(8,128)(2,1)S(1)}, u32[]{:S(2)}, u32[]{:S(2)}) collective-permute-start(s16[4,128,1152]{2,1,0:T(8,128)(2,1)S(1)} %shard_map.79), channel_id=1, source_target_pairs={{0,16},{16,0},{1,17},{17,1},{2,18},{18,2},{3,19},{19,3},{4,20},{20... | collective-permute-start | bytes 3538952 | tf_op jit(solution)/shard_map/ppermute | solution.py:130
  61.2 15.5 %collective-permute-start.12 = (s16[128,1152]{1,0:T(8,128)(2,1)S(1)}, s16[128,1152]{1,0:T(8,128)(2,1)S(1)}, u32[]{:S(2)}, u32[]{:S(2)}) collective-permute-start(s16[128,1152]{1,0:T(8,128)(2,1)S(1)} %get-tuple-element.44), channel_id=1, source_target_pairs={{0,14},{2,0},{4,2},{6,4},{8,6},{10,8},{12,10},{14,12},{1,15},{3,1}... | collective-permute-start | bytes 884744 | tf_op jit(solution)/shard_map/ppermute | solution.py:282
  63.4 14.9 %copy-start.8 = (s16[4,128,1152]{2,1,0:T(8,128)(2,1)S(1)}, s16[4,128,1152]{2,1,0:T(8,128)(2,1)}, u32[]{:S(2)}) copy-start(s16[4,128,1152]{2,1,0:T(8,128)(2,1)} %copy-done.7) | copy-start | bytes 3538948
  63.4 14.9 %collective-permute-start.13 = (s16[128,1152]{1,0:T(8,128)(2,1)S(1)}, s16[128,1152]{1,0:T(8,128)(2,1)S(1)}, u32[]{:S(2)}, u32[]{:S(2)}) collective-permute-start(s16[128,1152]{1,0:T(8,128)(2,1)S(1)} %get-tuple-element.45), channel_id=1, source_target_pairs={{0,2},{2,4},{4,6},{6,8},{8,10},{10,12},{12,14},{14,0},{1,3},{3,5},... | collective-permute-start | bytes 884744 | tf_op jit(solution)/shard_map/ppermute | solution.py:282
  65.5 5.7 %collective-permute-start.14 = (f32[4,2048]{1,0:T(4,128)S(1)}, f32[4,2048]{1,0:T(4,128)S(1)}, u32[]{:S(2)}, u32[]{:S(2)}) collective-permute-start(f32[4,2048]{1,0:T(4,128)S(1)} %get-tuple-element.46.refs_0_), channel_id=1, source_target_pairs={{0,1},{1,0},{2,3},{3,2},{4,5},{5,4},{6,7},{7,6},{8,9},{9,8},{10,11... | collective-permute-start | bytes 98312 | tf_op jit(solution)/shard_map/ppermute | solution.py:130
  71.2 5.4 %collective-permute-start.15 = (f32[4,2048]{1,0:T(4,128)S(1)}, f32[4,2048]{1,0:T(4,128)S(1)}, u32[]{:S(2)}, u32[]{:S(2)}) collective-permute-start(f32[4,2048]{1,0:T(4,128)S(1)} %shard_map.81.refs_0_), channel_id=1, source_target_pairs={{0,2},{2,0},{4,6},{6,4},{8,10},{10,8},{12,14},{14,12},{1,3},{3,1},... | collective-permute-start | bytes 98312 | tf_op jit(solution)/shard_map/ppermute | solution.py:130
  78.9 9.3 %collective-permute-start.16 = (s16[128,1152]{1,0:T(8,128)(2,1)S(1)}, s16[128,1152]{1,0:T(8,128)(2,1)S(1)}, u32[]{:S(2)}, u32[]{:S(2)}) collective-permute-start(s16[128,1152]{1,0:T(8,128)(2,1)S(1)} %get-tuple-element.47), channel_id=1, source_target_pairs={{0,14},{2,0},{4,2},{6,4},{8,6},{10,8},{12,10},{14,12},{1,15},{3,1}... | collective-permute-start | bytes 884744 | tf_op jit(solution)/shard_map/ppermute | solution.py:282
  79.8 8.4 %collective-permute-start.17 = (s16[128,1152]{1,0:T(8,128)(2,1)S(1)}, s16[128,1152]{1,0:T(8,128)(2,1)S(1)}, u32[]{:S(2)}, u32[]{:S(2)}) collective-permute-start(s16[128,1152]{1,0:T(8,128)(2,1)S(1)} %get-tuple-element.48), channel_id=1, source_target_pairs={{0,2},{2,4},{4,6},{6,8},{8,10},{10,12},{12,14},{14,0},{1,3},{3,5},... | collective-permute-start | bytes 884744 | tf_op jit(solution)/shard_map/ppermute | solution.py:282
  80.4 7.8 %collective-permute-start.18 = (f32[4,2048]{1,0:T(4,128)S(1)}, f32[4,2048]{1,0:T(4,128)S(1)}, u32[]{:S(2)}, u32[]{:S(2)}) collective-permute-start(f32[4,2048]{1,0:T(4,128)S(1)} %shard_map.82.refs_4_.refs_0_), channel_id=1, source_target_pairs={{0,4},{2,6},{4,0},{6,2},{8,12},{10,14},{12,8},{14,10},{1,5},{3,7},... | collective-permute-start | bytes 98312 | tf_op jit(solution)/shard_map/ppermute | solution.py:130
  90.2 12.8 %collective-permute-start.19 = (bf16[16,64,2048]{2,1,0:T(8,128)(2,1)}, bf16[16,64,2048]{2,1,0:T(8,128)(2,1)}, u32[]{:S(2)}, u32[]{:S(2)}) collective-permute-start(bf16[16,64,2048]{2,1,0:T(8,128)(2,1)} %shard_map.86.weights), channel_id=1, source_target_pairs={{0,1},{1,0},{2,3},{3,2},{4,5},{5,4},{6,7},{7,6},{8,9},{9,8},{10,11... | collective-permute-start | bytes 12582920 | tf_op jit(solution)/shard_map/ppermute | solution.py:130
  95.8 19.0 %collective-permute-start.20 = (s16[128,1152]{1,0:T(8,128)(2,1)S(1)}, s16[128,1152]{1,0:T(8,128)(2,1)S(1)}, u32[]{:S(2)}, u32[]{:S(2)}) collective-permute-start(s16[128,1152]{1,0:T(8,128)(2,1)S(1)} %get-tuple-element.52), channel_id=1, source_target_pairs={{0,14},{2,0},{4,2},{6,4},{8,6},{10,8},{12,10},{14,12},{1,15},{3,1}... | collective-permute-start | bytes 884744 | tf_op jit(solution)/shard_map/ppermute | solution.py:282
  96.7 18.1 %collective-permute-start.21 = (s16[128,1152]{1,0:T(8,128)(2,1)S(1)}, s16[128,1152]{1,0:T(8,128)(2,1)S(1)}, u32[]{:S(2)}, u32[]{:S(2)}) collective-permute-start(s16[128,1152]{1,0:T(8,128)(2,1)S(1)} %get-tuple-element.53), channel_id=1, source_target_pairs={{0,2},{2,4},{4,6},{6,8},{8,10},{10,12},{12,14},{14,0},{1,3},{3,5},... | collective-permute-start | bytes 884744 | tf_op jit(solution)/shard_map/ppermute | solution.py:282
  97.3 13.8 %collective-permute-start.22 = (f32[4,2048]{1,0:T(4,128)S(1)}, f32[4,2048]{1,0:T(4,128)S(1)}, u32[]{:S(2)}, u32[]{:S(2)}) collective-permute-start(f32[4,2048]{1,0:T(4,128)S(1)} %shard_map.84.refs_4_.refs_0_), channel_id=1, source_target_pairs={{0,8},{2,10},{4,12},{6,14},{8,0},{10,2},{12,4},{14,6},{1,9},{3,11}... | collective-permute-start | bytes 98312 | tf_op jit(solution)/shard_map/ppermute | solution.py:130
  102.9 11.9 %copy-start.3 = (f32[8,128,1024]{2,1,0:T(8,128)S(1)}, f32[8,128,1024]{2,1,0:T(8,128)}, u32[]{:S(2)}) copy-start(f32[8,128,1024]{2,1,0:T(8,128)} %copy-done.2) | copy-start | bytes 12582916
  111.8 3.1 %collective-permute-start.23 = (f32[4,2048]{1,0:T(4,128)S(1)}, f32[4,2048]{1,0:T(4,128)S(1)}, u32[]{:S(2)}, u32[]{:S(2)}) collective-permute-start(f32[4,2048]{1,0:T(4,128)S(1)} %shard_map.88.refs_0_), channel_id=1, source_target_pairs={{0,16},{16,0},{1,17},{17,1},{2,18},{18,2},{3,19},{19,3},{4,20},{20... | collective-permute-start | bytes 98312 | tf_op jit(solution)/shard_map/ppermute | solution.py:130
  116.0 14.1 %collective-permute-start.24 = (s16[128,1152]{1,0:T(8,128)(2,1)S(1)}, s16[128,1152]{1,0:T(8,128)(2,1)S(1)}, u32[]{:S(2)}, u32[]{:S(2)}) collective-permute-start(s16[128,1152]{1,0:T(8,128)(2,1)S(1)} %get-tuple-element.59), channel_id=1, source_target_pairs={{0,14},{2,0},{4,2},{6,4},{8,6},{10,8},{12,10},{14,12},{1,15},{3,1}... | collective-permute-start | bytes 884744 | tf_op jit(solution)/shard_map/ppermute | solution.py:282
  117.0 13.0 %collective-permute-start.26 = (f32[2,2048]{1,0:T(2,128)S(1)}, f32[2,2048]{1,0:T(2,128)S(1)}, u32[]{:S(2)}, u32[]{:S(2)}) collective-permute-start(f32[2,2048]{1,0:T(2,128)S(1)} %get-tuple-element.55.refs_4_.refs_5_), channel_id=1, source_target_pairs={{0,32},{16,48},{32,64},{48,80},{64,96},{80,112},{96,144},{112,128}... | collective-permute-start | bytes 49160 | tf_op jit(solution)/shard_map/ppermute | solution.py:152
  117.8 12.3 %collective-permute-start.25 = (f32[2,2048]{1,0:T(2,128)S(1)}, f32[2,2048]{1,0:T(2,128)S(1)}, u32[]{:S(2)}, u32[]{:S(2)}) collective-permute-start(f32[2,2048]{1,0:T(2,128)S(1)} %get-tuple-element.61.refs_6_), channel_id=1, source_target_pairs={{0,240},{16,224},{32,0},{48,16},{64,32},{80,48},{96,64},{112,80},{... | collective-permute-start | bytes 49160 | tf_op jit(solution)/shard_map/ppermute | solution.py:152
  131.4 3.3 %collective-permute-start.27 = (f32[64,1024]{1,0:T(8,128)S(1)}, f32[64,1024]{1,0:T(8,128)S(1)}, u32[]{:S(2)}, u32[]{:S(2)}) collective-permute-start(f32[64,1024]{1,0:T(8,128)S(1)} %get-tuple-element.63), channel_id=1, source_target_pairs={{0,1},{1,0},{2,3},{3,2},{4,5},{5,4},{6,7},{7,6},{8,9},{9,8},{10,11... | collective-permute-start | bytes 786440 | tf_op jit(solution)/shard_map/ppermute | solution.py:130
  (13 other events, 15.7 us)
Sparse Core Ops, SparseCore 0:
  19.3 64.9 all-gather.1

commit v2 on v1

--- a/solution.py
+++ b/solution.py
@@ -420,25 +420,24 @@
     )
     right, left = shard_sum(value, STEPS_ALONG[4:], {"z4": (mark,)}, "z4")
     arrived = neighbours(right, left)
-    received, sent = hops(0, (), arrived, first)
-    second = partner(held(second, sent), "xl", 1)
+    second = partner(held(second, arrived), "xl", 1)
     back, basis = kernel_call(
         basis_kernel,
         (right, left, *arrived, acts, cotan, weight_bf),
         (f32(4, width), f32(8, rows)),
         at,
-        sent,
     )
     value = shard_sum(back, STEPS_BACK[:2], {})
+    received, sent = hops(0, (), (value,), first)
+    value = shard_sum(value, STEPS_BACK[2:4], {"z2": sent})
     received, sent = hops(1, received, (value,), first)
-    value = shard_sum(value, STEPS_BACK[2:3], {"z2": sent})
-    received, sent = hops(2, received, (value,), second)
+    right, left = shard_sum(value, STEPS_BACK[4:], {"xl1": sent}, "xl1")
+    arrived = neighbours(right, left)
+    received, sent = hops(2, received, arrived, second)
     weights = held(weights, sent, (), NO_ROOM)
     both = (cotan, weights, partner(weights, "core", 1))
     half, mark = backward_input(core, x, 0, *both, sent)
-    right, left = shard_sum(value, STEPS_BACK[3:], {"z4": (mark,)}, "xl1")
-    received, sent = hops(3, received, (right,), second)
-    arrived = neighbours(right, left)
+    received, sent = hops(3, received, (mark,), second)
     grad_in, mark = backward_input(core, x, 2, *both, sent, (half,))
     kept, given, _ = kernel_call(
         total_kernel,

time: 144 us -> 157 us (1.090)
  waiting for transfers between devices: 30.7 us -> 38.8 us
  starting transfers between devices: 46.6 us -> 50.5 us
  Pallas kernels: 37.6 us -> 39.8 us
    ppermute x4, waiting for transfers between devices: 5.91 us -> 11.8 us  [passed_along(): return lax.ppermute(value, CYCLE + ('xl',), pairs)]
    ppermute x7, starting transfers between devices: 6.24 us -> 11.2 us  [shifted(): lax.ppermute(value, axis, [(i, (i + steps) % count) for i in range(count)])]
    ppermute x17, waiting for transfers between devices: 23.2 us -> 26.9 us  [partner(): return lax.ppermute(value, axis, [(i, i ^ step) for i in range(count)])]
    pallas_call x4, Pallas kernels: 2.24 us -> 4.38 us  [hop(): pl.pallas_call(functools.partial(hop_kernel, step, len(after)), grid=(1,)...]
    ppermute x17, starting transfers between devices: 30.2 us -> 28.6 us  [partner(): return lax.ppermute(value, axis, [(i, i ^ step) for i in range(count)])]
    unnamed x32 -> x28, local copies, waits for them, and re-layouts: 11.1 us -> 9.97 us
  transfers between devices with their start and end apart: 29 -> 29, of which waited for: 11 -> 13; matrix products, arithmetic and copies ran while one was open for 2% -> 2% of each run, Pallas kernels for 24% -> 24%
where the time goes in v2:
time: 157 us; the launch traced here: 156 us
  starting transfers between devices  50.5 us (32%)
  Pallas kernels  39.8 us (25%)
  waiting for transfers between devices  38.8 us (25%)
  between operations  14.3 us (9%)
  local copies, waits for them, and re-layouts  10.2 us (6%)
  other arithmetic  2.77 us (2%)
    ppermute x17, starting transfers between devices, partner(): return lax.ppermute(value, axis, [(i, i ^ step) for i in range(count)])  28.6 us
    ppermute x17, waiting for transfers between devices, partner(): return lax.ppermute(value, axis, [(i, i ^ step) for i in range(count)])  26.9 us
    pallas_call x2, Pallas kernels, backward_input(): pl.pallas_call(input_kernel, grid_spec=pltpu.PrefetchScalarGridSpec(num_s...  15.8 us
    pallas_call x3, Pallas kernels, chunks(): pl.pallas_call(body, grid_spec=pltpu.PrefetchScalarGridSpec(num_scalar_pr...  13.6 us
    ppermute x4, waiting for transfers between devices, passed_along(): return lax.ppermute(value, CYCLE + ('xl',), pairs)  11.8 us
    ppermute x7, starting transfers between devices, shifted(): lax.ppermute(value, axis, [(i, (i + steps) % count) for i in range(count)])  11.2 us
    ppermute x4, starting transfers between devices, passed_along(): return lax.ppermute(value, CYCLE + ('xl',), pairs)  10.7 us
    unnamed x28, local copies, waits for them, and re-layouts  9.97 us
  transfers between devices with their start and end apart: 29, of which 13 were waited for; matrix products, arithmetic and copies ran while one was open for 2% of the time, Pallas kernels for 24%

profile of v2, /device:TPU:1, one launch (start us, length us, event | category | flops | bytes accessed | tf_op | source)
XLA Modules:
  0.0 156.3 jit_solution(10562038931728558567)
XLA Ops:
  7.2 3.3 %collective-permute-start.1 = (bf16[512,2048]{1,0:T(8,128)(2,1)}, bf16[512,2048]{1,0:T(8,128)(2,1)}, u32[]{:S(2)}, u32[]{:S(2)}) collective-permute-start(bf16[512,2048]{1,0:T(8,128)(2,1)} %bitcast.36), channel_id=1, source_target_pairs={{0,1},{1,0},{2,3},{3,2},{4,5},{5,4},{6,7},{7,6},{8,9},{9,8},{10,11... | collective-permute-start | bytes 6291464 | tf_op jit(solution)/shard_map/ppermute | solution.py:130
  11.5 1.6 %copy-done = bf16[1,512,2048]{2,1,0:T(8,128)(2,1)S(1)} copy-done((bf16[1,512,2048]{2,1,0:T(8,128)(2,1)S(1)}, bf16[1,512,2048]{2,1,0:T(8,128)(2,1)}, u32[]{:S(2)}) %copy-start) | copy-done | bytes 2097176
  13.1 1.6 %copy-done.4 = bf16[1,512,2048]{2,1,0:T(8,128)(2,1)S(1)} copy-done((bf16[1,512,2048]{2,1,0:T(8,128)(2,1)S(1)}, bf16[1,512,2048]{2,1,0:T(8,128)(2,1)}, u32[]{:S(2)}) %copy-start.4) | copy-done | bytes 2097176
  19.2 1.8 %collective-permute-start.4 = (f32[4,2048]{1,0:T(4,128)S(1)}, f32[4,2048]{1,0:T(4,128)S(1)}, u32[]{:S(2)}, u32[]{:S(2)}) collective-permute-start(f32[4,2048]{1,0:T(4,128)S(1)} %shard_map.68.refs_3_.refs_4_.refs_0_), channel_id=1, source_target_pairs={{0,16},{16,0},{1,17},{17,1},{2,18},{18,2},{3,19},{19,3},{4,20},{20... | collective-permute-start | bytes 98312 | tf_op jit(solution)/shard_map/ppermute | solution.py:130
  21.2 1.6 %copy-done.5 = bf16[1,512,2048]{2,1,0:T(8,128)(2,1)S(1)} copy-done((bf16[1,512,2048]{2,1,0:T(8,128)(2,1)S(1)}, bf16[1,512,2048]{2,1,0:T(8,128)(2,1)}, u32[]{:S(2)}) %copy-start.5) | copy-done | bytes 2097176
  22.7 5.0 %shard_map.70 = (s16[4,128,1152]{2,1,0:T(8,128)(2,1)}, f32[8,128]{1,0:T(8,128)S(1)}) custom-call(s32[10]{0:T(128)S(1)} %stack.79.place, bf16[512,2048]{1,0:T(8,128)(2,1)S(1)} %bitcast.38, bf16[512,2048]{1,0:T(8,128)(2,1)} %collective-permute-done.1.refs_1_, bf16[512,2048]{1,0:T(8,128)(2,1)S(1)} %bitcast.32, ...), custom_call_target="tpu_custom_call" | custom-call | tf_op jit(solution)/shard_map/pallas_call | solution.py:217
  29.3 3.2 %collective-permute-done.5.refs_1_ = f32[4,2048]{1,0:T(4,128)S(1)} collective-permute-done((f32[4,2048]{1,0:T(4,128)S(1)}, f32[4,2048]{1,0:T(4,128)S(1)}, u32[]{:S(2)}, u32[]{:S(2)}) %collective-permute-start.5) | collective-permute-done | bytes 32800 | tf_op jit(solution)/shard_map/ppermute | solution.py:130
  33.5 1.6 %copy-done.6 = bf16[1,512,2048]{2,1,0:T(8,128)(2,1)S(1)} copy-done((bf16[1,512,2048]{2,1,0:T(8,128)(2,1)S(1)}, bf16[1,512,2048]{2,1,0:T(8,128)(2,1)}, u32[]{:S(2)}) %copy-start.6) | copy-done | bytes 2097176
  35.1 4.6 %shard_map.73 = (f32[8,128,1024]{2,1,0:T(8,128)S(1)}, f32[8,128]{1,0:T(8,128)S(1)}) custom-call(s32[10]{0:T(128)S(1)} %stack.77.place, bf16[512,2048]{1,0:T(8,128)(2,1)S(1)} %bitcast.39, bf16[512,2048]{1,0:T(8,128)(2,1)} %collective-permute-done.1.refs_1_, bf16[512,2048]{1,0:T(8,128)(2,1)S(1)} %bitcast.33, ...), custom_call_target="tpu_custom_call" | custom-call | tf_op jit(solution)/shard_map/pallas_call | solution.py:217
  39.7 5.3 %collective-permute-start.7 = (f32[4,2048]{1,0:T(4,128)S(1)}, f32[4,2048]{1,0:T(4,128)S(1)}, u32[]{:S(2)}, u32[]{:S(2)}) collective-permute-start(f32[4,2048]{1,0:T(4,128)S(1)} %shard_map.74.refs_4_.refs_0_), channel_id=1, source_target_pairs={{0,8},{2,10},{4,12},{6,14},{8,0},{10,2},{12,4},{14,6},{1,9},{3,11}... | collective-permute-start | bytes 98312 | tf_op jit(solution)/shard_map/ppermute | solution.py:130
  45.0 4.0 %shard_map.75 = (s16[4,128,1152]{2,1,0:T(8,128)(2,1)S(1)}, f32[8,128]{1,0:T(8,128)S(1)}) custom-call(s32[10]{0:T(128)S(1)} %stack.79.place, bf16[512,2048]{1,0:T(8,128)(2,1)S(1)} %bitcast.40, bf16[512,2048]{1,0:T(8,128)(2,1)} %collective-permute-done.1.refs_1_, bf16[512,2048]{1,0:T(8,128)(2,1)S(1)} %bitcast.34, ...), custom_call_target="tpu_custom_call" | custom-call | tf_op jit(solution)/shard_map/pallas_call | solution.py:217
  49.1 5.4 %collective-permute-start.8 = (f32[2,2048]{1,0:T(2,128)S(1)}, f32[2,2048]{1,0:T(2,128)S(1)}, u32[]{:S(2)}, u32[]{:S(2)}) collective-permute-start(f32[2,2048]{1,0:T(2,128)S(1)} %get-tuple-element.40.refs_2_), channel_id=1, source_target_pairs={{0,240},{16,224},{32,0},{48,16},{64,32},{80,48},{96,64},{112,80},{... | collective-permute-start | bytes 49160 | tf_op jit(solution)/shard_map/ppermute | solution.py:152
  55.3 5.0 %collective-permute-done.9.refs_2_.refs_4_ = f32[2,2048]{1,0:T(2,128)S(1)} collective-permute-done((f32[2,2048]{1,0:T(2,128)S(1)}, f32[2,2048]{1,0:T(2,128)S(1)}, u32[]{:S(2)}, u32[]{:S(2)}) %collective-permute-start.9) | collective-permute-done | bytes 16416 | tf_op jit(solution)/shard_map/ppermute | solution.py:152
  60.3 2.1 %shard_map.79 = (f32[4,2048]{1,0:T(4,128)S(1)}, f32[8,64]{1,0:T(8,128)S(1)}) custom-call(s32[1]{0:T(128)} %bitcast.6.refs_0_, f32[2,2048]{1,0:T(2,128)S(1)} %get-tuple-element.41.refs_1_, f32[2,2048]{1,0:T(2,128)S(1)} %get-tuple-element.40.refs_2_, f32[2,2048]{1,0:T(2,128)S(1)} %collective-permute-done.8.refs_1_.refs_3_, ...), custom_call_target="tpu_custom_call" | custom-call | tf_op jit(solution)/shard_map/pallas_call | solution.py:70
  62.5 3.6 %collective-permute-start.12 = (f32[4,2048]{1,0:T(4,128)S(1)}, f32[4,2048]{1,0:T(4,128)S(1)}, u32[]{:S(2)}, u32[]{:S(2)}) collective-permute-start(f32[4,2048]{1,0:T(4,128)S(1)} %get-tuple-element.43.refs_0_), channel_id=1, source_target_pairs={{0,1},{1,0},{2,3},{3,2},{4,5},{5,4},{6,7},{7,6},{8,9},{9,8},{10,11... | collective-permute-start | bytes 98312 | tf_op jit(solution)/shard_map/ppermute | solution.py:130
  67.6 3.3 %collective-permute-done.13.refs_1_ = f32[4,2048]{1,0:T(4,128)S(1)} collective-permute-done((f32[4,2048]{1,0:T(4,128)S(1)}, f32[4,2048]{1,0:T(4,128)S(1)}, u32[]{:S(2)}, u32[]{:S(2)}) %collective-permute-start.13) | collective-permute-done | bytes 32800 | tf_op jit(solution)/shard_map/ppermute | solution.py:130
  70.9 1.6 shard_map.82
  72.5 3.0 %collective-permute-start.14 = (s16[128,1152]{1,0:T(8,128)(2,1)S(1)}, s16[128,1152]{1,0:T(8,128)(2,1)S(1)}, u32[]{:S(2)}, u32[]{:S(2)}) collective-permute-start(s16[128,1152]{1,0:T(8,128)(2,1)S(1)} %get-tuple-element.44), channel_id=1, source_target_pairs={{0,14},{2,0},{4,2},{6,4},{8,6},{10,8},{12,10},{14,12},{1,15},{3,1}... | collective-permute-start | bytes 884744 | tf_op jit(solution)/shard_map/ppermute | solution.py:282
  75.5 9.2 %collective-permute-done.16.refs_1_ = f32[4,2048]{1,0:T(4,128)S(1)} collective-permute-done((f32[4,2048]{1,0:T(4,128)S(1)}, f32[4,2048]{1,0:T(4,128)S(1)}, u32[]{:S(2)}, u32[]{:S(2)}) %collective-permute-start.16) | collective-permute-done | bytes 32800 | tf_op jit(solution)/shard_map/ppermute | solution.py:130
  84.7 3.6 %collective-permute-start.17 = (f32[4,2048]{1,0:T(4,128)S(1)}, f32[4,2048]{1,0:T(4,128)S(1)}, u32[]{:S(2)}, u32[]{:S(2)}) collective-permute-start(f32[4,2048]{1,0:T(4,128)S(1)} %shard_map.83.refs_0_), channel_id=1, source_target_pairs={{0,8},{2,10},{4,12},{6,14},{8,0},{10,2},{12,4},{14,6},{1,9},{3,11}... | collective-permute-start | bytes 98312 | tf_op jit(solution)/shard_map/ppermute | solution.py:130
  88.2 3.1 %collective-permute-done.17.refs_1_ = f32[4,2048]{1,0:T(4,128)S(1)} collective-permute-done((f32[4,2048]{1,0:T(4,128)S(1)}, f32[4,2048]{1,0:T(4,128)S(1)}, u32[]{:S(2)}, u32[]{:S(2)}) %collective-permute-start.17) | collective-permute-done | bytes 32800 | tf_op jit(solution)/shard_map/ppermute | solution.py:130
  91.4 1.7 %shard_map.85 = (s16[128,1152]{1,0:T(8,128)(2,1)S(1)}, s16[128,1152]{1,0:T(8,128)(2,1)S(1)}, f32[8,128]{1,0:T(8,128)S(1)}) custom-call(f32[8,128,1024]{2,1,0:T(8,128)S(1)} %get-tuple-element.36.refs_0_, s16[4,128,1152]{2,1,0:T(8,128)(2,1)} %collective-permute-done.11.refs_1_, s16[128,1152]{1,0:T(8,128)(2,1)S(1)} %collective-permute-done.14.refs_2_, ...), custom_call_target="tpu_custom_call" | custom-call | tf_op jit(solution)/shard_map/pallas_call | solution.py:255
  93.1 2.2 %collective-permute-start.18 = (s16[128,1152]{1,0:T(8,128)(2,1)S(1)}, s16[128,1152]{1,0:T(8,128)(2,1)S(1)}, u32[]{:S(2)}, u32[]{:S(2)}) collective-permute-start(s16[128,1152]{1,0:T(8,128)(2,1)S(1)} %get-tuple-element.47), channel_id=1, source_target_pairs={{0,14},{2,0},{4,2},{6,4},{8,6},{10,8},{12,10},{14,12},{1,15},{3,1}... | collective-permute-start | bytes 884744 | tf_op jit(solution)/shard_map/ppermute | solution.py:282
  96.2 1.8 %collective-permute-done.20.refs_1_ = f32[4,2048]{1,0:T(4,128)S(1)} collective-permute-done((f32[4,2048]{1,0:T(4,128)S(1)}, f32[4,2048]{1,0:T(4,128)S(1)}, u32[]{:S(2)}, u32[]{:S(2)}) %collective-permute-start.20) | collective-permute-done | bytes 32800 | tf_op jit(solution)/shard_map/ppermute | solution.py:130
  98.0 5.3 %collective-permute-start.21 = (f32[2,2048]{1,0:T(2,128)S(1)}, f32[2,2048]{1,0:T(2,128)S(1)}, u32[]{:S(2)}, u32[]{:S(2)}) collective-permute-start(f32[2,2048]{1,0:T(2,128)S(1)} %get-tuple-element.50.refs_6_), channel_id=1, source_target_pairs={{0,240},{16,224},{32,0},{48,16},{64,32},{80,48},{96,64},{112,80},{... | collective-permute-start | bytes 49160 | tf_op jit(solution)/shard_map/ppermute | solution.py:152
  104.2 5.0 %collective-permute-done.22.refs_5_.refs_8_ = f32[2,2048]{1,0:T(2,128)S(1)} collective-permute-done((f32[2,2048]{1,0:T(2,128)S(1)}, f32[2,2048]{1,0:T(2,128)S(1)}, u32[]{:S(2)}, u32[]{:S(2)}) %collective-permute-start.22) | collective-permute-done | bytes 16416 | tf_op jit(solution)/shard_map/ppermute | solution.py:152
  111.2 5.6 %collective-permute-start.23 = (bf16[16,64,2048]{2,1,0:T(8,128)(2,1)}, bf16[16,64,2048]{2,1,0:T(8,128)(2,1)}, u32[]{:S(2)}, u32[]{:S(2)}) collective-permute-start(bf16[16,64,2048]{2,1,0:T(8,128)(2,1)} %shard_map.88.weights), channel_id=1, source_target_pairs={{0,1},{1,0},{2,3},{3,2},{4,5},{5,4},{6,7},{7,6},{8,9},{9,8},{10,11... | collective-permute-start | bytes 12582920 | tf_op jit(solution)/shard_map/ppermute | solution.py:130
  116.8 3.0 %collective-permute-start.24 = (s16[128,1152]{1,0:T(8,128)(2,1)S(1)}, s16[128,1152]{1,0:T(8,128)(2,1)S(1)}, u32[]{:S(2)}, u32[]{:S(2)}) collective-permute-start(s16[128,1152]{1,0:T(8,128)(2,1)S(1)} %get-tuple-element.54), channel_id=1, source_target_pairs={{0,14},{2,0},{4,2},{6,4},{8,6},{10,8},{12,10},{14,12},{1,15},{3,1}... | collective-permute-start | bytes 884744 | tf_op jit(solution)/shard_map/ppermute | solution.py:282
  120.3 3.6 %collective-permute-done.23.other_weights = bf16[16,64,2048]{2,1,0:T(8,128)(2,1)} collective-permute-done((bf16[16,64,2048]{2,1,0:T(8,128)(2,1)}, bf16[16,64,2048]{2,1,0:T(8,128)(2,1)}, u32[]{:S(2)}, u32[]{:S(2)}) %collective-permute-start.23) | collective-permute-done | bytes 4194336 | tf_op jit(solution)/shard_map/ppermute | solution.py:130
  123.9 8.1 %shard_map.89 = (bf16[512,2048]{1,0:T(8,128)(2,1)}, f32[8,128]{1,0:T(8,128)}) custom-call(s32[3]{0:T(128)} %pad_add_fusion.2.at, bf16[512,2048]{1,0:T(8,128)(2,1)} %bitcast.29, bf16[16,64,2048]{2,1,0:T(8,128)(2,1)} %shard_map.88.weights, bf16[16,64,2048]{2,1,0:T(8,128)(2,1)} %collective-permute-done.23.other_weights, f32[8,128]{1,0:T(8,128)} %copy-done.9), custom_call_target="tpu_custom_call" | custom-call | tf_op jit(solution)/shard_map/pallas_call | solution.py:326
  133.3 3.0 %collective-permute-start.26 = (s16[128,1152]{1,0:T(8,128)(2,1)S(1)}, s16[128,1152]{1,0:T(8,128)(2,1)S(1)}, u32[]{:S(2)}, u32[]{:S(2)}) collective-permute-start(s16[128,1152]{1,0:T(8,128)(2,1)S(1)} %get-tuple-element.60), channel_id=1, source_target_pairs={{0,14},{2,0},{4,2},{6,4},{8,6},{10,8},{12,10},{14,12},{1,15},{3,1}... | collective-permute-start | bytes 884744 | tf_op jit(solution)/shard_map/ppermute | solution.py:282
  136.9 7.6 %shard_map.91 = (bf16[512,2048]{1,0:T(8,128)(2,1)}, f32[8,128]{1,0:T(8,128)}) custom-call(s32[3]{0:T(128)} %pad_add_fusion.at, bf16[512,2048]{1,0:T(8,128)(2,1)} %bitcast.30, bf16[16,64,2048]{2,1,0:T(8,128)(2,1)} %shard_map.88.weights, bf16[16,64,2048]{2,1,0:T(8,128)(2,1)} %collective-permute-done.23.other_weights, ...), custom_call_target="tpu_custom_call", output_to_operand_aliasing={{0}: (4, {})} | custom-call | tf_op jit(solution)/shard_map/pallas_call | solution.py:326
  (91 shorter events, 21.7 us)
Async XLA Ops:
  7.2 103.3 %all-gather.2.cloned.1.call-start = ((), (), s32[]{:S(2)}) async-start(), calls=%async_computation | async-start | bytes 4718592 | tf_op jit(solution)/shard_map/all_gather | solution.py:401
  7.2 12.0 %collective-permute-start.1 = (bf16[512,2048]{1,0:T(8,128)(2,1)}, bf16[512,2048]{1,0:T(8,128)(2,1)}, u32[]{:S(2)}, u32[]{:S(2)}) collective-permute-start(bf16[512,2048]{1,0:T(8,128)(2,1)} %bitcast.36), channel_id=1, source_target_pairs={{0,1},{1,0},{2,3},{3,2},{4,5},{5,4},{6,7},{7,6},{8,9},{9,8},{10,11... | collective-permute-start | bytes 6291464 | tf_op jit(solution)/shard_map/ppermute | solution.py:130
  10.5 8.6 %collective-permute-start.2 = (bf16[512,2048]{1,0:T(8,128)(2,1)}, bf16[512,2048]{1,0:T(8,128)(2,1)}, u32[]{:S(2)}, u32[]{:S(2)}) collective-permute-start(bf16[512,2048]{1,0:T(8,128)(2,1)} %bitcast.28), channel_id=1, source_target_pairs={{0,1},{1,0},{2,3},{3,2},{4,5},{5,4},{6,7},{7,6},{8,9},{9,8},{10,11... | collective-permute-start | bytes 6291464 | tf_op jit(solution)/shard_map/ppermute | solution.py:130
  10.6 7.7 %collective-permute-start = (bf16[64,2048]{1,0:T(8,128)(2,1)}, bf16[64,2048]{1,0:T(8,128)(2,1)S(1)}, u32[]{:S(2)}, u32[]{:S(2)}) collective-permute-start(bf16[64,2048]{1,0:T(8,128)(2,1)} %bitcast.42), channel_id=1, source_target_pairs={{0,16},{16,0},{1,17},{17,1},{2,18},{18,2},{3,19},{19,3},{4,20},{20... | collective-permute-start | bytes 786440 | tf_op jit(solution)/shard_map/ppermute | solution.py:130
  17.0 1.4 collective-permute-start.3
  19.2 8.6 %collective-permute-start.4 = (f32[4,2048]{1,0:T(4,128)S(1)}, f32[4,2048]{1,0:T(4,128)S(1)}, u32[]{:S(2)}, u32[]{:S(2)}) collective-permute-start(f32[4,2048]{1,0:T(4,128)S(1)} %shard_map.68.refs_3_.refs_4_.refs_0_), channel_id=1, source_target_pairs={{0,16},{16,0},{1,17},{17,1},{2,18},{18,2},{3,19},{19,3},{4,20},{20... | collective-permute-start | bytes 98312 | tf_op jit(solution)/shard_map/ppermute | solution.py:130
  27.8 43.1 %collective-permute-start.11 = (s16[4,128,1152]{2,1,0:T(8,128)(2,1)}, s16[4,128,1152]{2,1,0:T(8,128)(2,1)}, u32[]{:S(2)}, u32[]{:S(2)}) collective-permute-start(s16[4,128,1152]{2,1,0:T(8,128)(2,1)} %shard_map.78), channel_id=1, source_target_pairs={{0,16},{16,0},{1,17},{17,1},{2,18},{18,2},{3,19},{19,3},{4,20},{20... | collective-permute-start | bytes 3538952 | tf_op jit(solution)/shard_map/ppermute | solution.py:130
  29.3 3.2 %collective-permute-start.5 = (f32[4,2048]{1,0:T(4,128)S(1)}, f32[4,2048]{1,0:T(4,128)S(1)}, u32[]{:S(2)}, u32[]{:S(2)}) collective-permute-start(f32[4,2048]{1,0:T(4,128)S(1)} %shard_map.71.refs_0_.refs_1_), channel_id=1, source_target_pairs={{0,2},{2,0},{4,6},{6,4},{8,10},{10,8},{12,14},{14,12},{1,3},{3,1},... | collective-permute-start | bytes 98312 | tf_op jit(solution)/shard_map/ppermute | solution.py:130
  32.4 7.3 %collective-permute-start.6 = (f32[4,2048]{1,0:T(4,128)S(1)}, f32[4,2048]{1,0:T(4,128)S(1)}, u32[]{:S(2)}, u32[]{:S(2)}) collective-permute-start(f32[4,2048]{1,0:T(4,128)S(1)} %shard_map.72.refs_4_.refs_0_), channel_id=1, source_target_pairs={{0,4},{2,6},{4,0},{6,2},{8,12},{10,14},{12,8},{14,10},{1,5},{3,7},... | collective-permute-start | bytes 98312 | tf_op jit(solution)/shard_map/ppermute | solution.py:130
  39.7 69.5 %copy-start.2 = (f32[8,128,1024]{2,1,0:T(8,128)}, f32[8,128,1024]{2,1,0:T(8,128)S(1)}, u32[]{:S(2)}) copy-start(f32[8,128,1024]{2,1,0:T(8,128)S(1)} %get-tuple-element.36.refs_0_) | copy-start | bytes 12582916
  39.7 9.3 %collective-permute-start.7 = (f32[4,2048]{1,0:T(4,128)S(1)}, f32[4,2048]{1,0:T(4,128)S(1)}, u32[]{:S(2)}, u32[]{:S(2)}) collective-permute-start(f32[4,2048]{1,0:T(4,128)S(1)} %shard_map.74.refs_4_.refs_0_), channel_id=1, source_target_pairs={{0,8},{2,10},{4,12},{6,14},{8,0},{10,2},{12,4},{14,6},{1,9},{3,11}... | collective-permute-start | bytes 98312 | tf_op jit(solution)/shard_map/ppermute | solution.py:130
  49.0 11.3 %copy-start.8 = (bf16[1,64,2048]{2,1,0:T(8,128)(2,1)S(1)}, bf16[1,64,2048]{2,1,0:T(8,128)(2,1)}, u32[]{:S(2)}) copy-start(bf16[1,64,2048]{2,1,0:T(8,128)(2,1)} %param.6) | copy-start | bytes 786436
  49.1 6.2 %collective-permute-start.8 = (f32[2,2048]{1,0:T(2,128)S(1)}, f32[2,2048]{1,0:T(2,128)S(1)}, u32[]{:S(2)}, u32[]{:S(2)}) collective-permute-start(f32[2,2048]{1,0:T(2,128)S(1)} %get-tuple-element.40.refs_2_), channel_id=1, source_target_pairs={{0,240},{16,224},{32,0},{48,16},{64,32},{80,48},{96,64},{112,80},{... | collective-permute-start | bytes 49160 | tf_op jit(solution)/shard_map/ppermute | solution.py:152
  54.4 5.9 %collective-permute-start.9 = (f32[2,2048]{1,0:T(2,128)S(1)}, f32[2,2048]{1,0:T(2,128)S(1)}, u32[]{:S(2)}, u32[]{:S(2)}) collective-permute-start(f32[2,2048]{1,0:T(2,128)S(1)} %get-tuple-element.41.refs_1_), channel_id=1, source_target_pairs={{0,32},{16,48},{32,64},{48,80},{64,96},{80,112},{96,144},{112,128}... | collective-permute-start | bytes 49160 | tf_op jit(solution)/shard_map/ppermute | solution.py:152
  60.3 43.0 %collective-permute-start.10 = (s16[4,128,1152]{2,1,0:T(8,128)(2,1)S(1)}, s16[4,128,1152]{2,1,0:T(8,128)(2,1)S(1)}, u32[]{:S(2)}, u32[]{:S(2)}) collective-permute-start(s16[4,128,1152]{2,1,0:T(8,128)(2,1)S(1)} %shard_map.77), channel_id=1, source_target_pairs={{0,16},{16,0},{1,17},{17,1},{2,18},{18,2},{3,19},{19,3},{4,20},{20... | collective-permute-start | bytes 3538952 | tf_op jit(solution)/shard_map/ppermute | solution.py:130
  62.5 4.5 %collective-permute-start.12 = (f32[4,2048]{1,0:T(4,128)S(1)}, f32[4,2048]{1,0:T(4,128)S(1)}, u32[]{:S(2)}, u32[]{:S(2)}) collective-permute-start(f32[4,2048]{1,0:T(4,128)S(1)} %get-tuple-element.43.refs_0_), channel_id=1, source_target_pairs={{0,1},{1,0},{2,3},{3,2},{4,5},{5,4},{6,7},{7,6},{8,9},{9,8},{10,11... | collective-permute-start | bytes 98312 | tf_op jit(solution)/shard_map/ppermute | solution.py:130
  67.0 3.9 %collective-permute-start.13 = (f32[4,2048]{1,0:T(4,128)S(1)}, f32[4,2048]{1,0:T(4,128)S(1)}, u32[]{:S(2)}, u32[]{:S(2)}) collective-permute-start(f32[4,2048]{1,0:T(4,128)S(1)} %shard_map.80.refs_0_), channel_id=1, source_target_pairs={{0,2},{2,0},{4,6},{6,4},{8,10},{10,8},{12,14},{14,12},{1,3},{3,1},... | collective-permute-start | bytes 98312 | tf_op jit(solution)/shard_map/ppermute | solution.py:130
  72.5 18.9 %collective-permute-start.14 = (s16[128,1152]{1,0:T(8,128)(2,1)S(1)}, s16[128,1152]{1,0:T(8,128)(2,1)S(1)}, u32[]{:S(2)}, u32[]{:S(2)}) collective-permute-start(s16[128,1152]{1,0:T(8,128)(2,1)S(1)} %get-tuple-element.44), channel_id=1, source_target_pairs={{0,14},{2,0},{4,2},{6,4},{8,6},{10,8},{12,10},{14,12},{1,15},{3,1}... | collective-permute-start | bytes 884744 | tf_op jit(solution)/shard_map/ppermute | solution.py:282
  75.5 15.9 %collective-permute-start.15 = (s16[128,1152]{1,0:T(8,128)(2,1)S(1)}, s16[128,1152]{1,0:T(8,128)(2,1)S(1)}, u32[]{:S(2)}, u32[]{:S(2)}) collective-permute-start(s16[128,1152]{1,0:T(8,128)(2,1)S(1)} %get-tuple-element.45), channel_id=1, source_target_pairs={{0,2},{2,4},{4,6},{6,8},{8,10},{10,12},{12,14},{14,0},{1,3},{3,5},... | collective-permute-start | bytes 884744 | tf_op jit(solution)/shard_map/ppermute | solution.py:282
  75.5 9.2 %collective-permute-start.16 = (f32[4,2048]{1,0:T(4,128)S(1)}, f32[4,2048]{1,0:T(4,128)S(1)}, u32[]{:S(2)}, u32[]{:S(2)}) collective-permute-start(f32[4,2048]{1,0:T(4,128)S(1)} %shard_map.81.refs_2_.refs_0_), channel_id=1, source_target_pairs={{0,4},{2,6},{4,0},{6,2},{8,12},{10,14},{12,8},{14,10},{1,5},{3,7},... | collective-permute-start | bytes 98312 | tf_op jit(solution)/shard_map/ppermute | solution.py:130
  84.7 6.7 %collective-permute-start.17 = (f32[4,2048]{1,0:T(4,128)S(1)}, f32[4,2048]{1,0:T(4,128)S(1)}, u32[]{:S(2)}, u32[]{:S(2)}) collective-permute-start(f32[4,2048]{1,0:T(4,128)S(1)} %shard_map.83.refs_0_), channel_id=1, source_target_pairs={{0,8},{2,10},{4,12},{6,14},{8,0},{10,2},{12,4},{14,6},{1,9},{3,11}... | collective-permute-start | bytes 98312 | tf_op jit(solution)/shard_map/ppermute | solution.py:130
  93.1 16.2 %collective-permute-start.18 = (s16[128,1152]{1,0:T(8,128)(2,1)S(1)}, s16[128,1152]{1,0:T(8,128)(2,1)S(1)}, u32[]{:S(2)}, u32[]{:S(2)}) collective-permute-start(s16[128,1152]{1,0:T(8,128)(2,1)S(1)} %get-tuple-element.47), channel_id=1, source_target_pairs={{0,14},{2,0},{4,2},{6,4},{8,6},{10,8},{12,10},{14,12},{1,15},{3,1}... | collective-permute-start | bytes 884744 | tf_op jit(solution)/shard_map/ppermute | solution.py:282
  95.3 14.0 %collective-permute-start.19 = (s16[128,1152]{1,0:T(8,128)(2,1)S(1)}, s16[128,1152]{1,0:T(8,128)(2,1)S(1)}, u32[]{:S(2)}, u32[]{:S(2)}) collective-permute-start(s16[128,1152]{1,0:T(8,128)(2,1)S(1)} %get-tuple-element.48), channel_id=1, source_target_pairs={{0,2},{2,4},{4,6},{6,8},{8,10},{10,12},{12,14},{14,0},{1,3},{3,5},... | collective-permute-start | bytes 884744 | tf_op jit(solution)/shard_map/ppermute | solution.py:282
  95.3 2.8 %collective-permute-start.20 = (f32[4,2048]{1,0:T(4,128)S(1)}, f32[4,2048]{1,0:T(4,128)S(1)}, u32[]{:S(2)}, u32[]{:S(2)}) collective-permute-start(f32[4,2048]{1,0:T(4,128)S(1)} %shard_map.84.refs_4_.refs_0_), channel_id=1, source_target_pairs={{0,16},{16,0},{1,17},{17,1},{2,18},{18,2},{3,19},{19,3},{4,20},{20... | collective-permute-start | bytes 98312 | tf_op jit(solution)/shard_map/ppermute | solution.py:130
  98.0 6.2 %collective-permute-start.21 = (f32[2,2048]{1,0:T(2,128)S(1)}, f32[2,2048]{1,0:T(2,128)S(1)}, u32[]{:S(2)}, u32[]{:S(2)}) collective-permute-start(f32[2,2048]{1,0:T(2,128)S(1)} %get-tuple-element.50.refs_6_), channel_id=1, source_target_pairs={{0,240},{16,224},{32,0},{48,16},{64,32},{80,48},{96,64},{112,80},{... | collective-permute-start | bytes 49160 | tf_op jit(solution)/shard_map/ppermute | solution.py:152
  103.3 5.9 %collective-permute-start.22 = (f32[2,2048]{1,0:T(2,128)S(1)}, f32[2,2048]{1,0:T(2,128)S(1)}, u32[]{:S(2)}, u32[]{:S(2)}) collective-permute-start(f32[2,2048]{1,0:T(2,128)S(1)} %get-tuple-element.51.refs_5_), channel_id=1, source_target_pairs={{0,32},{16,48},{32,64},{48,80},{64,96},{80,112},{96,144},{112,128}... | collective-permute-start | bytes 49160 | tf_op jit(solution)/shard_map/ppermute | solution.py:152
  111.2 12.7 %collective-permute-start.23 = (bf16[16,64,2048]{2,1,0:T(8,128)(2,1)}, bf16[16,64,2048]{2,1,0:T(8,128)(2,1)}, u32[]{:S(2)}, u32[]{:S(2)}) collective-permute-start(bf16[16,64,2048]{2,1,0:T(8,128)(2,1)} %shard_map.88.weights), channel_id=1, source_target_pairs={{0,1},{1,0},{2,3},{3,2},{4,5},{5,4},{6,7},{7,6},{8,9},{9,8},{10,11... | collective-permute-start | bytes 12582920 | tf_op jit(solution)/shard_map/ppermute | solution.py:130
  116.8 15.3 %collective-permute-start.24 = (s16[128,1152]{1,0:T(8,128)(2,1)S(1)}, s16[128,1152]{1,0:T(8,128)(2,1)S(1)}, u32[]{:S(2)}, u32[]{:S(2)}) collective-permute-start(s16[128,1152]{1,0:T(8,128)(2,1)S(1)} %get-tuple-element.54), channel_id=1, source_target_pairs={{0,14},{2,0},{4,2},{6,4},{8,6},{10,8},{12,10},{14,12},{1,15},{3,1}... | collective-permute-start | bytes 884744 | tf_op jit(solution)/shard_map/ppermute | solution.py:282
  119.7 12.3 %collective-permute-start.25 = (s16[128,1152]{1,0:T(8,128)(2,1)S(1)}, s16[128,1152]{1,0:T(8,128)(2,1)S(1)}, u32[]{:S(2)}, u32[]{:S(2)}) collective-permute-start(s16[128,1152]{1,0:T(8,128)(2,1)S(1)} %get-tuple-element.55), channel_id=1, source_target_pairs={{0,2},{2,4},{4,6},{6,8},{8,10},{10,12},{12,14},{14,0},{1,3},{3,5},... | collective-permute-start | bytes 884744 | tf_op jit(solution)/shard_map/ppermute | solution.py:282
  123.9 8.2 %copy-start.3 = (f32[8,128,1024]{2,1,0:T(8,128)S(1)}, f32[8,128,1024]{2,1,0:T(8,128)}, u32[]{:S(2)}) copy-start(f32[8,128,1024]{2,1,0:T(8,128)} %copy-done.2) | copy-start | bytes 12582916
  133.3 11.2 %collective-permute-start.26 = (s16[128,1152]{1,0:T(8,128)(2,1)S(1)}, s16[128,1152]{1,0:T(8,128)(2,1)S(1)}, u32[]{:S(2)}, u32[]{:S(2)}) collective-permute-start(s16[128,1152]{1,0:T(8,128)(2,1)S(1)} %get-tuple-element.60), channel_id=1, source_target_pairs={{0,14},{2,0},{4,2},{6,4},{8,6},{10,8},{12,10},{14,12},{1,15},{3,1}... | collective-permute-start | bytes 884744 | tf_op jit(solution)/shard_map/ppermute | solution.py:282
  145.8 1.9 %collective-permute-start.27 = (f32[64,1024]{1,0:T(8,128)S(1)}, f32[64,1024]{1,0:T(8,128)S(1)}, u32[]{:S(2)}, u32[]{:S(2)}) collective-permute-start(f32[64,1024]{1,0:T(8,128)S(1)} %get-tuple-element.63), channel_id=1, source_target_pairs={{0,1},{1,0},{2,3},{3,2},{4,5},{5,4},{6,7},{7,6},{8,9},{9,8},{10,11... | collective-permute-start | bytes 786440 | tf_op jit(solution)/shard_map/ppermute | solution.py:130
  (11 other events, 15.6 us)
Sparse Core Ops, SparseCore 0:
  19.3 58.9 all-gather.1

commit v3 on v1

--- a/solution.py
+++ b/solution.py
@@ -19,7 +19,6 @@
 NO_ROOM = 56 * 2**20
 MARK = jax.ShapeDtypeStruct((8, 128), jnp.float32)
 NO_COST = pl.CostEstimate(flops=0, bytes_accessed=0, transcendentals=0)
-STEPS_BACK = (("core", 1), ("z", 1), ("z", 2), ("z", 4), ("xl", 1))
 STEPS_ALONG = (("core", 1), ("xl", 1), ("z", 1), ("z", 2), ("z", 4))
 
 CYCLE = ("xh", "y")
@@ -257,7 +256,7 @@
         grid=(1,),
         in_specs=[
             pl.BlockSpec((2, rows, columns), lambda i: (step, 0, 0)),
-            pl.BlockSpec((2, rows, wide), lambda i: (step % 2, 0, 0)),
+            pl.BlockSpec((2, rows, wide), lambda i: (step if step < 2 else 0, 0, 0)),
         ]
         + [whole] * len(received)
         + [pl.BlockSpec(memory_space=pltpu.VMEM)] * len(after),
@@ -415,8 +414,9 @@
         return (shifted(down, "z", -1), shifted(up, "z", 1) if step < 3 else up), (mark,)
 
     value = shard_sum(value, STEPS_ALONG[3:4], {"z2": (mark,)})
-    second, mark = chunks(
-        functools.partial(chunk_kernel, 4), (pieces, MARK), scalars, *tokens, (value,)
+    piece = jax.ShapeDtypeStruct((2, 2 * rows, columns + LANES), jnp.int16)
+    second, third, mark = chunks(
+        functools.partial(chunk_kernel, 4), (piece, piece, MARK), scalars, *tokens, (value,)
     )
     right, left = shard_sum(value, STEPS_ALONG[4:], {"z4": (mark,)}, "z4")
     arrived = neighbours(right, left)
@@ -429,15 +429,17 @@
         at,
         sent,
     )
-    value = shard_sum(back, STEPS_BACK[:2], {})
+    value = shard_sum(back, STEPS_ALONG[:2], {})
+    third = partner(held(third, (value,)), "xl", 1)
+    value = shard_sum(value, STEPS_ALONG[2:3], {})
     received, sent = hops(1, received, (value,), first)
-    value = shard_sum(value, STEPS_BACK[2:3], {"z2": sent})
+    value = shard_sum(value, STEPS_ALONG[3:4], {"z2": sent})
     received, sent = hops(2, received, (value,), second)
     weights = held(weights, sent, (), NO_ROOM)
     both = (cotan, weights, partner(weights, "core", 1))
     half, mark = backward_input(core, x, 0, *both, sent)
-    right, left = shard_sum(value, STEPS_BACK[3:], {"z4": (mark,)}, "xl1")
-    received, sent = hops(3, received, (right,), second)
+    right, left = shard_sum(value, STEPS_ALONG[4:], {"z4": (mark,)}, "z4")
+    received, sent = hops(3, received, (right,), third)
     arrived = neighbours(right, left)
     grad_in, mark = backward_input(core, x, 2, *both, sent, (half,))
     kept, given, _ = kernel_call(

time: 144 us -> 141 us (0.979)
  waiting for transfers between devices: 30.7 us -> 28 us
    ppermute x17 -> x18, waiting for transfers between devices: 23.2 us -> 20.7 us  [partner(): return lax.ppermute(value, axis, [(i, i ^ step) for i in range(count)])]
    ppermute x17 -> x18, starting transfers between devices: 30.2 us -> 29.8 us  [partner(): return lax.ppermute(value, axis, [(i, i ^ step) for i in range(count)])]
  transfers between devices with their start and end apart: 29 -> 30, of which waited for: 11 -> 11; matrix products, arithmetic and copies ran while one was open for 2% -> 2% of each run, Pallas kernels for 24% -> 25%
where the time goes in v3:
time: 141 us; the launch traced here: 140 us
  starting transfers between devices  46.8 us (33%)
  Pallas kernels  37.7 us (27%)
  waiting for transfers between devices  28 us (20%)
  between operations  14.4 us (10%)
  local copies, waits for them, and re-layouts  10.2 us (7%)
  other arithmetic  2.78 us (2%)
    ppermute x18, starting transfers between devices, partner(): return lax.ppermute(value, axis, [(i, i ^ step) for i in range(count)])  29.8 us
    ppermute x18, waiting for transfers between devices, partner(): return lax.ppermute(value, axis, [(i, i ^ step) for i in range(count)])  20.7 us
    pallas_call x2, Pallas kernels, backward_input(): pl.pallas_call(input_kernel, grid_spec=pltpu.PrefetchScalarGridSpec(num_s...  15.7 us
    pallas_call x3, Pallas kernels, chunks(): pl.pallas_call(body, grid_spec=pltpu.PrefetchScalarGridSpec(num_scalar_pr...  13.6 us
    ppermute x4, starting transfers between devices, passed_along(): return lax.ppermute(value, CYCLE + ('xl',), pairs)  10 us
    unnamed x32, local copies, waits for them, and re-layouts  9.98 us
    ppermute x7, starting transfers between devices, shifted(): lax.ppermute(value, axis, [(i, (i + steps) % count) for i in range(count)])  6.9 us
    ppermute x4, waiting for transfers between devices, passed_along(): return lax.ppermute(value, CYCLE + ('xl',), pairs)  5.91 us
  transfers between devices with their start and end apart: 30, of which 11 were waited for; matrix products, arithmetic and copies ran while one was open for 2% of the time, Pallas kernels for 25%

profile of v3, /device:TPU:1, one launch (start us, length us, event | category | flops | bytes accessed | tf_op | source)
XLA Modules:
  0.0 139.9 jit_solution(2390783729425707850)
XLA Ops:
  7.2 3.3 %collective-permute-start.1 = (bf16[512,2048]{1,0:T(8,128)(2,1)}, bf16[512,2048]{1,0:T(8,128)(2,1)}, u32[]{:S(2)}, u32[]{:S(2)}) collective-permute-start(bf16[512,2048]{1,0:T(8,128)(2,1)} %bitcast.36), channel_id=1, source_target_pairs={{0,1},{1,0},{2,3},{3,2},{4,5},{5,4},{6,7},{7,6},{8,9},{9,8},{10,11... | collective-permute-start | bytes 6291464 | tf_op jit(solution)/shard_map/ppermute | solution.py:129
  11.5 1.6 %copy-done = bf16[1,512,2048]{2,1,0:T(8,128)(2,1)S(1)} copy-done((bf16[1,512,2048]{2,1,0:T(8,128)(2,1)S(1)}, bf16[1,512,2048]{2,1,0:T(8,128)(2,1)}, u32[]{:S(2)}) %copy-start) | copy-done | bytes 2097176
  13.1 1.6 %copy-done.4 = bf16[1,512,2048]{2,1,0:T(8,128)(2,1)S(1)} copy-done((bf16[1,512,2048]{2,1,0:T(8,128)(2,1)S(1)}, bf16[1,512,2048]{2,1,0:T(8,128)(2,1)}, u32[]{:S(2)}) %copy-start.4) | copy-done | bytes 2097176
  15.6 1.4 shard_map.67.refs_0_
  19.2 1.8 %collective-permute-start.4 = (f32[4,2048]{1,0:T(4,128)S(1)}, f32[4,2048]{1,0:T(4,128)S(1)}, u32[]{:S(2)}, u32[]{:S(2)}) collective-permute-start(f32[4,2048]{1,0:T(4,128)S(1)} %shard_map.68.refs_3_.refs_4_.refs_0_), channel_id=1, source_target_pairs={{0,16},{16,0},{1,17},{17,1},{2,18},{18,2},{3,19},{19,3},{4,20},{20... | collective-permute-start | bytes 98312 | tf_op jit(solution)/shard_map/ppermute | solution.py:129
  21.2 1.6 %copy-done.5 = bf16[1,512,2048]{2,1,0:T(8,128)(2,1)S(1)} copy-done((bf16[1,512,2048]{2,1,0:T(8,128)(2,1)S(1)}, bf16[1,512,2048]{2,1,0:T(8,128)(2,1)}, u32[]{:S(2)}) %copy-start.5) | copy-done | bytes 2097176
  22.7 5.0 %shard_map.70 = (s16[4,128,1152]{2,1,0:T(8,128)(2,1)}, f32[8,128]{1,0:T(8,128)S(1)}) custom-call(s32[10]{0:T(128)S(1)} %stack.79.place, bf16[512,2048]{1,0:T(8,128)(2,1)S(1)} %bitcast.38, bf16[512,2048]{1,0:T(8,128)(2,1)} %collective-permute-done.1.refs_1_, bf16[512,2048]{1,0:T(8,128)(2,1)S(1)} %bitcast.32, ...), custom_call_target="tpu_custom_call" | custom-call | tf_op jit(solution)/shard_map/pallas_call | solution.py:216
  27.8 1.4 %collective-permute-start.7 = (s16[4,128,1152]{2,1,0:T(8,128)(2,1)}, s16[4,128,1152]{2,1,0:T(8,128)(2,1)S(1)}, u32[]{:S(2)}, u32[]{:S(2)}) collective-permute-start(s16[4,128,1152]{2,1,0:T(8,128)(2,1)} %shard_map.76), channel_id=1, source_target_pairs={{0,16},{16,0},{1,17},{17,1},{2,18},{18,2},{3,19},{19,3},{4,20},{20... | collective-permute-start | bytes 3538952 | tf_op jit(solution)/shard_map/ppermute | solution.py:129
  29.3 3.1 %collective-permute-done.5.refs_1_ = f32[4,2048]{1,0:T(4,128)S(1)} collective-permute-done((f32[4,2048]{1,0:T(4,128)S(1)}, f32[4,2048]{1,0:T(4,128)S(1)}, u32[]{:S(2)}, u32[]{:S(2)}) %collective-permute-start.5) | collective-permute-done | bytes 32800 | tf_op jit(solution)/shard_map/ppermute | solution.py:129
  33.5 1.6 %copy-done.6 = bf16[1,512,2048]{2,1,0:T(8,128)(2,1)S(1)} copy-done((bf16[1,512,2048]{2,1,0:T(8,128)(2,1)S(1)}, bf16[1,512,2048]{2,1,0:T(8,128)(2,1)}, u32[]{:S(2)}) %copy-start.6) | copy-done | bytes 2097176
  35.1 4.6 %shard_map.73 = (f32[8,128,1024]{2,1,0:T(8,128)S(1)}, f32[8,128]{1,0:T(8,128)S(1)}) custom-call(s32[10]{0:T(128)S(1)} %stack.77.place, bf16[512,2048]{1,0:T(8,128)(2,1)S(1)} %bitcast.39, bf16[512,2048]{1,0:T(8,128)(2,1)} %collective-permute-done.1.refs_1_, bf16[512,2048]{1,0:T(8,128)(2,1)S(1)} %bitcast.33, ...), custom_call_target="tpu_custom_call" | custom-call | tf_op jit(solution)/shard_map/pallas_call | solution.py:216
  39.7 5.3 %collective-permute-start.8 = (f32[4,2048]{1,0:T(4,128)S(1)}, f32[4,2048]{1,0:T(4,128)S(1)}, u32[]{:S(2)}, u32[]{:S(2)}) collective-permute-start(f32[4,2048]{1,0:T(4,128)S(1)} %shard_map.74.refs_4_.refs_0_), channel_id=1, source_target_pairs={{0,8},{2,10},{4,12},{6,14},{8,0},{10,2},{12,4},{14,6},{1,9},{3,11}... | collective-permute-start | bytes 98312 | tf_op jit(solution)/shard_map/ppermute | solution.py:129
  45.0 4.0 %shard_map.75 = (s16[2,128,1152]{2,1,0:T(8,128)(2,1)S(1)}, s16[2,128,1152]{2,1,0:T(8,128)(2,1)S(1)}, f32[8,128]{1,0:T(8,128)S(1)}) custom-call(s32[10]{0:T(128)S(1)} %stack.79.place, bf16[512,2048]{1,0:T(8,128)(2,1)S(1)} %bitcast.40, bf16[512,2048]{1,0:T(8,128)(2,1)} %collective-permute-done.1.refs_1_, bf16[512,2048]{1,0:T(8,128)(2,1)S(1)} %bitcast.34, ...), custom_call_target="tpu_custom_call" | custom-call | tf_op jit(solution)/shard_map/pallas_call | solution.py:216
  49.0 5.2 %collective-permute-start.9 = (f32[2,2048]{1,0:T(2,128)S(1)}, f32[2,2048]{1,0:T(2,128)S(1)}, u32[]{:S(2)}, u32[]{:S(2)}) collective-permute-start(f32[2,2048]{1,0:T(2,128)S(1)} %get-tuple-element.42.refs_2_), channel_id=1, source_target_pairs={{0,240},{16,224},{32,0},{48,16},{64,32},{80,48},{96,64},{112,80},{... | collective-permute-start | bytes 49160 | tf_op jit(solution)/shard_map/ppermute | solution.py:151
  55.1 5.0 %collective-permute-done.10.refs_3_.refs_4_ = f32[2,2048]{1,0:T(2,128)S(1)} collective-permute-done((f32[2,2048]{1,0:T(2,128)S(1)}, f32[2,2048]{1,0:T(2,128)S(1)}, u32[]{:S(2)}, u32[]{:S(2)}) %collective-permute-start.10) | collective-permute-done | bytes 16416 | tf_op jit(solution)/shard_map/ppermute | solution.py:151
  60.7 2.2 %collective-permute-start.12 = (s16[128,1152]{1,0:T(8,128)(2,1)S(1)}, s16[128,1152]{1,0:T(8,128)(2,1)S(1)}, u32[]{:S(2)}, u32[]{:S(2)}) collective-permute-start(s16[128,1152]{1,0:T(8,128)(2,1)S(1)} %get-tuple-element.45), channel_id=1, source_target_pairs={{0,14},{2,0},{4,2},{6,4},{8,6},{10,8},{12,10},{14,12},{1,15},{3,1}... | collective-permute-start | bytes 884744 | tf_op jit(solution)/shard_map/ppermute | solution.py:281
  63.0 2.1 %shard_map.80 = (f32[4,2048]{1,0:T(4,128)S(1)}, f32[8,64]{1,0:T(8,128)S(1)}) custom-call(s32[1]{0:T(128)} %bitcast.6.refs_0_, f32[2,2048]{1,0:T(2,128)S(1)} %get-tuple-element.43.refs_1_, f32[2,2048]{1,0:T(2,128)S(1)} %get-tuple-element.42.refs_2_, f32[2,2048]{1,0:T(2,128)S(1)} %collective-permute-done.9.refs_2_.refs_3_, ...), custom_call_target="tpu_custom_call" | custom-call | tf_op jit(solution)/shard_map/pallas_call | solution.py:69
  65.1 4.9 %collective-permute-start.14 = (f32[4,2048]{1,0:T(4,128)S(1)}, f32[4,2048]{1,0:T(4,128)S(1)}, u32[]{:S(2)}, u32[]{:S(2)}) collective-permute-start(f32[4,2048]{1,0:T(4,128)S(1)} %get-tuple-element.47.refs_0_), channel_id=1, source_target_pairs={{0,1},{1,0},{2,3},{3,2},{4,5},{5,4},{6,7},{7,6},{8,9},{9,8},{10,11... | collective-permute-start | bytes 98312 | tf_op jit(solution)/shard_map/ppermute | solution.py:129
  70.8 1.7 %collective-permute-start.15 = (f32[4,2048]{1,0:T(4,128)S(1)}, f32[4,2048]{1,0:T(4,128)S(1)}, u32[]{:S(2)}, u32[]{:S(2)}) collective-permute-start(f32[4,2048]{1,0:T(4,128)S(1)} %shard_map.81.refs_0_), channel_id=1, source_target_pairs={{0,16},{16,0},{1,17},{17,1},{2,18},{18,2},{3,19},{19,3},{4,20},{20... | collective-permute-start | bytes 98312 | tf_op jit(solution)/shard_map/ppermute | solution.py:129
  72.6 2.1 %collective-permute-done.15.refs_1_ = f32[4,2048]{1,0:T(4,128)S(1)} collective-permute-done((f32[4,2048]{1,0:T(4,128)S(1)}, f32[4,2048]{1,0:T(4,128)S(1)}, u32[]{:S(2)}, u32[]{:S(2)}) %collective-permute-start.15) | collective-permute-done | bytes 32800 | tf_op jit(solution)/shard_map/ppermute | solution.py:129
  74.7 4.2 %collective-permute-done.16.refs_1_ = f32[4,2048]{1,0:T(4,128)S(1)} collective-permute-done((f32[4,2048]{1,0:T(4,128)S(1)}, f32[4,2048]{1,0:T(4,128)S(1)}, u32[]{:S(2)}, u32[]{:S(2)}) %collective-permute-start.16) | collective-permute-done | bytes 32800 | tf_op jit(solution)/shard_map/ppermute | solution.py:129
  79.5 3.0 %collective-permute-start.17 = (s16[128,1152]{1,0:T(8,128)(2,1)S(1)}, s16[128,1152]{1,0:T(8,128)(2,1)S(1)}, u32[]{:S(2)}, u32[]{:S(2)}) collective-permute-start(s16[128,1152]{1,0:T(8,128)(2,1)S(1)} %get-tuple-element.48), channel_id=1, source_target_pairs={{0,14},{2,0},{4,2},{6,4},{8,6},{10,8},{12,10},{14,12},{1,15},{3,1}... | collective-permute-start | bytes 884744 | tf_op jit(solution)/shard_map/ppermute | solution.py:281
  82.6 5.4 %collective-permute-done.19.refs_1_ = f32[4,2048]{1,0:T(4,128)S(1)} collective-permute-done((f32[4,2048]{1,0:T(4,128)S(1)}, f32[4,2048]{1,0:T(4,128)S(1)}, u32[]{:S(2)}, u32[]{:S(2)}) %collective-permute-start.19) | collective-permute-done | bytes 32800 | tf_op jit(solution)/shard_map/ppermute | solution.py:129
  88.0 1.4 %collective-permute-done.18.refs_3_ = s16[128,1152]{1,0:T(8,128)(2,1)S(1)} collective-permute-done((s16[128,1152]{1,0:T(8,128)(2,1)S(1)}, s16[128,1152]{1,0:T(8,128)(2,1)S(1)}, u32[]{:S(2)}, u32[]{:S(2)}) %collective-permute-start.18) | collective-permute-done | bytes 294944 | tf_op jit(solution)/shard_map/ppermute | solution.py:281
  91.4 6.4 %collective-permute-start.20 = (bf16[16,64,2048]{2,1,0:T(8,128)(2,1)}, bf16[16,64,2048]{2,1,0:T(8,128)(2,1)}, u32[]{:S(2)}, u32[]{:S(2)}) collective-permute-start(bf16[16,64,2048]{2,1,0:T(8,128)(2,1)} %shard_map.87.weights), channel_id=1, source_target_pairs={{0,1},{1,0},{2,3},{3,2},{4,5},{5,4},{6,7},{7,6},{8,9},{9,8},{10,11... | collective-permute-start | bytes 12582920 | tf_op jit(solution)/shard_map/ppermute | solution.py:129
  98.0 1.3 collective-permute-start.23
  99.3 1.9 %collective-permute-start.24 = (f32[4,2048]{1,0:T(4,128)S(1)}, f32[4,2048]{1,0:T(4,128)S(1)}, u32[]{:S(2)}, u32[]{:S(2)}) collective-permute-start(f32[4,2048]{1,0:T(4,128)S(1)} %shard_map.85.refs_4_.refs_0_), channel_id=1, source_target_pairs={{0,8},{2,10},{4,12},{6,14},{8,0},{10,2},{12,4},{14,6},{1,9},{3,11}... | collective-permute-start | bytes 98312 | tf_op jit(solution)/shard_map/ppermute | solution.py:129
  101.8 3.2 %collective-permute-done.20.other_weights = bf16[16,64,2048]{2,1,0:T(8,128)(2,1)} collective-permute-done((bf16[16,64,2048]{2,1,0:T(8,128)(2,1)}, bf16[16,64,2048]{2,1,0:T(8,128)(2,1)}, u32[]{:S(2)}, u32[]{:S(2)}) %collective-permute-start.20) | collective-permute-done | bytes 4194336 | tf_op jit(solution)/shard_map/ppermute | solution.py:129
  104.9 8.1 %shard_map.88 = (bf16[512,2048]{1,0:T(8,128)(2,1)}, f32[8,128]{1,0:T(8,128)}) custom-call(s32[3]{0:T(128)} %pad_add_fusion.2.at, bf16[512,2048]{1,0:T(8,128)(2,1)} %bitcast.29, bf16[16,64,2048]{2,1,0:T(8,128)(2,1)} %shard_map.87.weights, bf16[16,64,2048]{2,1,0:T(8,128)(2,1)} %collective-permute-done.20.other_weights, f32[8,128]{1,0:T(8,128)} %copy-done.11), custom_call_target="tpu_custom_call" | custom-call | tf_op jit(solution)/shard_map/pallas_call | solution.py:325
  114.6 4.7 %collective-permute-start.26 = (f32[2,2048]{1,0:T(2,128)S(1)}, f32[2,2048]{1,0:T(2,128)S(1)}, u32[]{:S(2)}, u32[]{:S(2)}) collective-permute-start(f32[2,2048]{1,0:T(2,128)S(1)} %get-tuple-element.63.refs_6_), channel_id=1, source_target_pairs={{0,240},{16,224},{32,0},{48,16},{64,32},{80,48},{96,64},{112,80},{... | collective-permute-start | bytes 49160 | tf_op jit(solution)/shard_map/ppermute | solution.py:151
  119.8 7.6 %shard_map.92 = (bf16[512,2048]{1,0:T(8,128)(2,1)}, f32[8,128]{1,0:T(8,128)}) custom-call(s32[3]{0:T(128)} %pad_add_fusion.at, bf16[512,2048]{1,0:T(8,128)(2,1)} %bitcast.30, bf16[16,64,2048]{2,1,0:T(8,128)(2,1)} %shard_map.87.weights, bf16[16,64,2048]{2,1,0:T(8,128)(2,1)} %collective-permute-done.20.other_weights, ...), custom_call_target="tpu_custom_call", output_to_operand_aliasing={{0}: (4, {})} | custom-call | tf_op jit(solution)/shard_map/pallas_call | solution.py:325
  128.8 1.2 collective-permute-start.28
  (98 shorter events, 17.5 us)
Async XLA Ops:
  7.2 83.5 %all-gather.2.cloned.1.call-start = ((), (), s32[]{:S(2)}) async-start(), calls=%async_computation | async-start | bytes 4718592 | tf_op jit(solution)/shard_map/all_gather | solution.py:400
  7.2 12.0 %collective-permute-start.1 = (bf16[512,2048]{1,0:T(8,128)(2,1)}, bf16[512,2048]{1,0:T(8,128)(2,1)}, u32[]{:S(2)}, u32[]{:S(2)}) collective-permute-start(bf16[512,2048]{1,0:T(8,128)(2,1)} %bitcast.36), channel_id=1, source_target_pairs={{0,1},{1,0},{2,3},{3,2},{4,5},{5,4},{6,7},{7,6},{8,9},{9,8},{10,11... | collective-permute-start | bytes 6291464 | tf_op jit(solution)/shard_map/ppermute | solution.py:129
  10.5 8.6 %collective-permute-start.2 = (bf16[512,2048]{1,0:T(8,128)(2,1)}, bf16[512,2048]{1,0:T(8,128)(2,1)}, u32[]{:S(2)}, u32[]{:S(2)}) collective-permute-start(bf16[512,2048]{1,0:T(8,128)(2,1)} %bitcast.28), channel_id=1, source_target_pairs={{0,1},{1,0},{2,3},{3,2},{4,5},{5,4},{6,7},{7,6},{8,9},{9,8},{10,11... | collective-permute-start | bytes 6291464 | tf_op jit(solution)/shard_map/ppermute | solution.py:129
  10.6 7.7 %collective-permute-start = (bf16[64,2048]{1,0:T(8,128)(2,1)}, bf16[64,2048]{1,0:T(8,128)(2,1)S(1)}, u32[]{:S(2)}, u32[]{:S(2)}) collective-permute-start(bf16[64,2048]{1,0:T(8,128)(2,1)} %bitcast.42), channel_id=1, source_target_pairs={{0,16},{16,0},{1,17},{17,1},{2,18},{18,2},{3,19},{19,3},{4,20},{20... | collective-permute-start | bytes 786440 | tf_op jit(solution)/shard_map/ppermute | solution.py:129
  17.0 1.4 collective-permute-start.3
  19.2 8.6 %collective-permute-start.4 = (f32[4,2048]{1,0:T(4,128)S(1)}, f32[4,2048]{1,0:T(4,128)S(1)}, u32[]{:S(2)}, u32[]{:S(2)}) collective-permute-start(f32[4,2048]{1,0:T(4,128)S(1)} %shard_map.68.refs_3_.refs_4_.refs_0_), channel_id=1, source_target_pairs={{0,16},{16,0},{1,17},{17,1},{2,18},{18,2},{3,19},{19,3},{4,20},{20... | collective-permute-start | bytes 98312 | tf_op jit(solution)/shard_map/ppermute | solution.py:129
  27.8 32.4 %collective-permute-start.7 = (s16[4,128,1152]{2,1,0:T(8,128)(2,1)}, s16[4,128,1152]{2,1,0:T(8,128)(2,1)S(1)}, u32[]{:S(2)}, u32[]{:S(2)}) collective-permute-start(s16[4,128,1152]{2,1,0:T(8,128)(2,1)} %shard_map.76), channel_id=1, source_target_pairs={{0,16},{16,0},{1,17},{17,1},{2,18},{18,2},{3,19},{19,3},{4,20},{20... | collective-permute-start | bytes 3538952 | tf_op jit(solution)/shard_map/ppermute | solution.py:129
  29.3 3.1 %collective-permute-start.5 = (f32[4,2048]{1,0:T(4,128)S(1)}, f32[4,2048]{1,0:T(4,128)S(1)}, u32[]{:S(2)}, u32[]{:S(2)}) collective-permute-start(f32[4,2048]{1,0:T(4,128)S(1)} %shard_map.71.refs_0_.refs_1_), channel_id=1, source_target_pairs={{0,2},{2,0},{4,6},{6,4},{8,10},{10,8},{12,14},{14,12},{1,3},{3,1},... | collective-permute-start | bytes 98312 | tf_op jit(solution)/shard_map/ppermute | solution.py:129
  32.3 7.4 %collective-permute-start.6 = (f32[4,2048]{1,0:T(4,128)S(1)}, f32[4,2048]{1,0:T(4,128)S(1)}, u32[]{:S(2)}, u32[]{:S(2)}) collective-permute-start(f32[4,2048]{1,0:T(4,128)S(1)} %shard_map.72.refs_4_.refs_0_), channel_id=1, source_target_pairs={{0,4},{2,6},{4,0},{6,2},{8,12},{10,14},{12,8},{14,10},{1,5},{3,7},... | collective-permute-start | bytes 98312 | tf_op jit(solution)/shard_map/ppermute | solution.py:129
  39.7 49.7 %copy-start.2 = (f32[8,128,1024]{2,1,0:T(8,128)}, f32[8,128,1024]{2,1,0:T(8,128)S(1)}, u32[]{:S(2)}) copy-start(f32[8,128,1024]{2,1,0:T(8,128)S(1)} %get-tuple-element.37.refs_0_) | copy-start | bytes 12582916
  39.7 9.3 %collective-permute-start.8 = (f32[4,2048]{1,0:T(4,128)S(1)}, f32[4,2048]{1,0:T(4,128)S(1)}, u32[]{:S(2)}, u32[]{:S(2)}) collective-permute-start(f32[4,2048]{1,0:T(4,128)S(1)} %shard_map.74.refs_4_.refs_0_), channel_id=1, source_target_pairs={{0,8},{2,10},{4,12},{6,14},{8,0},{10,2},{12,4},{14,6},{1,9},{3,11}... | collective-permute-start | bytes 98312 | tf_op jit(solution)/shard_map/ppermute | solution.py:129
  49.0 11.7 %copy-start.9 = (s16[2,128,1152]{2,1,0:T(8,128)(2,1)}, s16[2,128,1152]{2,1,0:T(8,128)(2,1)S(1)}, u32[]{:S(2)}) copy-start(s16[2,128,1152]{2,1,0:T(8,128)(2,1)S(1)} %get-tuple-element.53.refs_0_) | copy-start | bytes 1769476
  49.0 6.1 %collective-permute-start.9 = (f32[2,2048]{1,0:T(2,128)S(1)}, f32[2,2048]{1,0:T(2,128)S(1)}, u32[]{:S(2)}, u32[]{:S(2)}) collective-permute-start(f32[2,2048]{1,0:T(2,128)S(1)} %get-tuple-element.42.refs_2_), channel_id=1, source_target_pairs={{0,240},{16,224},{32,0},{48,16},{64,32},{80,48},{96,64},{112,80},{... | collective-permute-start | bytes 49160 | tf_op jit(solution)/shard_map/ppermute | solution.py:151
  54.3 5.9 %collective-permute-start.10 = (f32[2,2048]{1,0:T(2,128)S(1)}, f32[2,2048]{1,0:T(2,128)S(1)}, u32[]{:S(2)}, u32[]{:S(2)}) collective-permute-start(f32[2,2048]{1,0:T(2,128)S(1)} %get-tuple-element.43.refs_1_), channel_id=1, source_target_pairs={{0,32},{16,48},{32,64},{48,80},{64,96},{80,112},{96,144},{112,128}... | collective-permute-start | bytes 49160 | tf_op jit(solution)/shard_map/ppermute | solution.py:151
  60.7 18.2 %collective-permute-start.12 = (s16[128,1152]{1,0:T(8,128)(2,1)S(1)}, s16[128,1152]{1,0:T(8,128)(2,1)S(1)}, u32[]{:S(2)}, u32[]{:S(2)}) collective-permute-start(s16[128,1152]{1,0:T(8,128)(2,1)S(1)} %get-tuple-element.45), channel_id=1, source_target_pairs={{0,14},{2,0},{4,2},{6,4},{8,6},{10,8},{12,10},{14,12},{1,15},{3,1}... | collective-permute-start | bytes 884744 | tf_op jit(solution)/shard_map/ppermute | solution.py:281
  62.9 15.9 %collective-permute-start.13 = (s16[128,1152]{1,0:T(8,128)(2,1)S(1)}, s16[128,1152]{1,0:T(8,128)(2,1)S(1)}, u32[]{:S(2)}, u32[]{:S(2)}) collective-permute-start(s16[128,1152]{1,0:T(8,128)(2,1)S(1)} %get-tuple-element.46), channel_id=1, source_target_pairs={{0,2},{2,4},{4,6},{6,8},{8,10},{10,12},{12,14},{14,0},{1,3},{3,5},... | collective-permute-start | bytes 884744 | tf_op jit(solution)/shard_map/ppermute | solution.py:281
  62.9 25.0 %collective-permute-start.11 = (s16[2,128,1152]{2,1,0:T(8,128)(2,1)S(1)}, s16[2,128,1152]{2,1,0:T(8,128)(2,1)S(1)}, u32[]{:S(2)}, u32[]{:S(2)}) collective-permute-start(s16[2,128,1152]{2,1,0:T(8,128)(2,1)S(1)} %shard_map.79), channel_id=1, source_target_pairs={{0,16},{16,0},{1,17},{17,1},{2,18},{18,2},{3,19},{19,3},{4,20},{20... | collective-permute-start | bytes 1769480 | tf_op jit(solution)/shard_map/ppermute | solution.py:129
  65.1 5.7 %collective-permute-start.14 = (f32[4,2048]{1,0:T(4,128)S(1)}, f32[4,2048]{1,0:T(4,128)S(1)}, u32[]{:S(2)}, u32[]{:S(2)}) collective-permute-start(f32[4,2048]{1,0:T(4,128)S(1)} %get-tuple-element.47.refs_0_), channel_id=1, source_target_pairs={{0,1},{1,0},{2,3},{3,2},{4,5},{5,4},{6,7},{7,6},{8,9},{9,8},{10,11... | collective-permute-start | bytes 98312 | tf_op jit(solution)/shard_map/ppermute | solution.py:129
  70.8 3.9 %collective-permute-start.15 = (f32[4,2048]{1,0:T(4,128)S(1)}, f32[4,2048]{1,0:T(4,128)S(1)}, u32[]{:S(2)}, u32[]{:S(2)}) collective-permute-start(f32[4,2048]{1,0:T(4,128)S(1)} %shard_map.81.refs_0_), channel_id=1, source_target_pairs={{0,16},{16,0},{1,17},{17,1},{2,18},{18,2},{3,19},{19,3},{4,20},{20... | collective-permute-start | bytes 98312 | tf_op jit(solution)/shard_map/ppermute | solution.py:129
  74.7 4.2 %collective-permute-start.16 = (f32[4,2048]{1,0:T(4,128)S(1)}, f32[4,2048]{1,0:T(4,128)S(1)}, u32[]{:S(2)}, u32[]{:S(2)}) collective-permute-start(f32[4,2048]{1,0:T(4,128)S(1)} %shard_map.82.refs_0_.refs_1_), channel_id=1, source_target_pairs={{0,2},{2,0},{4,6},{6,4},{8,10},{10,8},{12,14},{14,12},{1,3},{3,1},... | collective-permute-start | bytes 98312 | tf_op jit(solution)/shard_map/ppermute | solution.py:129
  79.5 8.4 %collective-permute-start.17 = (s16[128,1152]{1,0:T(8,128)(2,1)S(1)}, s16[128,1152]{1,0:T(8,128)(2,1)S(1)}, u32[]{:S(2)}, u32[]{:S(2)}) collective-permute-start(s16[128,1152]{1,0:T(8,128)(2,1)S(1)} %get-tuple-element.48), channel_id=1, source_target_pairs={{0,14},{2,0},{4,2},{6,4},{8,6},{10,8},{12,10},{14,12},{1,15},{3,1}... | collective-permute-start | bytes 884744 | tf_op jit(solution)/shard_map/ppermute | solution.py:281
  82.6 6.8 %collective-permute-start.18 = (s16[128,1152]{1,0:T(8,128)(2,1)S(1)}, s16[128,1152]{1,0:T(8,128)(2,1)S(1)}, u32[]{:S(2)}, u32[]{:S(2)}) collective-permute-start(s16[128,1152]{1,0:T(8,128)(2,1)S(1)} %get-tuple-element.49), channel_id=1, source_target_pairs={{0,2},{2,4},{4,6},{6,8},{8,10},{10,12},{12,14},{14,0},{1,3},{3,5},... | collective-permute-start | bytes 884744 | tf_op jit(solution)/shard_map/ppermute | solution.py:281
  82.6 5.4 %collective-permute-start.19 = (f32[4,2048]{1,0:T(4,128)S(1)}, f32[4,2048]{1,0:T(4,128)S(1)}, u32[]{:S(2)}, u32[]{:S(2)}) collective-permute-start(f32[4,2048]{1,0:T(4,128)S(1)} %shard_map.83.refs_4_.refs_0_), channel_id=1, source_target_pairs={{0,4},{2,6},{4,0},{6,2},{8,12},{10,14},{12,8},{14,10},{1,5},{3,7},... | collective-permute-start | bytes 98312 | tf_op jit(solution)/shard_map/ppermute | solution.py:129
  91.4 13.6 %collective-permute-start.20 = (bf16[16,64,2048]{2,1,0:T(8,128)(2,1)}, bf16[16,64,2048]{2,1,0:T(8,128)(2,1)}, u32[]{:S(2)}, u32[]{:S(2)}) collective-permute-start(bf16[16,64,2048]{2,1,0:T(8,128)(2,1)} %shard_map.87.weights), channel_id=1, source_target_pairs={{0,1},{1,0},{2,3},{3,2},{4,5},{5,4},{6,7},{7,6},{8,9},{9,8},{10,11... | collective-permute-start | bytes 12582920 | tf_op jit(solution)/shard_map/ppermute | solution.py:129
  97.8 16.0 %collective-permute-start.21 = (s16[2,128,1152]{2,1,0:T(8,128)(2,1)S(1)}, s16[2,128,1152]{2,1,0:T(8,128)(2,1)S(1)}, u32[]{:S(2)}, u32[]{:S(2)}) collective-permute-start(s16[2,128,1152]{2,1,0:T(8,128)(2,1)S(1)} %shard_map.89), channel_id=1, source_target_pairs={{0,16},{16,0},{1,17},{17,1},{2,18},{18,2},{3,19},{19,3},{4,20},{20... | collective-permute-start | bytes 1769480 | tf_op jit(solution)/shard_map/ppermute | solution.py:129
  97.8 16.0 %collective-permute-start.22 = (s16[128,1152]{1,0:T(8,128)(2,1)S(1)}, s16[128,1152]{1,0:T(8,128)(2,1)S(1)}, u32[]{:S(2)}, u32[]{:S(2)}) collective-permute-start(s16[128,1152]{1,0:T(8,128)(2,1)S(1)} %get-tuple-element.54), channel_id=1, source_target_pairs={{0,14},{2,0},{4,2},{6,4},{8,6},{10,8},{12,10},{14,12},{1,15},{3,1}... | collective-permute-start | bytes 884744 | tf_op jit(solution)/shard_map/ppermute | solution.py:281
  98.0 15.8 %collective-permute-start.23 = (s16[128,1152]{1,0:T(8,128)(2,1)S(1)}, s16[128,1152]{1,0:T(8,128)(2,1)S(1)}, u32[]{:S(2)}, u32[]{:S(2)}) collective-permute-start(s16[128,1152]{1,0:T(8,128)(2,1)S(1)} %get-tuple-element.55), channel_id=1, source_target_pairs={{0,2},{2,4},{4,6},{6,8},{8,10},{10,12},{12,14},{14,0},{1,3},{3,5},... | collective-permute-start | bytes 884744 | tf_op jit(solution)/shard_map/ppermute | solution.py:281
  99.3 13.8 %collective-permute-start.24 = (f32[4,2048]{1,0:T(4,128)S(1)}, f32[4,2048]{1,0:T(4,128)S(1)}, u32[]{:S(2)}, u32[]{:S(2)}) collective-permute-start(f32[4,2048]{1,0:T(4,128)S(1)} %shard_map.85.refs_4_.refs_0_), channel_id=1, source_target_pairs={{0,8},{2,10},{4,12},{6,14},{8,0},{10,2},{12,4},{14,6},{1,9},{3,11}... | collective-permute-start | bytes 98312 | tf_op jit(solution)/shard_map/ppermute | solution.py:129
  114.3 13.2 %collective-permute-start.25 = (s16[128,1152]{1,0:T(8,128)(2,1)S(1)}, s16[128,1152]{1,0:T(8,128)(2,1)S(1)}, u32[]{:S(2)}, u32[]{:S(2)}) collective-permute-start(s16[128,1152]{1,0:T(8,128)(2,1)S(1)} %get-tuple-element.61), channel_id=1, source_target_pairs={{0,14},{2,0},{4,2},{6,4},{8,6},{10,8},{12,10},{14,12},{1,15},{3,1}... | collective-permute-start | bytes 884744 | tf_op jit(solution)/shard_map/ppermute | solution.py:281
  114.5 13.0 %collective-permute-start.27 = (f32[2,2048]{1,0:T(2,128)S(1)}, f32[2,2048]{1,0:T(2,128)S(1)}, u32[]{:S(2)}, u32[]{:S(2)}) collective-permute-start(f32[2,2048]{1,0:T(2,128)S(1)} %get-tuple-element.57.refs_4_.refs_5_), channel_id=1, source_target_pairs={{0,32},{16,48},{32,64},{48,80},{64,96},{80,112},{96,144},{112,128}... | collective-permute-start | bytes 49160 | tf_op jit(solution)/shard_map/ppermute | solution.py:151
  114.6 12.9 %collective-permute-start.26 = (f32[2,2048]{1,0:T(2,128)S(1)}, f32[2,2048]{1,0:T(2,128)S(1)}, u32[]{:S(2)}, u32[]{:S(2)}) collective-permute-start(f32[2,2048]{1,0:T(2,128)S(1)} %get-tuple-element.63.refs_6_), channel_id=1, source_target_pairs={{0,240},{16,224},{32,0},{48,16},{64,32},{80,48},{96,64},{112,80},{... | collective-permute-start | bytes 49160 | tf_op jit(solution)/shard_map/ppermute | solution.py:151
  128.8 2.4 %collective-permute-start.28 = (f32[64,1024]{1,0:T(8,128)S(1)}, f32[64,1024]{1,0:T(8,128)S(1)}, u32[]{:S(2)}, u32[]{:S(2)}) collective-permute-start(f32[64,1024]{1,0:T(8,128)S(1)} %get-tuple-element.65), channel_id=1, source_target_pairs={{0,1},{1,0},{2,3},{3,2},{4,5},{5,4},{6,7},{7,6},{8,9},{9,8},{10,11... | collective-permute-start | bytes 786440 | tf_op jit(solution)/shard_map/ppermute | solution.py:129
  (14 other events, 36.3 us)
Sparse Core Ops, SparseCore 0:
  19.3 64.6 all-gather.1

commit v4 on v3

--- a/solution.py
+++ b/solution.py
@@ -16,7 +16,7 @@
 STEPS = 32767.0
 VMEM = 16 * 2**20
 MOST_VMEM = 24 * 2**20
-NO_ROOM = 56 * 2**20
+NO_ROOM = 52 * 2**20
 MARK = jax.ShapeDtypeStruct((8, 128), jnp.float32)
 NO_COST = pl.CostEstimate(flops=0, bytes_accessed=0, transcendentals=0)
 STEPS_ALONG = (("core", 1), ("xl", 1), ("z", 1), ("z", 2), ("z", 4))

time: 141 us -> 137 us (0.972)
  local copies, waits for them, and re-layouts: 10.2 us -> 7.59 us
    unnamed x32 -> x22, local copies, waits for them, and re-layouts: 9.98 us -> 7.33 us
  transfers between devices with their start and end apart: 30 -> 30, of which waited for: 11 -> 11; matrix products, arithmetic and copies ran while one was open for 2% -> 1% of each run, Pallas kernels for 25% -> 25%
where the time goes in v4:
time: 137 us; the launch traced here: 136 us
  starting transfers between devices  47.5 us (35%)
  Pallas kernels  36.4 us (27%)
  waiting for transfers between devices  28.5 us (21%)
  between operations  14.3 us (10%)
  local copies, waits for them, and re-layouts  7.59 us (6%)
  other arithmetic  1.76 us (1%)
    ppermute x18, starting transfers between devices, partner(): return lax.ppermute(value, axis, [(i, i ^ step) for i in range(count)])  30.5 us
    ppermute x18, waiting for transfers between devices, partner(): return lax.ppermute(value, axis, [(i, i ^ step) for i in range(count)])  21.6 us
    pallas_call x2, Pallas kernels, backward_input(): pl.pallas_call(input_kernel, grid_spec=pltpu.PrefetchScalarGridSpec(num_s...  15.2 us
    pallas_call x3, Pallas kernels, chunks(): pl.pallas_call(body, grid_spec=pltpu.PrefetchScalarGridSpec(num_scalar_pr...  13.6 us
    ppermute x4, starting transfers between devices, passed_along(): return lax.ppermute(value, CYCLE + ('xl',), pairs)  10.1 us
    unnamed x22, local copies, waits for them, and re-layouts  7.33 us
    ppermute x7, starting transfers between devices, shifted(): lax.ppermute(value, axis, [(i, (i + steps) % count) for i in range(count)])  6.88 us
    ppermute x4, waiting for transfers between devices, passed_along(): return lax.ppermute(value, CYCLE + ('xl',), pairs)  5.91 us
  transfers between devices with their start and end apart: 30, of which 11 were waited for; matrix products, arithmetic and copies ran while one was open for 1% of the time, Pallas kernels for 25%

profile of v4, /device:TPU:1, one launch (start us, length us, event | category | flops | bytes accessed | tf_op | source)
XLA Modules:
  0.0 136.2 jit_solution(7385568812309827045)
XLA Ops:
  7.2 3.3 %collective-permute-start.1 = (bf16[512,2048]{1,0:T(8,128)(2,1)}, bf16[512,2048]{1,0:T(8,128)(2,1)}, u32[]{:S(2)}, u32[]{:S(2)}) collective-permute-start(bf16[512,2048]{1,0:T(8,128)(2,1)} %bitcast.36), channel_id=1, source_target_pairs={{0,1},{1,0},{2,3},{3,2},{4,5},{5,4},{6,7},{7,6},{8,9},{9,8},{10,11... | collective-permute-start | bytes 6291464 | tf_op jit(solution)/shard_map/ppermute | solution.py:129
  11.5 1.6 %copy-done = bf16[1,512,2048]{2,1,0:T(8,128)(2,1)S(1)} copy-done((bf16[1,512,2048]{2,1,0:T(8,128)(2,1)S(1)}, bf16[1,512,2048]{2,1,0:T(8,128)(2,1)}, u32[]{:S(2)}) %copy-start) | copy-done | bytes 2097176
  13.1 1.6 %copy-done.4 = bf16[1,512,2048]{2,1,0:T(8,128)(2,1)S(1)} copy-done((bf16[1,512,2048]{2,1,0:T(8,128)(2,1)S(1)}, bf16[1,512,2048]{2,1,0:T(8,128)(2,1)}, u32[]{:S(2)}) %copy-start.4) | copy-done | bytes 2097176
  15.6 1.4 %shard_map.67.refs_0_ = f32[4,2048]{1,0:T(4,128)S(1)} custom-call(s32[1]{0:T(128)} %bitcast.6.refs_0_, bf16[16,2048]{1,0:T(8,128)(2,1)S(1)} %pad.4.refs_1_, bf16[512,2048]{1,0:T(8,128)(2,1)S(1)} %bitcast.37, bf16[512,2048]{1,0:T(8,128)(2,1)S(1)} %bitcast.31, bf16[64,2048]{1,0:T(8,128)(2,1)S(1)} %bitcast.43), custom_call_target="tpu_custom_call" | custom-call | tf_op jit(solution)/shard_map/pallas_call | solution.py:69
  19.2 1.8 %collective-permute-start.4 = (f32[4,2048]{1,0:T(4,128)S(1)}, f32[4,2048]{1,0:T(4,128)S(1)}, u32[]{:S(2)}, u32[]{:S(2)}) collective-permute-start(f32[4,2048]{1,0:T(4,128)S(1)} %shard_map.68.refs_3_.refs_4_.refs_0_), channel_id=1, source_target_pairs={{0,16},{16,0},{1,17},{17,1},{2,18},{18,2},{3,19},{19,3},{4,20},{20... | collective-permute-start | bytes 98312 | tf_op jit(solution)/shard_map/ppermute | solution.py:129
  21.2 1.6 %copy-done.5 = bf16[1,512,2048]{2,1,0:T(8,128)(2,1)S(1)} copy-done((bf16[1,512,2048]{2,1,0:T(8,128)(2,1)S(1)}, bf16[1,512,2048]{2,1,0:T(8,128)(2,1)}, u32[]{:S(2)}) %copy-start.5) | copy-done | bytes 2097176
  22.7 5.0 %shard_map.70 = (s16[4,128,1152]{2,1,0:T(8,128)(2,1)}, f32[8,128]{1,0:T(8,128)S(1)}) custom-call(s32[10]{0:T(128)S(1)} %stack.79.place, bf16[512,2048]{1,0:T(8,128)(2,1)S(1)} %bitcast.38, bf16[512,2048]{1,0:T(8,128)(2,1)} %collective-permute-done.1.refs_1_, bf16[512,2048]{1,0:T(8,128)(2,1)S(1)} %bitcast.32, ...), custom_call_target="tpu_custom_call" | custom-call | tf_op jit(solution)/shard_map/pallas_call | solution.py:216
  27.8 1.4 %collective-permute-start.7 = (s16[4,128,1152]{2,1,0:T(8,128)(2,1)}, s16[4,128,1152]{2,1,0:T(8,128)(2,1)S(1)}, u32[]{:S(2)}, u32[]{:S(2)}) collective-permute-start(s16[4,128,1152]{2,1,0:T(8,128)(2,1)} %shard_map.76), channel_id=1, source_target_pairs={{0,16},{16,0},{1,17},{17,1},{2,18},{18,2},{3,19},{19,3},{4,20},{20... | collective-permute-start | bytes 3538952 | tf_op jit(solution)/shard_map/ppermute | solution.py:129
  29.3 3.1 %collective-permute-done.5.refs_1_ = f32[4,2048]{1,0:T(4,128)S(1)} collective-permute-done((f32[4,2048]{1,0:T(4,128)S(1)}, f32[4,2048]{1,0:T(4,128)S(1)}, u32[]{:S(2)}, u32[]{:S(2)}) %collective-permute-start.5) | collective-permute-done | bytes 32800 | tf_op jit(solution)/shard_map/ppermute | solution.py:129
  33.5 1.6 %copy-done.6 = bf16[1,512,2048]{2,1,0:T(8,128)(2,1)S(1)} copy-done((bf16[1,512,2048]{2,1,0:T(8,128)(2,1)S(1)}, bf16[1,512,2048]{2,1,0:T(8,128)(2,1)}, u32[]{:S(2)}) %copy-start.6) | copy-done | bytes 2097176
  35.1 4.6 %shard_map.73 = (f32[8,128,1024]{2,1,0:T(8,128)S(1)}, f32[8,128]{1,0:T(8,128)S(1)}) custom-call(s32[10]{0:T(128)S(1)} %stack.77.place, bf16[512,2048]{1,0:T(8,128)(2,1)S(1)} %bitcast.39, bf16[512,2048]{1,0:T(8,128)(2,1)} %collective-permute-done.1.refs_1_, bf16[512,2048]{1,0:T(8,128)(2,1)S(1)} %bitcast.33, ...), custom_call_target="tpu_custom_call" | custom-call | tf_op jit(solution)/shard_map/pallas_call | solution.py:216
  39.7 5.3 %collective-permute-start.8 = (f32[4,2048]{1,0:T(4,128)S(1)}, f32[4,2048]{1,0:T(4,128)S(1)}, u32[]{:S(2)}, u32[]{:S(2)}) collective-permute-start(f32[4,2048]{1,0:T(4,128)S(1)} %shard_map.74.refs_4_.refs_0_), channel_id=1, source_target_pairs={{0,8},{2,10},{4,12},{6,14},{8,0},{10,2},{12,4},{14,6},{1,9},{3,11}... | collective-permute-start | bytes 98312 | tf_op jit(solution)/shard_map/ppermute | solution.py:129
  45.0 4.0 %shard_map.75 = (s16[2,128,1152]{2,1,0:T(8,128)(2,1)S(1)}, s16[2,128,1152]{2,1,0:T(8,128)(2,1)S(1)}, f32[8,128]{1,0:T(8,128)S(1)}) custom-call(s32[10]{0:T(128)S(1)} %stack.79.place, bf16[512,2048]{1,0:T(8,128)(2,1)S(1)} %bitcast.40, bf16[512,2048]{1,0:T(8,128)(2,1)} %collective-permute-done.1.refs_1_, bf16[512,2048]{1,0:T(8,128)(2,1)S(1)} %bitcast.34, ...), custom_call_target="tpu_custom_call" | custom-call | tf_op jit(solution)/shard_map/pallas_call | solution.py:216
  49.0 5.2 %collective-permute-start.9 = (f32[2,2048]{1,0:T(2,128)S(1)}, f32[2,2048]{1,0:T(2,128)S(1)}, u32[]{:S(2)}, u32[]{:S(2)}) collective-permute-start(f32[2,2048]{1,0:T(2,128)S(1)} %get-tuple-element.42.refs_2_), channel_id=1, source_target_pairs={{0,240},{16,224},{32,0},{48,16},{64,32},{80,48},{96,64},{112,80},{... | collective-permute-start | bytes 49160 | tf_op jit(solution)/shard_map/ppermute | solution.py:151
  55.1 5.0 %collective-permute-done.10.refs_3_.refs_4_ = f32[2,2048]{1,0:T(2,128)S(1)} collective-permute-done((f32[2,2048]{1,0:T(2,128)S(1)}, f32[2,2048]{1,0:T(2,128)S(1)}, u32[]{:S(2)}, u32[]{:S(2)}) %collective-permute-start.10) | collective-permute-done | bytes 16416 | tf_op jit(solution)/shard_map/ppermute | solution.py:151
  60.7 2.2 %collective-permute-start.12 = (s16[128,1152]{1,0:T(8,128)(2,1)S(1)}, s16[128,1152]{1,0:T(8,128)(2,1)S(1)}, u32[]{:S(2)}, u32[]{:S(2)}) collective-permute-start(s16[128,1152]{1,0:T(8,128)(2,1)S(1)} %get-tuple-element.45), channel_id=1, source_target_pairs={{0,14},{2,0},{4,2},{6,4},{8,6},{10,8},{12,10},{14,12},{1,15},{3,1}... | collective-permute-start | bytes 884744 | tf_op jit(solution)/shard_map/ppermute | solution.py:281
  62.9 2.1 %shard_map.80 = (f32[4,2048]{1,0:T(4,128)S(1)}, f32[8,64]{1,0:T(8,128)S(1)}) custom-call(s32[1]{0:T(128)} %bitcast.6.refs_0_, f32[2,2048]{1,0:T(2,128)S(1)} %get-tuple-element.43.refs_1_, f32[2,2048]{1,0:T(2,128)S(1)} %get-tuple-element.42.refs_2_, f32[2,2048]{1,0:T(2,128)S(1)} %collective-permute-done.9.refs_2_.refs_3_, ...), custom_call_target="tpu_custom_call" | custom-call | tf_op jit(solution)/shard_map/pallas_call | solution.py:69
  65.0 4.9 %collective-permute-start.14 = (f32[4,2048]{1,0:T(4,128)S(1)}, f32[4,2048]{1,0:T(4,128)S(1)}, u32[]{:S(2)}, u32[]{:S(2)}) collective-permute-start(f32[4,2048]{1,0:T(4,128)S(1)} %get-tuple-element.47.refs_0_), channel_id=1, source_target_pairs={{0,1},{1,0},{2,3},{3,2},{4,5},{5,4},{6,7},{7,6},{8,9},{9,8},{10,11... | collective-permute-start | bytes 98312 | tf_op jit(solution)/shard_map/ppermute | solution.py:129
  70.8 1.7 %collective-permute-start.15 = (f32[4,2048]{1,0:T(4,128)S(1)}, f32[4,2048]{1,0:T(4,128)S(1)}, u32[]{:S(2)}, u32[]{:S(2)}) collective-permute-start(f32[4,2048]{1,0:T(4,128)S(1)} %shard_map.81.refs_0_), channel_id=1, source_target_pairs={{0,16},{16,0},{1,17},{17,1},{2,18},{18,2},{3,19},{19,3},{4,20},{20... | collective-permute-start | bytes 98312 | tf_op jit(solution)/shard_map/ppermute | solution.py:129
  72.5 2.1 %collective-permute-done.15.refs_1_ = f32[4,2048]{1,0:T(4,128)S(1)} collective-permute-done((f32[4,2048]{1,0:T(4,128)S(1)}, f32[4,2048]{1,0:T(4,128)S(1)}, u32[]{:S(2)}, u32[]{:S(2)}) %collective-permute-start.15) | collective-permute-done | bytes 32800 | tf_op jit(solution)/shard_map/ppermute | solution.py:129
  74.7 4.2 %collective-permute-done.16.refs_1_ = f32[4,2048]{1,0:T(4,128)S(1)} collective-permute-done((f32[4,2048]{1,0:T(4,128)S(1)}, f32[4,2048]{1,0:T(4,128)S(1)}, u32[]{:S(2)}, u32[]{:S(2)}) %collective-permute-start.16) | collective-permute-done | bytes 32800 | tf_op jit(solution)/shard_map/ppermute | solution.py:129
  79.5 3.0 %collective-permute-start.17 = (s16[128,1152]{1,0:T(8,128)(2,1)S(1)}, s16[128,1152]{1,0:T(8,128)(2,1)S(1)}, u32[]{:S(2)}, u32[]{:S(2)}) collective-permute-start(s16[128,1152]{1,0:T(8,128)(2,1)S(1)} %get-tuple-element.48), channel_id=1, source_target_pairs={{0,14},{2,0},{4,2},{6,4},{8,6},{10,8},{12,10},{14,12},{1,15},{3,1}... | collective-permute-start | bytes 884744 | tf_op jit(solution)/shard_map/ppermute | solution.py:281
  82.5 5.8 %collective-permute-done.19.refs_1_ = f32[4,2048]{1,0:T(4,128)S(1)} collective-permute-done((f32[4,2048]{1,0:T(4,128)S(1)}, f32[4,2048]{1,0:T(4,128)S(1)}, u32[]{:S(2)}, u32[]{:S(2)}) %collective-permute-start.19) | collective-permute-done | bytes 32800 | tf_op jit(solution)/shard_map/ppermute | solution.py:129
  90.0 6.7 %collective-permute-start.20 = (bf16[16,64,2048]{2,1,0:T(8,128)(2,1)}, bf16[16,64,2048]{2,1,0:T(8,128)(2,1)}, u32[]{:S(2)}, u32[]{:S(2)}) collective-permute-start(bf16[16,64,2048]{2,1,0:T(8,128)(2,1)} %shard_map.87.weights), channel_id=1, source_target_pairs={{0,1},{1,0},{2,3},{3,2},{4,5},{5,4},{6,7},{7,6},{8,9},{9,8},{10,11... | collective-permute-start | bytes 12582920 | tf_op jit(solution)/shard_map/ppermute | solution.py:129
  97.0 1.3 collective-permute-start.23
  98.2 1.9 %collective-permute-start.24 = (f32[4,2048]{1,0:T(4,128)S(1)}, f32[4,2048]{1,0:T(4,128)S(1)}, u32[]{:S(2)}, u32[]{:S(2)}) collective-permute-start(f32[4,2048]{1,0:T(4,128)S(1)} %shard_map.85.refs_4_.refs_0_), channel_id=1, source_target_pairs={{0,8},{2,10},{4,12},{6,14},{8,0},{10,2},{12,4},{14,6},{1,9},{3,11}... | collective-permute-start | bytes 98312 | tf_op jit(solution)/shard_map/ppermute | solution.py:129
  100.2 3.7 %collective-permute-done.20.other_weights = bf16[16,64,2048]{2,1,0:T(8,128)(2,1)} collective-permute-done((bf16[16,64,2048]{2,1,0:T(8,128)(2,1)}, bf16[16,64,2048]{2,1,0:T(8,128)(2,1)}, u32[]{:S(2)}, u32[]{:S(2)}) %collective-permute-start.20) | collective-permute-done | bytes 4194336 | tf_op jit(solution)/shard_map/ppermute | solution.py:129
  103.9 7.8 %shard_map.88 = (bf16[512,2048]{1,0:T(8,128)(2,1)}, f32[8,128]{1,0:T(8,128)S(1)}) custom-call(s32[3]{0:T(128)S(1)} %pad_add_fusion.2.at, bf16[512,2048]{1,0:T(8,128)(2,1)} %bitcast.29, bf16[16,64,2048]{2,1,0:T(8,128)(2,1)} %shard_map.87.weights, bf16[16,64,2048]{2,1,0:T(8,128)(2,1)} %collective-permute-done.20.other_weights, ...), custom_call_target="tpu_custom_call" | custom-call | tf_op jit(solution)/shard_map/pallas_call | solution.py:325
  112.5 4.7 %collective-permute-start.26 = (f32[2,2048]{1,0:T(2,128)S(1)}, f32[2,2048]{1,0:T(2,128)S(1)}, u32[]{:S(2)}, u32[]{:S(2)}) collective-permute-start(f32[2,2048]{1,0:T(2,128)S(1)} %get-tuple-element.63.refs_6_), channel_id=1, source_target_pairs={{0,240},{16,224},{32,0},{48,16},{64,32},{80,48},{96,64},{112,80},{... | collective-permute-start | bytes 49160 | tf_op jit(solution)/shard_map/ppermute | solution.py:151
  117.2 7.5 %shard_map.92 = (bf16[512,2048]{1,0:T(8,128)(2,1)}, f32[8,128]{1,0:T(8,128)S(1)}) custom-call(s32[3]{0:T(128)S(1)} %pad_add_fusion.at, bf16[512,2048]{1,0:T(8,128)(2,1)} %bitcast.30, bf16[16,64,2048]{2,1,0:T(8,128)(2,1)} %shard_map.87.weights, bf16[16,64,2048]{2,1,0:T(8,128)(2,1)} %collective-permute-done.20.other_weights, ...), custom_call_target="tpu_custom_call", output_to_operand_aliasing={{0}: (4, {})} | custom-call | tf_op jit(solution)/shard_map/pallas_call | solution.py:325
  125.3 1.7 %collective-permute-start.28 = (f32[64,1024]{1,0:T(8,128)S(1)}, f32[64,1024]{1,0:T(8,128)S(1)}, u32[]{:S(2)}, u32[]{:S(2)}) collective-permute-start(f32[64,1024]{1,0:T(8,128)S(1)} %get-tuple-element.65), channel_id=1, source_target_pairs={{0,1},{1,0},{2,3},{3,2},{4,5},{5,4},{6,7},{7,6},{8,9},{9,8},{10,11... | collective-permute-start | bytes 786440 | tf_op jit(solution)/shard_map/ppermute | solution.py:129
  128.2 1.1 shard_map.94
  (88 shorter events, 13.0 us)
Async XLA Ops:
  7.2 82.8 %all-gather.2.cloned.1.call-start = ((), (), s32[]{:S(2)}) async-start(), calls=%async_computation | async-start | bytes 4718592 | tf_op jit(solution)/shard_map/all_gather | solution.py:400
  7.2 12.0 %collective-permute-start.1 = (bf16[512,2048]{1,0:T(8,128)(2,1)}, bf16[512,2048]{1,0:T(8,128)(2,1)}, u32[]{:S(2)}, u32[]{:S(2)}) collective-permute-start(bf16[512,2048]{1,0:T(8,128)(2,1)} %bitcast.36), channel_id=1, source_target_pairs={{0,1},{1,0},{2,3},{3,2},{4,5},{5,4},{6,7},{7,6},{8,9},{9,8},{10,11... | collective-permute-start | bytes 6291464 | tf_op jit(solution)/shard_map/ppermute | solution.py:129
  10.5 8.6 %collective-permute-start.2 = (bf16[512,2048]{1,0:T(8,128)(2,1)}, bf16[512,2048]{1,0:T(8,128)(2,1)}, u32[]{:S(2)}, u32[]{:S(2)}) collective-permute-start(bf16[512,2048]{1,0:T(8,128)(2,1)} %bitcast.28), channel_id=1, source_target_pairs={{0,1},{1,0},{2,3},{3,2},{4,5},{5,4},{6,7},{7,6},{8,9},{9,8},{10,11... | collective-permute-start | bytes 6291464 | tf_op jit(solution)/shard_map/ppermute | solution.py:129
  10.6 7.7 %collective-permute-start = (bf16[64,2048]{1,0:T(8,128)(2,1)}, bf16[64,2048]{1,0:T(8,128)(2,1)S(1)}, u32[]{:S(2)}, u32[]{:S(2)}) collective-permute-start(bf16[64,2048]{1,0:T(8,128)(2,1)} %bitcast.42), channel_id=1, source_target_pairs={{0,16},{16,0},{1,17},{17,1},{2,18},{18,2},{3,19},{19,3},{4,20},{20... | collective-permute-start | bytes 786440 | tf_op jit(solution)/shard_map/ppermute | solution.py:129
  17.0 1.4 collective-permute-start.3
  19.2 8.6 %collective-permute-start.4 = (f32[4,2048]{1,0:T(4,128)S(1)}, f32[4,2048]{1,0:T(4,128)S(1)}, u32[]{:S(2)}, u32[]{:S(2)}) collective-permute-start(f32[4,2048]{1,0:T(4,128)S(1)} %shard_map.68.refs_3_.refs_4_.refs_0_), channel_id=1, source_target_pairs={{0,16},{16,0},{1,17},{17,1},{2,18},{18,2},{3,19},{19,3},{4,20},{20... | collective-permute-start | bytes 98312 | tf_op jit(solution)/shard_map/ppermute | solution.py:129
  27.8 32.4 %collective-permute-start.7 = (s16[4,128,1152]{2,1,0:T(8,128)(2,1)}, s16[4,128,1152]{2,1,0:T(8,128)(2,1)S(1)}, u32[]{:S(2)}, u32[]{:S(2)}) collective-permute-start(s16[4,128,1152]{2,1,0:T(8,128)(2,1)} %shard_map.76), channel_id=1, source_target_pairs={{0,16},{16,0},{1,17},{17,1},{2,18},{18,2},{3,19},{19,3},{4,20},{20... | collective-permute-start | bytes 3538952 | tf_op jit(solution)/shard_map/ppermute | solution.py:129
  29.3 3.1 %collective-permute-start.5 = (f32[4,2048]{1,0:T(4,128)S(1)}, f32[4,2048]{1,0:T(4,128)S(1)}, u32[]{:S(2)}, u32[]{:S(2)}) collective-permute-start(f32[4,2048]{1,0:T(4,128)S(1)} %shard_map.71.refs_0_.refs_1_), channel_id=1, source_target_pairs={{0,2},{2,0},{4,6},{6,4},{8,10},{10,8},{12,14},{14,12},{1,3},{3,1},... | collective-permute-start | bytes 98312 | tf_op jit(solution)/shard_map/ppermute | solution.py:129
  32.3 7.4 %collective-permute-start.6 = (f32[4,2048]{1,0:T(4,128)S(1)}, f32[4,2048]{1,0:T(4,128)S(1)}, u32[]{:S(2)}, u32[]{:S(2)}) collective-permute-start(f32[4,2048]{1,0:T(4,128)S(1)} %shard_map.72.refs_4_.refs_0_), channel_id=1, source_target_pairs={{0,4},{2,6},{4,0},{6,2},{8,12},{10,14},{12,8},{14,10},{1,5},{3,7},... | collective-permute-start | bytes 98312 | tf_op jit(solution)/shard_map/ppermute | solution.py:129
  39.7 49.6 %copy-start.2 = (f32[8,128,1024]{2,1,0:T(8,128)}, f32[8,128,1024]{2,1,0:T(8,128)S(1)}, u32[]{:S(2)}) copy-start(f32[8,128,1024]{2,1,0:T(8,128)S(1)} %get-tuple-element.37.refs_0_) | copy-start | bytes 12582916
  39.7 9.3 %collective-permute-start.8 = (f32[4,2048]{1,0:T(4,128)S(1)}, f32[4,2048]{1,0:T(4,128)S(1)}, u32[]{:S(2)}, u32[]{:S(2)}) collective-permute-start(f32[4,2048]{1,0:T(4,128)S(1)} %shard_map.74.refs_4_.refs_0_), channel_id=1, source_target_pairs={{0,8},{2,10},{4,12},{6,14},{8,0},{10,2},{12,4},{14,6},{1,9},{3,11}... | collective-permute-start | bytes 98312 | tf_op jit(solution)/shard_map/ppermute | solution.py:129
  49.0 11.7 %copy-start.9 = (s16[2,128,1152]{2,1,0:T(8,128)(2,1)}, s16[2,128,1152]{2,1,0:T(8,128)(2,1)S(1)}, u32[]{:S(2)}) copy-start(s16[2,128,1152]{2,1,0:T(8,128)(2,1)S(1)} %get-tuple-element.53.refs_0_) | copy-start | bytes 1769476
  49.0 6.1 %collective-permute-start.9 = (f32[2,2048]{1,0:T(2,128)S(1)}, f32[2,2048]{1,0:T(2,128)S(1)}, u32[]{:S(2)}, u32[]{:S(2)}) collective-permute-start(f32[2,2048]{1,0:T(2,128)S(1)} %get-tuple-element.42.refs_2_), channel_id=1, source_target_pairs={{0,240},{16,224},{32,0},{48,16},{64,32},{80,48},{96,64},{112,80},{... | collective-permute-start | bytes 49160 | tf_op jit(solution)/shard_map/ppermute | solution.py:151
  54.3 5.9 %collective-permute-start.10 = (f32[2,2048]{1,0:T(2,128)S(1)}, f32[2,2048]{1,0:T(2,128)S(1)}, u32[]{:S(2)}, u32[]{:S(2)}) collective-permute-start(f32[2,2048]{1,0:T(2,128)S(1)} %get-tuple-element.43.refs_1_), channel_id=1, source_target_pairs={{0,32},{16,48},{32,64},{48,80},{64,96},{80,112},{96,144},{112,128}... | collective-permute-start | bytes 49160 | tf_op jit(solution)/shard_map/ppermute | solution.py:151
  60.7 18.2 %collective-permute-start.12 = (s16[128,1152]{1,0:T(8,128)(2,1)S(1)}, s16[128,1152]{1,0:T(8,128)(2,1)S(1)}, u32[]{:S(2)}, u32[]{:S(2)}) collective-permute-start(s16[128,1152]{1,0:T(8,128)(2,1)S(1)} %get-tuple-element.45), channel_id=1, source_target_pairs={{0,14},{2,0},{4,2},{6,4},{8,6},{10,8},{12,10},{14,12},{1,15},{3,1}... | collective-permute-start | bytes 884744 | tf_op jit(solution)/shard_map/ppermute | solution.py:281
  62.9 15.9 %collective-permute-start.13 = (s16[128,1152]{1,0:T(8,128)(2,1)S(1)}, s16[128,1152]{1,0:T(8,128)(2,1)S(1)}, u32[]{:S(2)}, u32[]{:S(2)}) collective-permute-start(s16[128,1152]{1,0:T(8,128)(2,1)S(1)} %get-tuple-element.46), channel_id=1, source_target_pairs={{0,2},{2,4},{4,6},{6,8},{8,10},{10,12},{12,14},{14,0},{1,3},{3,5},... | collective-permute-start | bytes 884744 | tf_op jit(solution)/shard_map/ppermute | solution.py:281
  62.9 25.4 %collective-permute-start.11 = (s16[2,128,1152]{2,1,0:T(8,128)(2,1)S(1)}, s16[2,128,1152]{2,1,0:T(8,128)(2,1)S(1)}, u32[]{:S(2)}, u32[]{:S(2)}) collective-permute-start(s16[2,128,1152]{2,1,0:T(8,128)(2,1)S(1)} %shard_map.79), channel_id=1, source_target_pairs={{0,16},{16,0},{1,17},{17,1},{2,18},{18,2},{3,19},{19,3},{4,20},{20... | collective-permute-start | bytes 1769480 | tf_op jit(solution)/shard_map/ppermute | solution.py:129
  65.0 5.7 %collective-permute-start.14 = (f32[4,2048]{1,0:T(4,128)S(1)}, f32[4,2048]{1,0:T(4,128)S(1)}, u32[]{:S(2)}, u32[]{:S(2)}) collective-permute-start(f32[4,2048]{1,0:T(4,128)S(1)} %get-tuple-element.47.refs_0_), channel_id=1, source_target_pairs={{0,1},{1,0},{2,3},{3,2},{4,5},{5,4},{6,7},{7,6},{8,9},{9,8},{10,11... | collective-permute-start | bytes 98312 | tf_op jit(solution)/shard_map/ppermute | solution.py:129
  70.8 3.8 %collective-permute-start.15 = (f32[4,2048]{1,0:T(4,128)S(1)}, f32[4,2048]{1,0:T(4,128)S(1)}, u32[]{:S(2)}, u32[]{:S(2)}) collective-permute-start(f32[4,2048]{1,0:T(4,128)S(1)} %shard_map.81.refs_0_), channel_id=1, source_target_pairs={{0,16},{16,0},{1,17},{17,1},{2,18},{18,2},{3,19},{19,3},{4,20},{20... | collective-permute-start | bytes 98312 | tf_op jit(solution)/shard_map/ppermute | solution.py:129
  74.7 4.2 %collective-permute-start.16 = (f32[4,2048]{1,0:T(4,128)S(1)}, f32[4,2048]{1,0:T(4,128)S(1)}, u32[]{:S(2)}, u32[]{:S(2)}) collective-permute-start(f32[4,2048]{1,0:T(4,128)S(1)} %shard_map.82.refs_0_.refs_1_), channel_id=1, source_target_pairs={{0,2},{2,0},{4,6},{6,4},{8,10},{10,8},{12,14},{14,12},{1,3},{3,1},... | collective-permute-start | bytes 98312 | tf_op jit(solution)/shard_map/ppermute | solution.py:129
  79.5 8.8 %collective-permute-start.17 = (s16[128,1152]{1,0:T(8,128)(2,1)S(1)}, s16[128,1152]{1,0:T(8,128)(2,1)S(1)}, u32[]{:S(2)}, u32[]{:S(2)}) collective-permute-start(s16[128,1152]{1,0:T(8,128)(2,1)S(1)} %get-tuple-element.48), channel_id=1, source_target_pairs={{0,14},{2,0},{4,2},{6,4},{8,6},{10,8},{12,10},{14,12},{1,15},{3,1}... | collective-permute-start | bytes 884744 | tf_op jit(solution)/shard_map/ppermute | solution.py:281
  82.5 6.8 %collective-permute-start.18 = (s16[128,1152]{1,0:T(8,128)(2,1)S(1)}, s16[128,1152]{1,0:T(8,128)(2,1)S(1)}, u32[]{:S(2)}, u32[]{:S(2)}) collective-permute-start(s16[128,1152]{1,0:T(8,128)(2,1)S(1)} %get-tuple-element.49), channel_id=1, source_target_pairs={{0,2},{2,4},{4,6},{6,8},{8,10},{10,12},{12,14},{14,0},{1,3},{3,5},... | collective-permute-start | bytes 884744 | tf_op jit(solution)/shard_map/ppermute | solution.py:281
  82.5 5.8 %collective-permute-start.19 = (f32[4,2048]{1,0:T(4,128)S(1)}, f32[4,2048]{1,0:T(4,128)S(1)}, u32[]{:S(2)}, u32[]{:S(2)}) collective-permute-start(f32[4,2048]{1,0:T(4,128)S(1)} %shard_map.83.refs_4_.refs_0_), channel_id=1, source_target_pairs={{0,4},{2,6},{4,0},{6,2},{8,12},{10,14},{12,8},{14,10},{1,5},{3,7},... | collective-permute-start | bytes 98312 | tf_op jit(solution)/shard_map/ppermute | solution.py:129
  90.0 13.9 %collective-permute-start.20 = (bf16[16,64,2048]{2,1,0:T(8,128)(2,1)}, bf16[16,64,2048]{2,1,0:T(8,128)(2,1)}, u32[]{:S(2)}, u32[]{:S(2)}) collective-permute-start(bf16[16,64,2048]{2,1,0:T(8,128)(2,1)} %shard_map.87.weights), channel_id=1, source_target_pairs={{0,1},{1,0},{2,3},{3,2},{4,5},{5,4},{6,7},{7,6},{8,9},{9,8},{10,11... | collective-permute-start | bytes 12582920 | tf_op jit(solution)/shard_map/ppermute | solution.py:129
  96.8 14.9 %collective-permute-start.21 = (s16[2,128,1152]{2,1,0:T(8,128)(2,1)S(1)}, s16[2,128,1152]{2,1,0:T(8,128)(2,1)S(1)}, u32[]{:S(2)}, u32[]{:S(2)}) collective-permute-start(s16[2,128,1152]{2,1,0:T(8,128)(2,1)S(1)} %shard_map.89), channel_id=1, source_target_pairs={{0,16},{16,0},{1,17},{17,1},{2,18},{18,2},{3,19},{19,3},{4,20},{20... | collective-permute-start | bytes 1769480 | tf_op jit(solution)/shard_map/ppermute | solution.py:129
  96.8 14.9 %collective-permute-start.22 = (s16[128,1152]{1,0:T(8,128)(2,1)S(1)}, s16[128,1152]{1,0:T(8,128)(2,1)S(1)}, u32[]{:S(2)}, u32[]{:S(2)}) collective-permute-start(s16[128,1152]{1,0:T(8,128)(2,1)S(1)} %get-tuple-element.54), channel_id=1, source_target_pairs={{0,14},{2,0},{4,2},{6,4},{8,6},{10,8},{12,10},{14,12},{1,15},{3,1}... | collective-permute-start | bytes 884744 | tf_op jit(solution)/shard_map/ppermute | solution.py:281
  97.0 14.7 %collective-permute-start.23 = (s16[128,1152]{1,0:T(8,128)(2,1)S(1)}, s16[128,1152]{1,0:T(8,128)(2,1)S(1)}, u32[]{:S(2)}, u32[]{:S(2)}) collective-permute-start(s16[128,1152]{1,0:T(8,128)(2,1)S(1)} %get-tuple-element.55), channel_id=1, source_target_pairs={{0,2},{2,4},{4,6},{6,8},{8,10},{10,12},{12,14},{14,0},{1,3},{3,5},... | collective-permute-start | bytes 884744 | tf_op jit(solution)/shard_map/ppermute | solution.py:281
  98.2 13.4 %collective-permute-start.24 = (f32[4,2048]{1,0:T(4,128)S(1)}, f32[4,2048]{1,0:T(4,128)S(1)}, u32[]{:S(2)}, u32[]{:S(2)}) collective-permute-start(f32[4,2048]{1,0:T(4,128)S(1)} %shard_map.85.refs_4_.refs_0_), channel_id=1, source_target_pairs={{0,8},{2,10},{4,12},{6,14},{8,0},{10,2},{12,4},{14,6},{1,9},{3,11}... | collective-permute-start | bytes 98312 | tf_op jit(solution)/shard_map/ppermute | solution.py:129
  112.2 12.5 %collective-permute-start.25 = (s16[128,1152]{1,0:T(8,128)(2,1)S(1)}, s16[128,1152]{1,0:T(8,128)(2,1)S(1)}, u32[]{:S(2)}, u32[]{:S(2)}) collective-permute-start(s16[128,1152]{1,0:T(8,128)(2,1)S(1)} %get-tuple-element.61), channel_id=1, source_target_pairs={{0,14},{2,0},{4,2},{6,4},{8,6},{10,8},{12,10},{14,12},{1,15},{3,1}... | collective-permute-start | bytes 884744 | tf_op jit(solution)/shard_map/ppermute | solution.py:281
  112.3 12.4 %collective-permute-start.27 = (f32[2,2048]{1,0:T(2,128)S(1)}, f32[2,2048]{1,0:T(2,128)S(1)}, u32[]{:S(2)}, u32[]{:S(2)}) collective-permute-start(f32[2,2048]{1,0:T(2,128)S(1)} %get-tuple-element.57.refs_4_.refs_5_), channel_id=1, source_target_pairs={{0,32},{16,48},{32,64},{48,80},{64,96},{80,112},{96,144},{112,128}... | collective-permute-start | bytes 49160 | tf_op jit(solution)/shard_map/ppermute | solution.py:151
  112.5 12.2 %collective-permute-start.26 = (f32[2,2048]{1,0:T(2,128)S(1)}, f32[2,2048]{1,0:T(2,128)S(1)}, u32[]{:S(2)}, u32[]{:S(2)}) collective-permute-start(f32[2,2048]{1,0:T(2,128)S(1)} %get-tuple-element.63.refs_6_), channel_id=1, source_target_pairs={{0,240},{16,224},{32,0},{48,16},{64,32},{80,48},{96,64},{112,80},{... | collective-permute-start | bytes 49160 | tf_op jit(solution)/shard_map/ppermute | solution.py:151
  125.3 2.8 %collective-permute-start.28 = (f32[64,1024]{1,0:T(8,128)S(1)}, f32[64,1024]{1,0:T(8,128)S(1)}, u32[]{:S(2)}, u32[]{:S(2)}) collective-permute-start(f32[64,1024]{1,0:T(8,128)S(1)} %get-tuple-element.65), channel_id=1, source_target_pairs={{0,1},{1,0},{2,3},{3,2},{4,5},{5,4},{6,7},{7,6},{8,9},{9,8},{10,11... | collective-permute-start | bytes 786440 | tf_op jit(solution)/shard_map/ppermute | solution.py:129
  (9 other events, 26.6 us)
Sparse Core Ops, SparseCore 0:
  19.3 64.6 all-gather.1
